TPU v7x, 32 devices: a whole 2x2x4 slice. The times are simulated.
32 devices in a mesh: mem: 2 (over core), grid: 16 (over z, y, x).
Axes of the slice: x: 2, y: 2, z: 4, core: 2. Of those that a mesh axis runs over, the one named last changes fastest.
Arguments:
- control: bfloat16 [8, 32, 368, 736], P('mem', None, 'grid'), may hold values from -6 to 6
- perturbation: bfloat16 [8, 32, 736, 368], P('mem', None, 'grid'), may hold values from -6 to 6
- vertical: bfloat16 [32, 32], replicated, may hold values from 0 to 1
- lat_counts: int32 [16], replicated, may hold values from 1 to 23, 361 in all
- lon_counts: int32 [16], replicated, may hold values from 1 to 46, 720 in all
Outputs:
- increment: float32 [32, 736, 368], P('mem', 'grid')
Inputs may be any that keep to these rules, and one draw needn't show every extreme that they name: Slab g holds its first lat_counts[g] latitude slots as real rows, numbered on from the slabs before it. Slab g holds its first lon_counts[g] longitude slots as real columns, numbered on from the slabs before it.
All inputs are finite; a program needn't handle non-finite values.
Results may differ from a plain program's by a relative error of at most 0.0067.
Values may be sent and summed in bfloat16 or wider, within the bound.
No kernel may reach another device: no remote copies, remote signals or barrier semaphores. Data moves between devices by JAX's collectives and lax.ppermute only.
A program may use at most 128 MiB of HBM per device.

v0:
```python
import jax
import jax.numpy as jnp
from jax import lax
from jax.sharding import PartitionSpec as P

LAT = 361
LON = 720
LENGTH = 8
BAND = 48


def slot_table(counts, slot_count):
    devices = counts.shape[0]
    slot_ids = jnp.arange(devices * slot_count, dtype=jnp.int32)
    device_of = slot_ids // slot_count
    offset_in = slot_ids - device_of * slot_count
    offsets = jnp.cumsum(counts) - counts
    one_hot = device_of[:, None] == jnp.arange(devices, dtype=jnp.int32)[None, :]
    count_of = jnp.sum(jnp.where(one_hot, counts[None, :], 0), axis=1)
    start_of = jnp.sum(jnp.where(one_hot, offsets[None, :], 0), axis=1)
    return (start_of + offset_in, offset_in < count_of)


def pass_matrix(counts, slot_count, extent, periodic):
    position, usable = slot_table(counts, slot_count)
    lag = position[None, :] - position[:, None]
    if periodic:
        lag = jnp.where(lag < 0, lag + extent, lag)
    steps_f = jnp.arange(0, BAND + 1).astype(jnp.float32)
    normal_sum = jnp.sqrt(jnp.sum(jnp.exp(-2.0 * steps_f / LENGTH)))
    lag_f = lag.astype(jnp.float32)
    inside = (lag >= 0) & (lag <= BAND) & usable[:, None] & usable[None, :]
    weight = jnp.where(inside, jnp.exp(-lag_f / LENGTH) / normal_sum, 0.0)
    return weight.astype(jnp.bfloat16)


def per_device(control, perturbation, vertical, lat_counts, lon_counts):
    groups = lax.axis_size("grid")
    row_slots = control.shape[2]
    lon_pad = control.shape[3]
    col_slots = lon_pad // groups
    lon_matrix = pass_matrix(lon_counts, col_slots, LON, True)
    lat_matrix = pass_matrix(lat_counts, row_slots, LAT, False)
    smooth = jnp.dot(control.reshape(-1, lon_pad), lon_matrix, preferred_element_type=jnp.float32)
    smooth = smooth.astype(jnp.bfloat16).reshape(control.shape)
    columns = lax.all_to_all(smooth, "grid", split_axis=3, concat_axis=2, tiled=True)
    filtered = jnp.einsum(
        "mljc,ji->mlci", columns, lat_matrix, preferred_element_type=jnp.float32
    ).astype(jnp.bfloat16)
    mixed = jnp.einsum("kl,mlci->mkci", vertical, filtered, preferred_element_type=jnp.float32)
    partial_value = jnp.sum(mixed * perturbation.astype(jnp.float32), axis=0)
    summed = lax.psum(partial_value, "mem")
    level_share = partial_value.shape[0] // lax.axis_size("mem")
    return lax.dynamic_slice_in_dim(summed, lax.axis_index("mem") * level_share, level_share, 0)


def solution(mesh):
    in_specs = (P("mem", None, "grid", None), P("mem", None, "grid", None), P(), P(), P())
    out_specs = P("mem", "grid", None)
    return jax.shard_map(
        per_device, mesh=mesh, in_specs=in_specs, out_specs=out_specs, check_vma=False
    )
```

profile of v0, /device:TPU:9, one launch (start us, length us, event | category | flops | bytes accessed | tf_op | source)
XLA Modules:
  0.0 315.0 jit_solution(4713329346462881226)
XLA Ops:
  6.5 0.0 copy-start
  6.5 0.6 exponential_reduce_fusion
  7.2 0.7 copy.36
  7.9 0.1 reduce
  8.0 0.7 sub.95
  8.7 0.7 select_reduce_fusion
  10.2 6.9 %copy.37 = bf16[4,32,23,736]{3,2,1,0:T(8,128)(2,1)} copy(bf16[4,32,23,736]{3,1,2,0:T(8,128)(2,1)} %param.5) | data formatting | bytes 8667136 | tf_op args[0]
  17.1 7.7 %reshape.168 = bf16[2944,736]{1,0:T(8,128)(2,1)} reshape(bf16[4,32,23,736]{3,2,1,0:T(8,128)(2,1)} %copy.37) | data formatting | bytes 8667136 | tf_op jit(solution)/shard_map/reshape | solution.py:44
  24.8 9.1 %fusion.3 = bf16[2944,736]{0,1:T(8,128)(2,1)} fusion(bf16[2944,736]{1,0:T(8,128)(2,1)} %reshape.168, f32[]{:T(128)S(6)} %sqrt.4, s32[736]{0:T(1024)S(1)} %fusion.58, pred[736]{0:T(1024)(128)(4,1)S(1)} %fusion.57), kind=kOutput, calls=%fused_computation.6 | convolution fusion | flops 3199798272 | bytes 8670820 | tf_op jit(solution)/shard_map/dot_general | solution.py:44
  33.9 6.6 %copy.38 = bf16[2944,736]{1,0:T(8,128)(2,1)} copy(bf16[2944,736]{0,1:T(8,128)(2,1)} %fusion.3) | data formatting | bytes 8667136 | tf_op jit(solution)/shard_map/convert_element_type | solution.py:45
  40.5 7.3 %reshape.169 = bf16[4,32,23,736]{3,2,1,0:T(8,128)(2,1)} reshape(bf16[2944,736]{1,0:T(8,128)(2,1)} %copy.38) | data formatting | bytes 8667136 | tf_op jit(solution)/shard_map/reshape | solution.py:45
  47.8 31.5 %copy.39 = bf16[4,32,23,736]{1,0,2,3:T(4,128)(2,1)} copy(bf16[4,32,23,736]{3,2,1,0:T(8,128)(2,1)} %reshape.169) | data formatting | bytes 8667136 | tf_op jit(solution)/shard_map/reshape | solution.py:45
  79.3 22.1 %reshape.176 = bf16[16,2,67712]{2,1,0:T(2,128)(2,1)} reshape(bf16[736,23,4,32]{3,2,1,0:T(4,128)(2,1)} %bitcast.28) | data formatting | bytes 8667136
  101.4 0.0 copy-start.1
  101.4 6.8 %all-to-all-start = ((bf16[16,2,67712]{2,1,0:T(2,128)(2,1)}), bf16[16,2,67712]{2,1,0:T(2,128)(2,1)}, u32[]{:S(2)}, u32[]{:S(2)}) async-start(bf16[16,2,67712]{2,1,0:T(2,128)(2,1)} %reshape.176), calls=%async_computation | async-start | bytes 8667136 | tf_op jit(solution)/shard_map/all_to_all | solution.py:46
  108.2 0.2 all-reduce.2.cloned.1.call-start
  108.5 0.0 copy-done.1
  108.5 0.1 copy.42
  108.6 0.1 reduce.1
  108.7 0.1 select_reduce_fusion.2
  108.9 92.6 %all-to-all-done = bf16[16,2,67712]{2,1,0:T(2,128)(2,1)} async-done(((bf16[16,2,67712]{2,1,0:T(2,128)(2,1)}), bf16[16,2,67712]{2,1,0:T(2,128)(2,1)}, u32[]{:S(2)}, u32[]{:S(2)}) %all-to-all-start) | async-done | bytes 4333600 | tf_op jit(solution)/shard_map/all_to_all | solution.py:46
  201.4 19.3 %reshape.177 = bf16[736,23,4,32]{3,2,1,0:T(4,128)(2,1)} reshape(bf16[16,2,67712]{2,1,0:T(2,128)(2,1)} %all-to-all-done) | data formatting | bytes 8667136
  220.7 29.5 %copy.47 = bf16[4,32,23,16,46]{4,1,2,3,0:T(8,128)(2,1)} copy(bf16[4,32,23,16,46]{1,0,2,4,3:T(4,128)(2,1)} %bitcast.29) | data formatting | bytes 8667136 | tf_op jit(solution)/shard_map/all_to_all | solution.py:46
  250.2 20.0 %copy.43 = bf16[4,32,368,46]{2,1,3,0:T(8,128)(2,1)} copy(bf16[4,32,368,46]{3,1,2,0:T(8,128)(2,1)} %bitcast.30) | data formatting | bytes 8667136 | tf_op jit(solution)/shard_map/all_to_all | solution.py:46
  270.3 0.0 copy-done
  270.3 9.0 %fusion = f32[32,46,368]{2,0,1:T(8,128)} fusion(bf16[4,32,46,368]{3,1,2,0:T(8,128)(2,1)} %param.6, bf16[4,32,368,46]{2,1,3,0:T(8,128)(2,1)} %copy.43, f32[]{:T(128)S(6)} %sqrt.4, s32[368]{0:T(512)S(1)} %fusion.63, pred[368]{0:T(512)(128)(4,1)S(1)} %fusion.62, bf16[32,32]{1,0:T(8,128)(2,1)S(1)} %copy-done), kind=kOutput, calls=%fused_computation.1 | convolution fusion | flops 1743177728 | bytes 10837812 | tf_op jit(solution)/shard_map/kl,mlci->mkci/dot_general | solution.py:50
  279.3 0.0 all-reduce.2.cloned.1.call-update
  279.3 26.6 %all-reduce.2.cloned.1.call-done = f32[32,46,368]{2,0,1:T(8,128)} async-done(((f32[32,46,368]{2,0,1:T(8,128)}), f32[32,46,368]{2,0,1:T(8,128)}) %all-reduce.2.cloned.1.call-update) | async-done | bytes 2166800 | tf_op jit(solution)/shard_map/psum | solution.py:52
  305.8 2.3 constant_dynamic-slice_fusion
  (9 shorter events, 0.2 us)
Async XLA Ops:
  6.5 263.7 %copy-start = (bf16[32,32]{1,0:T(8,128)(2,1)S(1)}, bf16[32,32]{1,0:T(8,128)(2,1)}, u32[]{:S(2)}) copy-start(bf16[32,32]{1,0:T(8,128)(2,1)} %param.7) | copy-start | bytes 6148
  101.4 7.0 %copy-start.1 = (s32[16]{0:T(128)S(1)}, s32[16]{0:T(128)}, u32[]{:S(2)}) copy-start(s32[16]{0:T(128)} %param.8) | copy-start | bytes 196
  101.4 100.0 %all-to-all-start = ((bf16[16,2,67712]{2,1,0:T(2,128)(2,1)}), bf16[16,2,67712]{2,1,0:T(2,128)(2,1)}, u32[]{:S(2)}, u32[]{:S(2)}) async-start(bf16[16,2,67712]{2,1,0:T(2,128)(2,1)} %reshape.176), calls=%async_computation | async-start | bytes 8667136 | tf_op jit(solution)/shard_map/all_to_all | solution.py:46
  108.2 197.6 %all-reduce.2.cloned.1.call-start = ((), (), s32[]{:S(2)}) async-start(), calls=%async_computation.1 | async-start | bytes 4521984 | tf_op jit(solution)/shard_map/psum | solution.py:52
Sparse Core Ops, SparseCore 0:
  279.4 26.3 all-reduce.1
where the time goes:
time: 318 us; the launch traced here: 315 us
  local copies, waits for them, and re-layouts  154 us (48%)
  waiting for transfers between devices  119 us (37%)
  matrix products  18.1 us (6%)
  between operations  14.1 us (4%)
  starting transfers between devices  7.01 us (2%)
    all_to_all x1, waiting for transfers between devices, per_device(): lax.all_to_all(smooth, 'grid', split_axis=3, concat_axis=2, tiled=True)  92.6 us
    all_to_all x2, local copies, waits for them, and re-layouts, per_device(): lax.all_to_all(smooth, 'grid', split_axis=3, concat_axis=2, tiled=True)  49.5 us
    unnamed x7, local copies, waits for them, and re-layouts  48.4 us
    reshape x2, local copies, waits for them, and re-layouts, per_device(): smooth = smooth.astype(jnp.bfloat16).reshape(control.shape)  38.8 us
    psum x1, waiting for transfers between devices, per_device(): summed = lax.psum(partial_value, 'mem')  26.6 us
    dot_general x1, matrix products, per_device(): jnp.dot(control.reshape(-1, lon_pad), lon_matrix, preferred_element_type=...  9.09 us
    dot_general x1, matrix products, per_device(): jnp.einsum('kl,mlci->mkci', vertical, filtered, preferred_element_type=jn...  9 us
    reshape x1, local copies, waits for them, and re-layouts, per_device(): control.reshape(-1, lon_pad)  7.67 us
  transfers between devices with their start and end apart: 2, of which 2 were waited for; matrix products, arithmetic and copies ran while one was open for 0% of the time, Pallas kernels for 0%

commit v1 on v0

v1 whole, which is shorter than its diff:
```python
import functools
import math

import jax
import jax.numpy as jnp
import numpy as np
from jax import lax
from jax.experimental import pallas as pl
from jax.experimental.pallas import tpu as pltpu
from jax.sharding import PartitionSpec as P

LAT = 361
LON = 720
LENGTH = 8
BAND = 48
FAR = 1 << 20
NORM = np.float32(math.sqrt(sum(math.exp(-2.0 * e / LENGTH) for e in range(BAND + 1))))
VMEM_LIMIT = 56 * 1024 * 1024
NT = (((1,), (1,)), ((), ()))
NN = (((1,), (0,)), ((), ()))


def round_up(value, multiple):
    return -(-value // multiple) * multiple


def positions(counts, groups, slab, slots):
    place = jnp.full_like(slots, FAR)
    start = jnp.int32(0)
    for g in range(groups):
        count = counts[g]
        offset = slots - g * slab
        here = (offset >= 0) & (offset < count)
        place = jnp.where(here, offset + start, place)
        start = start + count
    return place


def weights(lag, real):
    inside = (lag >= 0) & (lag <= BAND) & real
    value = jnp.exp(lag.astype(jnp.float32) * (-1.0 / LENGTH)) / NORM
    return jnp.where(inside, value, 0.0).astype(jnp.bfloat16)


def lon_kernel(groups, counts, control, out, table, rows, packed, arrived):
    members, row_slots, levels, lon_pad = control.shape
    lanes = members * levels
    col_slots = lon_pad // groups
    col_rows = table.shape[0] // groups

    def fetch(i):
        return pltpu.make_async_copy(control.at[:, i], rows.at[i], arrived.at[i])

    for i in range(row_slots):
        fetch(i).start()

    source = positions(counts, groups, col_slots, lax.broadcasted_iota(jnp.int32, (1, lon_pad), 1))
    own = lax.broadcasted_iota(jnp.int32, (col_rows, 1), 0)
    start = jnp.int32(0)
    for g in range(groups):
        count = counts[g]
        lag = (own + start) - source
        lag = jnp.where(lag < 0, lag + LON, lag)
        table[g * col_rows:(g + 1) * col_rows, :] = weights(lag, own < count)
        start = start + count

    for i in range(row_slots):
        fetch(i).wait()
        field = rows[i].reshape(lanes, lon_pad)
        smooth = lax.dot_general(table[...], field, NT, preferred_element_type=jnp.float32)
        for g in range(groups):
            packed[g, i * col_slots:(i + 1) * col_slots, :] = smooth[g * col_rows:g * col_rows + col_slots]
    for g in range(groups):
        out[g] = packed[g].astype(jnp.bfloat16)


def lat_kernel(groups, row_slots, counts, member_group, mixer, received, pert, kept, given, table, field):
    members, col_slots, levels, lat_pad = pert.shape
    half = levels // 2
    useful = row_slots * col_slots
    second = member_group[0] == 1

    down = positions(counts, groups, row_slots, lax.broadcasted_iota(jnp.int32, (lat_pad, 1), 0))
    across = positions(counts, groups, row_slots, lax.broadcasted_iota(jnp.int32, (1, lat_pad), 1))
    table[...] = weights(down - across, down < FAR)
    for g in range(groups):
        field[g * useful:(g + 1) * useful, :] = received[g, :useful, :].astype(jnp.float32)

    def column(c, carry):
        part = field[pl.ds(c, lat_pad, col_slots), :].astype(jnp.bfloat16)
        smooth = lax.dot_general(table[...], part, NN, preferred_element_type=jnp.float32).astype(jnp.bfloat16)
        mixed = lax.dot_general(mixer[...], smooth, NT, preferred_element_type=jnp.float32)
        total = mixed[:levels] * pert[0, c].astype(jnp.float32)
        for m in range(1, members):
            total = total + mixed[m * levels:(m + 1) * levels] * pert[m, c].astype(jnp.float32)
        kept[c] = jnp.where(second, total[half:], total[:half])
        given[c] = jnp.where(second, total[:half], total[half:])
        return carry

    lax.fori_loop(0, col_slots, column, 0)


def per_device(control, perturbation, vertical, lat_counts, lon_counts):
    groups = lax.axis_size("grid")
    shares = lax.axis_size("mem")
    members, levels, row_slots, lon_pad = control.shape
    col_slots, lat_pad = perturbation.shape[2:]
    lanes = members * levels
    col_rows = round_up(col_slots, 8)
    sent_rows = round_up(row_slots * col_slots, 16)
    vmem = pl.BlockSpec(memory_space=pltpu.VMEM)
    smem = pl.BlockSpec(memory_space=pltpu.SMEM)
    params = pltpu.CompilerParams(vmem_limit_bytes=VMEM_LIMIT)

    smooth = pl.pallas_call(
        functools.partial(lon_kernel, groups),
        out_shape=jax.ShapeDtypeStruct((groups, sent_rows, lanes), jnp.bfloat16),
        in_specs=[smem, pl.BlockSpec(memory_space=pl.ANY)],
        out_specs=vmem,
        scratch_shapes=[
            pltpu.VMEM((groups * col_rows, lon_pad), jnp.bfloat16),
            pltpu.VMEM((row_slots, members, levels, lon_pad), jnp.bfloat16),
            pltpu.VMEM((groups, sent_rows, lanes), jnp.float32),
            pltpu.SemaphoreType.DMA((row_slots,)),
        ],
        compiler_params=params,
        name="lon_filter",
    )(lon_counts, jnp.transpose(control, (0, 2, 1, 3)))

    received = lax.all_to_all(smooth, "grid", split_axis=0, concat_axis=0, tiled=True)

    half = levels // 2
    member_group = (lax.axis_index("mem") if shares == 2 else jnp.int32(0)).reshape(1)
    mixer = jnp.kron(jnp.eye(members, dtype=jnp.bfloat16), vertical)

    shape = jax.ShapeDtypeStruct((col_slots, half, lat_pad), jnp.float32)
    kept, given = pl.pallas_call(
        functools.partial(lat_kernel, groups, row_slots),
        out_shape=(shape, shape),
        in_specs=[smem, smem, vmem, vmem, vmem],
        out_specs=(vmem, vmem),
        scratch_shapes=[
            pltpu.VMEM((lat_pad, lat_pad), jnp.bfloat16),
            pltpu.VMEM((lat_pad * col_slots, lanes), jnp.float32),
        ],
        compiler_params=params,
        name="lat_filter",
    )(lat_counts, member_group, mixer, received, jnp.transpose(perturbation, (0, 2, 1, 3)))
    if shares == 2:
        total = kept + lax.ppermute(given, "mem", [(0, 1), (1, 0)])
    else:
        total = lax.psum_scatter(
            jnp.concatenate([kept, given], axis=1), "mem", scatter_dimension=1, tiled=True
        )
    return jnp.transpose(total, (1, 0, 2))


def solution(mesh):
    in_specs = (P("mem", None, "grid", None), P("mem", None, "grid", None), P(), P(), P())
    out_specs = P("mem", "grid", None)
    return jax.shard_map(per_device, mesh=mesh, in_specs=in_specs, out_specs=out_specs, check_vma=False)
```

time: 318 us -> 161 us (0.51)
  the two profiles are of different devices: /device:TPU:9 before, /device:TPU:15 now
where the time goes in v1:
time: 161 us
  waiting for transfers between devices  101 us (63%)
  Pallas kernels  48.7 us (30%)
  starting transfers between devices  8.05 us (5%)
  other arithmetic  2.52 us (2%)
    all_to_all x1, waiting for transfers between devices, per_device(): lax.all_to_all(smooth, 'grid', split_axis=0, concat_axis=0, tiled=True)  98 us
    pallas_call x1, Pallas kernels, per_device(): pl.pallas_call(functools.partial(lat_kernel, groups, row_slots), out_shap...  27.1 us
    pallas_call x1, Pallas kernels, per_device(): pl.pallas_call(functools.partial(lon_kernel, groups), out_shape=jax.Shape...  21.7 us
    all_to_all x1, starting transfers between devices, per_device(): lax.all_to_all(smooth, 'grid', split_axis=0, concat_axis=0, tiled=True)  6.59 us
  transfers between devices with their start and end apart: 2, of which 2 were waited for; matrix products, arithmetic and copies ran while one was open for 1% of the time, Pallas kernels for 0%

profile of v1, /device:TPU:15, one launch (start us, length us, event | category | flops | bytes accessed | tf_op | source)
XLA Modules:
  0.0 160.7 jit_solution(16602345015591703394)
XLA Ops:
  0.0 21.7 %lon_filter.1 = bf16[16,1072,128]{2,1,0:T(8,128)(2,1)} custom-call(s32[16]{0:T(128)} %counts.2, bf16[4,23,32,736]{3,2,1,0:T(8,128)(2,1)} %bitcast.5), custom_call_target="tpu_custom_call" | custom-call | tf_op jit(solution)/shard_map/lon_filter/pallas_call | solution.py:115
  21.7 0.0 copy-start
  21.7 6.6 %all-to-all-start = ((bf16[16,1072,128]{2,1,0:T(8,128)(2,1)}), bf16[16,1072,128]{2,1,0:T(8,128)(2,1)}, u32[]{:S(2)}, u32[]{:S(2)}) async-start(bf16[16,1072,128]{2,1,0:T(8,128)(2,1)} %lon_filter.1), calls=%async_computation | async-start | bytes 8781824 | tf_op jit(solution)/shard_map/all_to_all | solution.py:130
  28.3 0.0 copy-done
  28.3 0.1 broadcast_multiply_fusion
  28.4 0.7 mul.27.mixer
  29.1 98.0 %all-to-all-done.received = bf16[16,1072,128]{2,1,0:T(8,128)(2,1)} async-done(((bf16[16,1072,128]{2,1,0:T(8,128)(2,1)}), bf16[16,1072,128]{2,1,0:T(8,128)(2,1)}, u32[]{:S(2)}, u32[]{:S(2)}) %all-to-all-start) | async-done | bytes 4390944 | tf_op jit(solution)/shard_map/all_to_all | solution.py:130
  127.2 27.1 %lat_filter.1 = (f32[46,16,368]{2,1,0:T(8,128)}, f32[46,16,368]{2,1,0:T(8,128)}) custom-call(s32[16]{0:T(128)} %counts.3, s32[1]{0:T(128)} %bitcast.member_group, bf16[128,128]{1,0:T(8,128)(2,1)} %mul.27.mixer, bf16[16,1072,128]{2,1,0:T(8,128)(2,1)} %all-to-all-done.received, bf16[4,46,32,368]{3,2,1,0:T(8,128)(2,1)} %bitcast.6), custom_call_target="tpu_custom_call" | custom-call | tf_op jit(solution)/shard_map/lat_filter/pallas_call | solution.py:137
  154.2 1.5 collective-permute-start
  155.7 2.6 %collective-permute-done = f32[46,16,368]{2,1,0:T(8,128)S(1)} collective-permute-done((f32[46,16,368]{2,1,0:T(8,128)}, f32[46,16,368]{2,1,0:T(8,128)S(1)}, u32[]{:S(2)}, u32[]{:S(2)}) %collective-permute-start) | collective-permute-done | bytes 1083424 | tf_op jit(solution)/shard_map/ppermute | solution.py:150
  158.3 2.4 %add_bitcast_fusion = f32[16,46,368]{2,0,1:T(8,128)} fusion(f32[46,16,368]{2,1,0:T(8,128)} %get-tuple-element.7, f32[46,16,368]{2,1,0:T(8,128)S(1)} %collective-permute-done), kind=kLoop, calls=%fused_computation | loop fusion | flops 270848 | bytes 3250176 | tf_op jit(solution)/shard_map/transpose | solution.py:155
  (1 shorter events, 0.0 us)
Async XLA Ops:
  21.7 6.6 %copy-start = (bf16[32,32]{1,0:T(8,128)(2,1)S(1)}, bf16[32,32]{1,0:T(8,128)(2,1)}, u32[]{:S(2)}) copy-start(bf16[32,32]{1,0:T(8,128)(2,1)} %param.7) | copy-start | bytes 6148
  21.7 105.5 %all-to-all-start = ((bf16[16,1072,128]{2,1,0:T(8,128)(2,1)}), bf16[16,1072,128]{2,1,0:T(8,128)(2,1)}, u32[]{:S(2)}, u32[]{:S(2)}) async-start(bf16[16,1072,128]{2,1,0:T(8,128)(2,1)} %lon_filter.1), calls=%async_computation | async-start | bytes 8781824 | tf_op jit(solution)/shard_map/all_to_all | solution.py:130
  154.2 4.1 %collective-permute-start = (f32[46,16,368]{2,1,0:T(8,128)}, f32[46,16,368]{2,1,0:T(8,128)S(1)}, u32[]{:S(2)}, u32[]{:S(2)}) collective-permute-start(f32[46,16,368]{2,1,0:T(8,128)} %get-tuple-element.8), channel_id=1, source_target_pairs={{0,16},{16,0},{1,17},{17,1},{2,18},{18,2},{3,19},{19,3},{4,20},{20... | collective-permute-start | bytes 3250184 | tf_op jit(solution)/shard_map/ppermute | solution.py:150

commit v2 on v1

v2 whole, which is shorter than its diff:
```python
import functools
import math

import jax
import jax.numpy as jnp
import numpy as np
from jax import lax
from jax.experimental import pallas as pl
from jax.experimental.pallas import tpu as pltpu
from jax.sharding import PartitionSpec as P

LAT = 361
LON = 720
LENGTH = 8
BAND = 48
FAR = 1 << 20
NORM = np.float32(math.sqrt(sum(math.exp(-2.0 * e / LENGTH) for e in range(BAND + 1))))
VMEM_LIMIT = 28 * 1024 * 1024
FIRST = 3
NT = (((1,), (1,)), ((), ()))
NN = (((1,), (0,)), ((), ()))


def round_up(value, multiple):
    return -(-value // multiple) * multiple


def sums_before(counts, starts, groups):
    total = jnp.int32(0)
    for g in range(groups):
        starts[g] = total
        total = total + counts[g]


def place_of(counts, starts, slab, slots, size):
    inside = (slots >= 0) & (slots < jnp.minimum(counts[slab], size))
    return jnp.where(inside, slots + starts[slab], FAR)


def weights(lag, real):
    inside = (lag >= 0) & (lag <= BAND) & real
    value = jnp.exp(lag.astype(jnp.float32) * (-1.0 / LENGTH)) / NORM
    return jnp.where(inside, value, 0.0).astype(jnp.bfloat16)


def lon_kernel(groups, masks, counts, me, control, *refs):
    outs, (table, rows, packed, starts, arrived) = refs[:len(masks)], refs[len(masks):]
    members, row_slots, levels, lon_pad = control.shape
    lanes = members * levels
    col_slots = lon_pad // groups
    col_rows = table.shape[0] // len(masks)

    def fetch(i):
        return pltpu.make_async_copy(control.at[:, i], rows.at[i], arrived.at[i])

    for i in range(row_slots):
        fetch(i).start()

    sums_before(counts, starts, groups)
    slots = lax.broadcasted_iota(jnp.int32, (1, lon_pad), 1)
    source = jnp.full_like(slots, FAR)
    for g in range(groups):
        source = jnp.minimum(source, place_of(counts, starts, g, slots - g * col_slots, col_slots))
    own = lax.broadcasted_iota(jnp.int32, (col_rows, 1), 0)
    for n, mask in enumerate(masks):
        slab = me[0] ^ mask
        lag = own + starts[slab] - source
        lag = jnp.where(lag < 0, lag + LON, lag)
        table[n * col_rows:(n + 1) * col_rows, :] = weights(lag, own < counts[slab])

    for i in range(0, row_slots, 2):
        count = min(2, row_slots - i)
        for r in range(count):
            fetch(i + r).wait()
        field = rows[i:i + count].reshape(count * lanes, lon_pad)
        smooth = lax.dot_general(table[...], field, NT, preferred_element_type=jnp.float32)
        for n in range(len(masks)):
            for r in range(count):
                packed[n, (i + r) * col_slots:(i + r + 1) * col_slots, :] = smooth[
                    n * col_rows:n * col_rows + col_slots, r * lanes:(r + 1) * lanes
                ]
    for n in range(len(masks)):
        outs[n][...] = packed[n].astype(jnp.bfloat16)


def lat_kernel(groups, row_slots, masks, counts, me, member_group, mixer, pert, *refs):
    received, (kept, given, table, field, starts) = refs[:groups], refs[groups:]
    members, col_slots, levels, lat_pad = pert.shape
    lanes = members * levels
    half = levels // 2
    useful = row_slots * col_slots
    second = member_group[0] == 1

    sums_before(counts, starts, groups)
    down_slots = lax.broadcasted_iota(jnp.int32, (lat_pad, 1), 0)
    across_slots = lax.broadcasted_iota(jnp.int32, (1, lat_pad), 1)
    down, across = jnp.full_like(down_slots, FAR), jnp.full_like(across_slots, FAR)
    for g in range(groups):
        down = jnp.minimum(down, place_of(counts, starts, g, down_slots - g * row_slots, row_slots))
        across = jnp.minimum(
            across, place_of(counts, starts, me[0] ^ masks[g], across_slots - g * row_slots, row_slots)
        )
    table[...] = weights(down - across, down < FAR)
    for g in range(groups):
        field[g * useful:(g + 1) * useful, :] = received[g][...].astype(jnp.float32)

    for c in range(0, col_slots, 2):
        part = jnp.concatenate(
            [field[pl.ds(c + r, lat_pad, col_slots), :].astype(jnp.bfloat16) for r in range(2)], axis=1
        )
        smooth = lax.dot_general(table[...], part, NN, preferred_element_type=jnp.float32).astype(jnp.bfloat16)
        for r in range(2):
            mixed = lax.dot_general(
                mixer[...], smooth[:, r * lanes:(r + 1) * lanes], NT, preferred_element_type=jnp.float32
            )
            total = mixed[:levels] * pert[0, c + r].astype(jnp.float32)
            for m in range(1, members):
                total = total + mixed[m * levels:(m + 1) * levels] * pert[m, c + r].astype(jnp.float32)
            kept[c + r] = jnp.where(second, total[half:], total[:half])
            given[c + r] = jnp.where(second, total[:half], total[half:])


def sending_order(groups):
    far = list(range(groups // 2, groups))
    near = list(range(groups // 4, groups // 2)) + list(range(1, groups // 4))
    order = []
    for n in range(groups // 2):
        order += far[n:n + 1] + near[n:n + 1]
    return order


def per_device(control, perturbation, vertical, lat_counts, lon_counts):
    groups = lax.axis_size("grid")
    shares = lax.axis_size("mem")
    members, levels, row_slots, lon_pad = control.shape
    col_slots, lat_pad = perturbation.shape[2:]
    lanes = members * levels
    col_rows = round_up(col_slots, 8)
    useful = row_slots * col_slots
    vmem = pl.BlockSpec(memory_space=pltpu.VMEM)
    smem = pl.BlockSpec(memory_space=pltpu.SMEM)
    params = pltpu.CompilerParams(vmem_limit_bytes=VMEM_LIMIT)
    me = lax.axis_index("grid").reshape(1)
    order = sending_order(groups)
    fields = jnp.transpose(control, (0, 2, 1, 3))

    def lon_filter(masks):
        return pl.pallas_call(
            functools.partial(lon_kernel, groups, masks),
            out_shape=[jax.ShapeDtypeStruct((useful, lanes), jnp.bfloat16)] * len(masks),
            in_specs=[smem, smem, pl.BlockSpec(memory_space=pl.ANY)],
            out_specs=[vmem] * len(masks),
            scratch_shapes=[
                pltpu.VMEM((len(masks) * col_rows, lon_pad), jnp.bfloat16),
                pltpu.VMEM((row_slots, members, levels, lon_pad), jnp.bfloat16),
                pltpu.VMEM((len(masks), useful, lanes), jnp.float32),
                pltpu.SMEM((groups,), jnp.int32),
                pltpu.SemaphoreType.DMA((row_slots,)),
            ],
            compiler_params=params,
            cost_estimate=pl.CostEstimate(
                flops=2 * len(masks) * col_rows * lon_pad * row_slots * lanes,
                bytes_accessed=2 * (lanes * row_slots * lon_pad + len(masks) * useful * lanes),
                transcendentals=0,
            ),
            name="lon_filter",
        )(lon_counts, me, fields)

    def send(mask, block):
        return lax.ppermute(block, "grid", [(g, g ^ mask) for g in range(groups)])

    first, rest = order[:FIRST], order[FIRST:] + [0]
    received = [send(mask, block) for mask, block in zip(first, lon_filter(first))]
    received += [send(mask, block) if mask else block for mask, block in zip(rest, lon_filter(rest))]
    masks = first + rest

    half = levels // 2
    member_group = (lax.axis_index("mem") if shares == 2 else jnp.int32(0)).reshape(1)
    mixer = jnp.kron(jnp.eye(members, dtype=jnp.bfloat16), vertical)

    shape = jax.ShapeDtypeStruct((col_slots, half, lat_pad), jnp.float32)
    kept, given = pl.pallas_call(
        functools.partial(lat_kernel, groups, row_slots, masks),
        out_shape=(shape, shape),
        in_specs=[smem, smem, smem] + [vmem] * (2 + groups),
        out_specs=(vmem, vmem),
        scratch_shapes=[
            pltpu.VMEM((lat_pad, lat_pad), jnp.bfloat16),
            pltpu.VMEM((lat_pad * col_slots, lanes), jnp.float32),
            pltpu.SMEM((groups,), jnp.int32),
        ],
        compiler_params=params,
        name="lat_filter",
    )(lat_counts, me, member_group, mixer, jnp.transpose(perturbation, (0, 2, 1, 3)), *received)
    if shares == 2:
        total = kept + lax.ppermute(given, "mem", [(0, 1), (1, 0)])
    else:
        total = lax.psum_scatter(
            jnp.concatenate([kept, given], axis=1), "mem", scatter_dimension=1, tiled=True
        )
    return jnp.transpose(total, (1, 0, 2))


def solution(mesh):
    in_specs = (P("mem", None, "grid", None), P("mem", None, "grid", None), P(), P(), P())
    out_specs = P("mem", "grid", None)
    return jax.shard_map(per_device, mesh=mesh, in_specs=in_specs, out_specs=out_specs, check_vma=False)
```

time: 161 us -> 127 us (0.79)
  the two profiles are of different devices: /device:TPU:15 before, /device:TPU:9 now
where the time goes in v2:
time: 127 us; the launch traced here: 126 us
  waiting for transfers between devices  48.1 us (38%)
  starting transfers between devices  39.9 us (31%)
  Pallas kernels  31.5 us (25%)
  local copies, waits for them, and re-layouts  5.35 us (4%)
  other arithmetic  1.27 us (1%)
    ppermute x15, waiting for transfers between devices, send(): return lax.ppermute(block, 'grid', [(g, g ^ mask) for g in range(groups)])  45.7 us
    ppermute x15, starting transfers between devices, send(): return lax.ppermute(block, 'grid', [(g, g ^ mask) for g in range(groups)])  38.3 us
    pallas_call x2, Pallas kernels, lon_filter(): pl.pallas_call(functools.partial(lon_kernel, groups, masks), out_shape=[j...  19.5 us
    pallas_call x1, Pallas kernels, per_device(): pl.pallas_call(functools.partial(lat_kernel, groups, row_slots, masks), o...  12 us
    unnamed x10, local copies, waits for them, and re-layouts  5.22 us
  transfers between devices with their start and end apart: 16, of which 11 were waited for; matrix products, arithmetic and copies ran while one was open for 0% of the time, Pallas kernels for 10%

profile of v2, /device:TPU:9, one launch (start us, length us, event | category | flops | bytes accessed | tf_op | source)
XLA Modules:
  0.0 126.3 jit_solution(7584126697319681190)
XLA Ops:
  0.0 0.0 copy-start
  0.0 2.3 %copy-done = bf16[4,32,23,736]{3,1,2,0:T(8,128)(2,1)S(1)} copy-done((bf16[4,32,23,736]{3,1,2,0:T(8,128)(2,1)S(1)}, bf16[4,32,23,736]{3,1,2,0:T(8,128)(2,1)}, u32[]{:S(2)}) %copy-start) | copy-done | bytes 4333592
  2.3 0.0 copy-start.2
  2.3 0.7 copy-done.2
  2.9 6.8 %lon_filter.2 = (bf16[1058,128]{1,0:T(8,128)(2,1)S(1)}, bf16[1058,128]{1,0:T(8,128)(2,1)S(1)}, bf16[1058,128]{1,0:T(8,128)(2,1)S(1)}) custom-call(s32[16]{0:T(128)S(1)} %copy-done.2, s32[1]{0:T(128)} %bitcast.me, bf16[4,23,32,736]{3,2,1,0:T(8,128)(2,1)S(1)} %bitcast.6), custom_call_target="tpu_custom_call" | custom-call | flops 624033792 | bytes 5146112 | tf_op jit(solution)/shard_map/lon_filter/pallas_call | solution.py:148
  9.7 2.4 %collective-permute-start = (bf16[1058,128]{1,0:T(8,128)(2,1)S(1)}, bf16[1058,128]{1,0:T(8,128)(2,1)S(1)}, u32[]{:S(2)}, u32[]{:S(2)}) collective-permute-start(bf16[1058,128]{1,0:T(8,128)(2,1)S(1)} %get-tuple-element.23), channel_id=1, source_target_pairs={{0,8},{1,9},{2,10},{3,11},{4,12},{5,13},{6,14},{7,15},{8,0},{9,1},... | collective-permute-start | bytes 812552 | tf_op jit(solution)/shard_map/ppermute | solution.py:170
  12.1 0.2 collective-permute-start.1
  12.3 0.0 copy-start.4
  12.3 0.0 copy-start.3
  12.3 1.0 collective-permute-start.2
  13.3 12.7 %lon_filter.3 = (bf16[1058,128]{1,0:T(8,128)(2,1)S(1)}, bf16[1058,128]{1,0:T(8,128)(2,1)S(1)}, bf16[1058,128]{1,0:T(8,128)(2,1)S(1)}, bf16[1058,128]{1,0:T(8,128...) custom-call(s32[16]{0:T(128)S(1)} %copy-done.2, ...), custom_call_target="tpu_custom_call" | custom-call | flops 2704146432 | bytes 7854592 | tf_op jit(solution)/shard_map/lon_filter/pallas_call | solution.py:148
  26.1 1.3 %collective-permute-start.3 = (bf16[1058,128]{1,0:T(8,128)(2,1)S(1)}, bf16[1058,128]{1,0:T(8,128)(2,1)S(1)}, u32[]{:S(2)}, u32[]{:S(2)}) collective-permute-start(bf16[1058,128]{1,0:T(8,128)(2,1)S(1)} %get-tuple-element.26), channel_id=1, source_target_pairs={{0,5},{1,4},{2,7},{3,6},{4,1},{5,0},{6,3},{7,2},{8,13},{9,12},{10,... | collective-permute-start | bytes 812552 | tf_op jit(solution)/shard_map/ppermute | solution.py:170
  27.4 3.2 %collective-permute-start.4 = (bf16[1058,128]{1,0:T(8,128)(2,1)S(1)}, bf16[1058,128]{1,0:T(8,128)(2,1)S(1)}, u32[]{:S(2)}, u32[]{:S(2)}) collective-permute-start(bf16[1058,128]{1,0:T(8,128)(2,1)S(1)} %get-tuple-element.27), channel_id=1, source_target_pairs={{0,10},{1,11},{2,8},{3,9},{4,14},{5,15},{6,12},{7,13},{8,2},{9,3},... | collective-permute-start | bytes 812552 | tf_op jit(solution)/shard_map/ppermute | solution.py:170
  30.6 0.0 collective-permute-done.refs_0_
  30.6 0.1 collective-permute-start.5
  30.7 0.0 collective-permute-done.1.refs_1_
  30.7 2.0 %collective-permute-start.6 = (bf16[1058,128]{1,0:T(8,128)(2,1)S(1)}, bf16[1058,128]{1,0:T(8,128)(2,1)S(1)}, u32[]{:S(2)}, u32[]{:S(2)}) collective-permute-start(bf16[1058,128]{1,0:T(8,128)(2,1)S(1)} %get-tuple-element.29), channel_id=1, source_target_pairs={{0,11},{1,10},{2,9},{3,8},{4,15},{5,14},{6,13},{7,12},{8,3},{9,2},... | collective-permute-start | bytes 812552 | tf_op jit(solution)/shard_map/ppermute | solution.py:170
  32.7 3.6 %collective-permute-done.2.refs_2_ = bf16[1058,128]{1,0:T(8,128)(2,1)S(1)} collective-permute-done((bf16[1058,128]{1,0:T(8,128)(2,1)S(1)}, bf16[1058,128]{1,0:T(8,128)(2,1)S(1)}, u32[]{:S(2)}, u32[]{:S(2)}) %collective-permute-start.2) | collective-permute-done | bytes 270880 | tf_op jit(solution)/shard_map/ppermute | solution.py:170
  36.3 1.4 %collective-permute-start.7 = (bf16[1058,128]{1,0:T(8,128)(2,1)S(1)}, bf16[1058,128]{1,0:T(8,128)(2,1)S(1)}, u32[]{:S(2)}, u32[]{:S(2)}) collective-permute-start(bf16[1058,128]{1,0:T(8,128)(2,1)S(1)} %get-tuple-element.30), channel_id=1, source_target_pairs={{0,7},{1,6},{2,5},{3,4},{4,3},{5,2},{6,1},{7,0},{8,15},{9,14},{10,... | collective-permute-start | bytes 812552 | tf_op jit(solution)/shard_map/ppermute | solution.py:170
  37.8 0.2 collective-permute-done.3.refs_3_
  37.9 4.1 %collective-permute-start.8 = (bf16[1058,128]{1,0:T(8,128)(2,1)S(1)}, bf16[1058,128]{1,0:T(8,128)(2,1)S(1)}, u32[]{:S(2)}, u32[]{:S(2)}) collective-permute-start(bf16[1058,128]{1,0:T(8,128)(2,1)S(1)} %get-tuple-element.31), channel_id=1, source_target_pairs={{0,12},{1,13},{2,14},{3,15},{4,8},{5,9},{6,10},{7,11},{8,4},{9,5},... | collective-permute-start | bytes 812552 | tf_op jit(solution)/shard_map/ppermute | solution.py:170
  42.1 5.5 %collective-permute-done.4.refs_4_ = bf16[1058,128]{1,0:T(8,128)(2,1)S(1)} collective-permute-done((bf16[1058,128]{1,0:T(8,128)(2,1)S(1)}, bf16[1058,128]{1,0:T(8,128)(2,1)S(1)}, u32[]{:S(2)}, u32[]{:S(2)}) %collective-permute-start.4) | collective-permute-done | bytes 270880 | tf_op jit(solution)/shard_map/ppermute | solution.py:170
  47.5 1.2 collective-permute-start.9
  48.7 0.8 collective-permute-done.5.refs_5_
  49.5 3.2 %collective-permute-start.10 = (bf16[1058,128]{1,0:T(8,128)(2,1)}, bf16[1058,128]{1,0:T(8,128)(2,1)S(1)}, u32[]{:S(2)}, u32[]{:S(2)}) collective-permute-start(bf16[1058,128]{1,0:T(8,128)(2,1)} %get-tuple-element.33), channel_id=1, source_target_pairs={{0,13},{1,12},{2,15},{3,14},{4,9},{5,8},{6,11},{7,10},{8,5},{9,4},... | collective-permute-start | bytes 812552 | tf_op jit(solution)/shard_map/ppermute | solution.py:170
  52.7 6.5 %collective-permute-done.6.refs_6_ = bf16[1058,128]{1,0:T(8,128)(2,1)S(1)} collective-permute-done((bf16[1058,128]{1,0:T(8,128)(2,1)S(1)}, bf16[1058,128]{1,0:T(8,128)(2,1)S(1)}, u32[]{:S(2)}, u32[]{:S(2)}) %collective-permute-start.6) | collective-permute-done | bytes 270880 | tf_op jit(solution)/shard_map/ppermute | solution.py:170
  59.2 1.2 collective-permute-start.11
  60.5 1.8 %collective-permute-done.7.refs_7_ = bf16[1058,128]{1,0:T(8,128)(2,1)S(1)} collective-permute-done((bf16[1058,128]{1,0:T(8,128)(2,1)S(1)}, bf16[1058,128]{1,0:T(8,128)(2,1)S(1)}, u32[]{:S(2)}, u32[]{:S(2)}) %collective-permute-start.7) | collective-permute-done | bytes 270880 | tf_op jit(solution)/shard_map/ppermute | solution.py:170
  62.3 12.6 %collective-permute-start.12 = (bf16[1058,128]{1,0:T(8,128)(2,1)}, bf16[1058,128]{1,0:T(8,128)(2,1)}, u32[]{:S(2)}, u32[]{:S(2)}) collective-permute-start(bf16[1058,128]{1,0:T(8,128)(2,1)} %get-tuple-element.35), channel_id=1, source_target_pairs={{0,14},{1,15},{2,12},{3,13},{4,10},{5,11},{6,8},{7,9},{8,6},{9,7},... | collective-permute-start | bytes 812552 | tf_op jit(solution)/shard_map/ppermute | solution.py:170
  74.9 1.8 %collective-permute-done.8.refs_8_ = bf16[1058,128]{1,0:T(8,128)(2,1)S(1)} collective-permute-done((bf16[1058,128]{1,0:T(8,128)(2,1)S(1)}, bf16[1058,128]{1,0:T(8,128)(2,1)S(1)}, u32[]{:S(2)}, u32[]{:S(2)}) %collective-permute-start.8) | collective-permute-done | bytes 270880 | tf_op jit(solution)/shard_map/ppermute | solution.py:170
  76.8 2.2 %collective-permute-start.13 = (bf16[1058,128]{1,0:T(8,128)(2,1)}, bf16[1058,128]{1,0:T(8,128)(2,1)}, u32[]{:S(2)}, u32[]{:S(2)}) collective-permute-start(bf16[1058,128]{1,0:T(8,128)(2,1)} %get-tuple-element.36), channel_id=1, source_target_pairs={{0,3},{1,2},{2,1},{3,0},{4,7},{5,6},{6,5},{7,4},{8,11},{9,10},{10,... | collective-permute-start | bytes 812552 | tf_op jit(solution)/shard_map/ppermute | solution.py:170
  78.9 0.0 collective-permute-done.9.refs_9_
  78.9 2.1 %collective-permute-start.14 = (bf16[1058,128]{1,0:T(8,128)(2,1)}, bf16[1058,128]{1,0:T(8,128)(2,1)}, u32[]{:S(2)}, u32[]{:S(2)}) collective-permute-start(bf16[1058,128]{1,0:T(8,128)(2,1)} %get-tuple-element.37), channel_id=1, source_target_pairs={{0,15},{1,14},{2,13},{3,12},{4,11},{5,10},{6,9},{7,8},{8,7},{9,6},... | collective-permute-start | bytes 812552 | tf_op jit(solution)/shard_map/ppermute | solution.py:170
  81.1 0.0 copy-done.4
  81.1 0.1 broadcast_multiply_fusion
  81.2 0.1 mul.27.mixer
  81.3 12.9 %collective-permute-done.10.refs_10_ = bf16[1058,128]{1,0:T(8,128)(2,1)S(1)} collective-permute-done((bf16[1058,128]{1,0:T(8,128)(2,1)}, bf16[1058,128]{1,0:T(8,128)(2,1)S(1)}, u32[]{:S(2)}, u32[]{:S(2)}) %collective-permute-start.10) | collective-permute-done | bytes 270880 | tf_op jit(solution)/shard_map/ppermute | solution.py:170
  94.2 0.0 collective-permute-done.11.refs_11_
  94.2 6.0 %collective-permute-done.12.refs_12_ = bf16[1058,128]{1,0:T(8,128)(2,1)} collective-permute-done((bf16[1058,128]{1,0:T(8,128)(2,1)}, bf16[1058,128]{1,0:T(8,128)(2,1)}, u32[]{:S(2)}, u32[]{:S(2)}) %collective-permute-start.12) | collective-permute-done | bytes 270880 | tf_op jit(solution)/shard_map/ppermute | solution.py:170
  100.2 0.0 collective-permute-done.13.refs_13_
  100.2 6.6 %collective-permute-done.14.refs_14_ = bf16[1058,128]{1,0:T(8,128)(2,1)} collective-permute-done((bf16[1058,128]{1,0:T(8,128)(2,1)}, bf16[1058,128]{1,0:T(8,128)(2,1)}, u32[]{:S(2)}, u32[]{:S(2)}) %collective-permute-start.14) | collective-permute-done | bytes 270880 | tf_op jit(solution)/shard_map/ppermute | solution.py:170
  106.8 0.0 copy-done.3
  106.8 0.0 copy-start.1
  106.8 2.3 %copy-done.1 = bf16[4,32,46,368]{3,1,2,0:T(8,128)(2,1)S(1)} copy-done((bf16[4,32,46,368]{3,1,2,0:T(8,128)(2,1)S(1)}, bf16[4,32,46,368]{3,1,2,0:T(8,128)(2,1)}, u32[]{:S(2)}) %copy-start.1) | copy-done | bytes 4333592
  109.1 12.0 %lat_filter.1 = (f32[46,16,368]{2,1,0:T(8,128)S(1)}, f32[46,16,368]{2,1,0:T(8,128)S(1)}) custom-call(s32[16]{0:T(128)S(1)} %copy-done.3, s32[1]{0:T(128)} %bitcast.me, s32[1]{0:T(128)} %bitcast.1.member_group, bf16[128,128]{1,0:T(8,128)(2,1)S(1)} %mul.27.mixer, bf16[4,46,32,368]{3,2,1,0:T(8,128)(2,1)S(1)} %bitcast.8, ...), custom_call_target="tpu_custom_call" | custom-call | tf_op jit(solution)/shard_map/lat_filter/pallas_call | solution.py:182
  121.1 1.6 %collective-permute-start.15 = (f32[46,16,368]{2,1,0:T(8,128)S(1)}, f32[46,16,368]{2,1,0:T(8,128)S(1)}, u32[]{:S(2)}, u32[]{:S(2)}) collective-permute-start(f32[46,16,368]{2,1,0:T(8,128)S(1)} %get-tuple-element.40), channel_id=1, source_target_pairs={{0,16},{16,0},{1,17},{17,1},{2,18},{18,2},{3,19},{19,3},{4,20},{20... | collective-permute-start | bytes 3250184 | tf_op jit(solution)/shard_map/ppermute | solution.py:196
  122.7 2.4 %collective-permute-done.15 = f32[46,16,368]{2,1,0:T(8,128)S(1)} collective-permute-done((f32[46,16,368]{2,1,0:T(8,128)S(1)}, f32[46,16,368]{2,1,0:T(8,128)S(1)}, u32[]{:S(2)}, u32[]{:S(2)}) %collective-permute-start.15) | collective-permute-done | bytes 1083424 | tf_op jit(solution)/shard_map/ppermute | solution.py:196
  125.1 1.1 add_bitcast_fusion
  (1 shorter events, 0.0 us)
Async XLA Ops:
  0.0 2.3 %copy-start = (bf16[4,32,23,736]{3,1,2,0:T(8,128)(2,1)S(1)}, bf16[4,32,23,736]{3,1,2,0:T(8,128)(2,1)}, u32[]{:S(2)}) copy-start(bf16[4,32,23,736]{3,1,2,0:T(8,128)(2,1)} %param.5) | copy-start | bytes 13000708
  2.3 0.7 copy-start.2
  9.7 20.9 %collective-permute-start = (bf16[1058,128]{1,0:T(8,128)(2,1)S(1)}, bf16[1058,128]{1,0:T(8,128)(2,1)S(1)}, u32[]{:S(2)}, u32[]{:S(2)}) collective-permute-start(bf16[1058,128]{1,0:T(8,128)(2,1)S(1)} %get-tuple-element.23), channel_id=1, source_target_pairs={{0,8},{1,9},{2,10},{3,11},{4,12},{5,13},{6,14},{7,15},{8,0},{9,1},... | collective-permute-start | bytes 812552 | tf_op jit(solution)/shard_map/ppermute | solution.py:170
  12.1 18.6 %collective-permute-start.1 = (bf16[1058,128]{1,0:T(8,128)(2,1)S(1)}, bf16[1058,128]{1,0:T(8,128)(2,1)S(1)}, u32[]{:S(2)}, u32[]{:S(2)}) collective-permute-start(bf16[1058,128]{1,0:T(8,128)(2,1)S(1)} %get-tuple-element.24), channel_id=1, source_target_pairs={{0,4},{1,5},{2,6},{3,7},{4,0},{5,1},{6,2},{7,3},{8,12},{9,13},{10,... | collective-permute-start | bytes 812552 | tf_op jit(solution)/shard_map/ppermute | solution.py:170
  12.3 68.8 %copy-start.4 = (bf16[32,32]{1,0:T(8,128)(2,1)S(1)}, bf16[32,32]{1,0:T(8,128)(2,1)}, u32[]{:S(2)}) copy-start(bf16[32,32]{1,0:T(8,128)(2,1)} %param.7) | copy-start | bytes 6148
  12.3 94.5 %copy-start.3 = (s32[16]{0:T(128)S(1)}, s32[16]{0:T(128)}, u32[]{:S(2)}) copy-start(s32[16]{0:T(128)} %counts.5) | copy-start | bytes 196
  12.3 24.0 %collective-permute-start.2 = (bf16[1058,128]{1,0:T(8,128)(2,1)S(1)}, bf16[1058,128]{1,0:T(8,128)(2,1)S(1)}, u32[]{:S(2)}, u32[]{:S(2)}) collective-permute-start(bf16[1058,128]{1,0:T(8,128)(2,1)S(1)} %get-tuple-element.25), channel_id=1, source_target_pairs={{0,9},{1,8},{2,11},{3,10},{4,13},{5,12},{6,15},{7,14},{8,1},{9,0},... | collective-permute-start | bytes 812552 | tf_op jit(solution)/shard_map/ppermute | solution.py:170
  26.1 11.9 %collective-permute-start.3 = (bf16[1058,128]{1,0:T(8,128)(2,1)S(1)}, bf16[1058,128]{1,0:T(8,128)(2,1)S(1)}, u32[]{:S(2)}, u32[]{:S(2)}) collective-permute-start(bf16[1058,128]{1,0:T(8,128)(2,1)S(1)} %get-tuple-element.26), channel_id=1, source_target_pairs={{0,5},{1,4},{2,7},{3,6},{4,1},{5,0},{6,3},{7,2},{8,13},{9,12},{10,... | collective-permute-start | bytes 812552 | tf_op jit(solution)/shard_map/ppermute | solution.py:170
  27.4 20.1 %collective-permute-start.4 = (bf16[1058,128]{1,0:T(8,128)(2,1)S(1)}, bf16[1058,128]{1,0:T(8,128)(2,1)S(1)}, u32[]{:S(2)}, u32[]{:S(2)}) collective-permute-start(bf16[1058,128]{1,0:T(8,128)(2,1)S(1)} %get-tuple-element.27), channel_id=1, source_target_pairs={{0,10},{1,11},{2,8},{3,9},{4,14},{5,15},{6,12},{7,13},{8,2},{9,3},... | collective-permute-start | bytes 812552 | tf_op jit(solution)/shard_map/ppermute | solution.py:170
  30.6 18.9 %collective-permute-start.5 = (bf16[1058,128]{1,0:T(8,128)(2,1)S(1)}, bf16[1058,128]{1,0:T(8,128)(2,1)S(1)}, u32[]{:S(2)}, u32[]{:S(2)}) collective-permute-start(bf16[1058,128]{1,0:T(8,128)(2,1)S(1)} %get-tuple-element.28), channel_id=1, source_target_pairs={{0,6},{1,7},{2,4},{3,5},{4,2},{5,3},{6,0},{7,1},{8,14},{9,15},{10,... | collective-permute-start | bytes 812552 | tf_op jit(solution)/shard_map/ppermute | solution.py:170
  30.7 28.5 %collective-permute-start.6 = (bf16[1058,128]{1,0:T(8,128)(2,1)S(1)}, bf16[1058,128]{1,0:T(8,128)(2,1)S(1)}, u32[]{:S(2)}, u32[]{:S(2)}) collective-permute-start(bf16[1058,128]{1,0:T(8,128)(2,1)S(1)} %get-tuple-element.29), channel_id=1, source_target_pairs={{0,11},{1,10},{2,9},{3,8},{4,15},{5,14},{6,13},{7,12},{8,3},{9,2},... | collective-permute-start | bytes 812552 | tf_op jit(solution)/shard_map/ppermute | solution.py:170
  36.3 26.0 %collective-permute-start.7 = (bf16[1058,128]{1,0:T(8,128)(2,1)S(1)}, bf16[1058,128]{1,0:T(8,128)(2,1)S(1)}, u32[]{:S(2)}, u32[]{:S(2)}) collective-permute-start(bf16[1058,128]{1,0:T(8,128)(2,1)S(1)} %get-tuple-element.30), channel_id=1, source_target_pairs={{0,7},{1,6},{2,5},{3,4},{4,3},{5,2},{6,1},{7,0},{8,15},{9,14},{10,... | collective-permute-start | bytes 812552 | tf_op jit(solution)/shard_map/ppermute | solution.py:170
  37.9 38.8 %collective-permute-start.8 = (bf16[1058,128]{1,0:T(8,128)(2,1)S(1)}, bf16[1058,128]{1,0:T(8,128)(2,1)S(1)}, u32[]{:S(2)}, u32[]{:S(2)}) collective-permute-start(bf16[1058,128]{1,0:T(8,128)(2,1)S(1)} %get-tuple-element.31), channel_id=1, source_target_pairs={{0,12},{1,13},{2,14},{3,15},{4,8},{5,9},{6,10},{7,11},{8,4},{9,5},... | collective-permute-start | bytes 812552 | tf_op jit(solution)/shard_map/ppermute | solution.py:170
  47.5 31.4 %collective-permute-start.9 = (bf16[1058,128]{1,0:T(8,128)(2,1)S(1)}, bf16[1058,128]{1,0:T(8,128)(2,1)S(1)}, u32[]{:S(2)}, u32[]{:S(2)}) collective-permute-start(bf16[1058,128]{1,0:T(8,128)(2,1)S(1)} %get-tuple-element.32), channel_id=1, source_target_pairs={{0,1},{1,0},{2,3},{3,2},{4,5},{5,4},{6,7},{7,6},{8,9},{9,8},{10,11... | collective-permute-start | bytes 812552 | tf_op jit(solution)/shard_map/ppermute | solution.py:170
  49.5 44.7 %collective-permute-start.10 = (bf16[1058,128]{1,0:T(8,128)(2,1)}, bf16[1058,128]{1,0:T(8,128)(2,1)S(1)}, u32[]{:S(2)}, u32[]{:S(2)}) collective-permute-start(bf16[1058,128]{1,0:T(8,128)(2,1)} %get-tuple-element.33), channel_id=1, source_target_pairs={{0,13},{1,12},{2,15},{3,14},{4,9},{5,8},{6,11},{7,10},{8,5},{9,4},... | collective-permute-start | bytes 812552 | tf_op jit(solution)/shard_map/ppermute | solution.py:170
  59.2 35.0 %collective-permute-start.11 = (bf16[1058,128]{1,0:T(8,128)(2,1)}, bf16[1058,128]{1,0:T(8,128)(2,1)}, u32[]{:S(2)}, u32[]{:S(2)}) collective-permute-start(bf16[1058,128]{1,0:T(8,128)(2,1)} %get-tuple-element.34), channel_id=1, source_target_pairs={{0,2},{1,3},{2,0},{3,1},{4,6},{5,7},{6,4},{7,5},{8,10},{9,11},{10,... | collective-permute-start | bytes 812552 | tf_op jit(solution)/shard_map/ppermute | solution.py:170
  62.3 37.9 %collective-permute-start.12 = (bf16[1058,128]{1,0:T(8,128)(2,1)}, bf16[1058,128]{1,0:T(8,128)(2,1)}, u32[]{:S(2)}, u32[]{:S(2)}) collective-permute-start(bf16[1058,128]{1,0:T(8,128)(2,1)} %get-tuple-element.35), channel_id=1, source_target_pairs={{0,14},{1,15},{2,12},{3,13},{4,10},{5,11},{6,8},{7,9},{8,6},{9,7},... | collective-permute-start | bytes 812552 | tf_op jit(solution)/shard_map/ppermute | solution.py:170
  76.8 23.5 %collective-permute-start.13 = (bf16[1058,128]{1,0:T(8,128)(2,1)}, bf16[1058,128]{1,0:T(8,128)(2,1)}, u32[]{:S(2)}, u32[]{:S(2)}) collective-permute-start(bf16[1058,128]{1,0:T(8,128)(2,1)} %get-tuple-element.36), channel_id=1, source_target_pairs={{0,3},{1,2},{2,1},{3,0},{4,7},{5,6},{6,5},{7,4},{8,11},{9,10},{10,... | collective-permute-start | bytes 812552 | tf_op jit(solution)/shard_map/ppermute | solution.py:170
  78.9 27.9 %collective-permute-start.14 = (bf16[1058,128]{1,0:T(8,128)(2,1)}, bf16[1058,128]{1,0:T(8,128)(2,1)}, u32[]{:S(2)}, u32[]{:S(2)}) collective-permute-start(bf16[1058,128]{1,0:T(8,128)(2,1)} %get-tuple-element.37), channel_id=1, source_target_pairs={{0,15},{1,14},{2,13},{3,12},{4,11},{5,10},{6,9},{7,8},{8,7},{9,6},... | collective-permute-start | bytes 812552 | tf_op jit(solution)/shard_map/ppermute | solution.py:170
  106.8 2.3 %copy-start.1 = (bf16[4,32,46,368]{3,1,2,0:T(8,128)(2,1)S(1)}, bf16[4,32,46,368]{3,1,2,0:T(8,128)(2,1)}, u32[]{:S(2)}) copy-start(bf16[4,32,46,368]{3,1,2,0:T(8,128)(2,1)} %param.6) | copy-start | bytes 13000708
  121.1 4.0 %collective-permute-start.15 = (f32[46,16,368]{2,1,0:T(8,128)S(1)}, f32[46,16,368]{2,1,0:T(8,128)S(1)}, u32[]{:S(2)}, u32[]{:S(2)}) collective-permute-start(f32[46,16,368]{2,1,0:T(8,128)S(1)} %get-tuple-element.40), channel_id=1, source_target_pairs={{0,16},{16,0},{1,17},{17,1},{2,18},{18,2},{3,19},{19,3},{4,20},{20... | collective-permute-start | bytes 3250184 | tf_op jit(solution)/shard_map/ppermute | solution.py:196

commit v3 on v2

v3 whole, which is shorter than its diff:
```python
import functools
import math

import jax
import jax.numpy as jnp
import numpy as np
from jax import lax
from jax.experimental import pallas as pl
from jax.experimental.pallas import tpu as pltpu
from jax.sharding import PartitionSpec as P

LAT = 361
LON = 720
LENGTH = 8
BAND = 48
FAR = 1 << 20
NORM = np.float32(math.sqrt(sum(math.exp(-2.0 * e / LENGTH) for e in range(BAND + 1))))
MIB = 1024 * 1024
LON_LIMIT = 24 * MIB
LAT_LIMIT = 26 * MIB
FIRST = 3
NT = (((1,), (1,)), ((), ()))
NN = (((1,), (0,)), ((), ()))


def round_up(value, multiple):
    return -(-value // multiple) * multiple


def sums_before(meta, first, starts, groups):
    total = jnp.int32(0)
    for g in range(groups):
        starts[g] = total
        total = total + meta[first + g]


def place_of(meta, first, starts, slab, slots, size):
    inside = (slots >= 0) & (slots < jnp.minimum(meta[first + slab], size))
    return jnp.where(inside, slots + starts[slab], FAR)


def weights(lag, real):
    inside = (lag >= 0) & (lag <= BAND) & real
    value = jnp.exp(lag.astype(jnp.float32) * (-1.0 / LENGTH)) / NORM
    return jnp.where(inside, value, 0.0).astype(jnp.bfloat16)


def lon_weights(groups, masks, meta, starts, table):
    lon_pad = table.shape[1]
    col_slots = lon_pad // groups
    col_rows = table.shape[0] // len(masks)
    sums_before(meta, 0, starts, groups)
    slots = lax.broadcasted_iota(jnp.int32, (1, lon_pad), 1)
    source = jnp.full_like(slots, FAR)
    for g in range(groups):
        source = jnp.minimum(source, place_of(meta, 0, starts, g, slots - g * col_slots, col_slots))
    own = lax.broadcasted_iota(jnp.int32, (col_rows, 1), 0)
    for n, mask in enumerate(masks):
        slab = meta[2 * groups] ^ mask
        lag = own + starts[slab] - source
        lag = jnp.where(lag < 0, lag + LON, lag)
        table[n * col_rows:(n + 1) * col_rows, :] = weights(lag, own < meta[slab])


def lon_kernel(groups, masks, meta, control, *refs):
    outs, (table, packed, starts) = refs[-3 - len(masks):-3], refs[-3:]
    members, row_slots, levels, lon_pad = control.shape
    lanes = members * levels
    col_slots = lon_pad // groups
    col_rows = table.shape[0] // len(masks)
    lon_weights(groups, masks, meta, starts, table)
    for i in range(0, row_slots, 2):
        count = min(2, row_slots - i)
        field = jnp.concatenate([control[:, i + r].reshape(lanes, lon_pad) for r in range(count)], axis=0)
        smooth = lax.dot_general(table[...], field, NT, preferred_element_type=jnp.float32)
        for n in range(len(masks)):
            for r in range(count):
                packed[n, (i + r) * col_slots:(i + r + 1) * col_slots, :] = smooth[
                    n * col_rows:n * col_rows + col_slots, r * lanes:(r + 1) * lanes
                ]
    for n in range(len(masks)):
        outs[n][...] = packed[n].astype(jnp.bfloat16)


def lat_weights(groups, row_slots, masks, meta, starts, table):
    lat_pad = table.shape[0]
    sums_before(meta, groups, starts, groups)
    down_slots = lax.broadcasted_iota(jnp.int32, (lat_pad, 1), 0)
    across_slots = lax.broadcasted_iota(jnp.int32, (1, lat_pad), 1)
    down, across = jnp.full_like(down_slots, FAR), jnp.full_like(across_slots, FAR)
    for g in range(groups):
        down = jnp.minimum(down, place_of(meta, groups, starts, g, down_slots - g * row_slots, row_slots))
        across = jnp.minimum(
            across, place_of(meta, groups, starts, meta[2 * groups] ^ masks[g], across_slots - g * row_slots, row_slots)
        )
    table[...] = weights(down - across, down < FAR)


def lat_columns(low, second, mixer, pert, table, field, kept, given):
    columns, half = kept.shape[:2]
    members, _, levels, lat_pad = pert.shape
    lanes = members * levels
    for c in range(0, columns, 2):
        part = jnp.concatenate(
            [field[pl.ds(c + r, lat_pad, columns), :].astype(jnp.bfloat16) for r in range(2)], axis=1
        )
        smooth = lax.dot_general(table[...], part, NN, preferred_element_type=jnp.float32).astype(jnp.bfloat16)
        for r in range(2):
            mixed = lax.dot_general(
                mixer[...], smooth[:, r * lanes:(r + 1) * lanes], NT, preferred_element_type=jnp.float32
            )
            total = mixed[:levels] * pert[0, low + c + r].astype(jnp.float32)
            for m in range(1, members):
                total = total + mixed[m * levels:(m + 1) * levels] * pert[m, low + c + r].astype(jnp.float32)
            kept[c + r] = jnp.where(second, total[half:], total[:half])
            given[c + r] = jnp.where(second, total[:half], total[half:])


def block_diagonal(vertical, copies):
    levels = vertical.shape[0]
    size = copies * levels
    place = lax.broadcasted_iota(jnp.int32, (size, levels), 0) - lax.broadcasted_iota(jnp.int32, (size, levels), 1)
    spread = place == 0
    across, down = (lax.broadcasted_iota(jnp.int32, (size, size), dim) for dim in (1, 0))
    same = (across < levels) & (down < levels)
    for m in range(1, copies):
        spread = spread | (place == m * levels)
        low, high = m * levels, (m + 1) * levels
        same = same | ((across >= low) & (across < high) & (down >= low) & (down < high))
    spread = jnp.where(spread, 1.0, 0.0).astype(jnp.bfloat16)
    tall = lax.dot_general(spread, vertical, NN, preferred_element_type=jnp.float32).astype(jnp.bfloat16)
    wide = lax.dot_general(tall, spread, NT, preferred_element_type=jnp.float32)
    return jnp.where(same, wide, 0.0).astype(jnp.bfloat16)


def lat_kernel(groups, row_slots, masks, meta, vertical, pert, *refs):
    received, (kept, given, mixer, table, field, starts) = refs[:groups], refs[groups:]
    columns = kept.shape[0]
    useful = row_slots * columns
    mixer[...] = block_diagonal(vertical[...], pert.shape[0])
    lat_weights(groups, row_slots, masks, meta, starts, table)
    for g in range(groups):
        field[g * useful:(g + 1) * useful, :] = received[g][...].astype(jnp.float32)
    lat_columns(0, meta[2 * groups + 1] == 1, mixer, pert, table, field, kept, given)


def sending_order(groups):
    quarter = groups // 4
    far = list(range(2 * quarter, 4 * quarter))
    near = list(range(quarter, 2 * quarter)) + list(range(1, quarter))
    order = []
    for n in range(2 * quarter):
        order += far[n:n + 1] + near[n:n + 1]
    return order


def per_device(control, perturbation, vertical, lat_counts, lon_counts):
    groups = lax.axis_size("grid")
    shares = lax.axis_size("mem")
    members, levels, row_slots, lon_pad = control.shape
    col_slots, lat_pad = perturbation.shape[2:]
    lanes = members * levels
    vmem = pl.BlockSpec(memory_space=pltpu.VMEM)
    smem = pl.BlockSpec(memory_space=pltpu.SMEM)
    hbm = pl.BlockSpec(memory_space=pl.ANY)
    places = jnp.stack([lax.axis_index("grid"), lax.axis_index("mem") if shares == 2 else 0]).astype(jnp.int32)
    meta = jnp.concatenate([lon_counts, lat_counts, places])
    pert = jnp.transpose(perturbation, (0, 2, 1, 3))

    fields = jnp.transpose(control, (0, 2, 1, 3))

    def lon_filter(masks, after):
        return list(pl.pallas_call(
            functools.partial(lon_kernel, groups, masks),
            out_shape=[jax.ShapeDtypeStruct((row_slots * col_slots, lanes), jnp.bfloat16)] * len(masks),
            in_specs=[smem, vmem] + [hbm] * len(after),
            out_specs=[vmem] * len(masks),
            scratch_shapes=[
                pltpu.VMEM((len(masks) * round_up(col_slots, 16), lon_pad), jnp.bfloat16),
                pltpu.VMEM((len(masks), row_slots * col_slots, lanes), jnp.float32),
                pltpu.SMEM((groups,), jnp.int32),
            ],
            compiler_params=pltpu.CompilerParams(vmem_limit_bytes=LON_LIMIT),
            name="lon_filter",
        )(meta, fields, *after))

    def send(mask, value):
        return lax.ppermute(value, "grid", [(g, g ^ mask) for g in range(groups)])

    order = sending_order(groups)
    masks = order + [0]
    values = lon_filter(order[:FIRST], [])
    values += lon_filter(masks[FIRST:], values[:1])
    received = [send(mask, value) if mask else value for mask, value in zip(masks, values)]

    half = levels // 2
    kept, given = pl.pallas_call(
        functools.partial(lat_kernel, groups, row_slots, masks),
        out_shape=[jax.ShapeDtypeStruct((col_slots, half, lat_pad), jnp.float32)] * 2,
        in_specs=[smem] + [vmem] * (2 + groups),
        out_specs=[vmem] * 2,
        scratch_shapes=[
            pltpu.VMEM((lanes, lanes), jnp.bfloat16),
            pltpu.VMEM((lat_pad, lat_pad), jnp.bfloat16),
            pltpu.VMEM((lat_pad * col_slots, lanes), jnp.float32),
            pltpu.SMEM((groups,), jnp.int32),
        ],
        compiler_params=pltpu.CompilerParams(vmem_limit_bytes=LAT_LIMIT),
        name="lat_filter",
    )(meta, vertical, pert, *received)
    if shares == 2:
        total = kept + lax.ppermute(given, "mem", [(0, 1), (1, 0)])
    else:
        total = lax.psum_scatter(
            jnp.concatenate([kept, given], axis=1), "mem", scatter_dimension=1, tiled=True
        )
    return jnp.transpose(total, (1, 0, 2))


def solution(mesh):
    in_specs = (P("mem", None, "grid", None), P("mem", None, "grid", None), P(), P(), P())
    out_specs = P("mem", "grid", None)
    return jax.shard_map(per_device, mesh=mesh, in_specs=in_specs, out_specs=out_specs, check_vma=False)
```

time: 127 us -> 122 us (0.961)
  waiting for transfers between devices: 48.1 us -> 75.5 us
  starting transfers between devices: 39.9 us -> 23.6 us
  Pallas kernels: 31.5 us -> 18.2 us
  local copies, waits for them, and re-layouts: 5.35 us -> 2.29 us
    ppermute x15, waiting for transfers between devices: 45.7 us -> 73.1 us  [send(): return lax.ppermute(value, 'grid', [(g, g ^ mask) for g in range(groups)])]
    ppermute x15, starting transfers between devices: 38.3 us -> 21.6 us  [send(): return lax.ppermute(value, 'grid', [(g, g ^ mask) for g in range(groups)])]
    pallas_call x2, Pallas kernels: 19.5 us -> 6.99 us  [lon_filter(): pl.pallas_call(functools.partial(lon_kernel, groups, masks), out_shape=[j...]
    unnamed x10 -> x6, local copies, waits for them, and re-layouts: 5.22 us -> 2.29 us
  transfers between devices with their start and end apart: 16 -> 16, of which waited for: 11 -> 11; matrix products, arithmetic and copies ran while one was open for 0% -> 0% of each run, Pallas kernels for 10% -> 4%
where the time goes in v3:
time: 122 us
  waiting for transfers between devices  75.5 us (62%)
  starting transfers between devices  23.6 us (19%)
  Pallas kernels  18.2 us (15%)
  local copies, waits for them, and re-layouts  2.29 us (2%)
  other arithmetic  1.88 us (2%)
    ppermute x15, waiting for transfers between devices, send(): return lax.ppermute(value, 'grid', [(g, g ^ mask) for g in range(groups)])  73.1 us
    ppermute x15, starting transfers between devices, send(): return lax.ppermute(value, 'grid', [(g, g ^ mask) for g in range(groups)])  21.6 us
    pallas_call x1, Pallas kernels, per_device(): pl.pallas_call(functools.partial(lat_kernel, groups, row_slots, masks), o...  11.3 us
    pallas_call x2, Pallas kernels, lon_filter(): pl.pallas_call(functools.partial(lon_kernel, groups, masks), out_shape=[j...  6.99 us
  transfers between devices with their start and end apart: 16, of which 11 were waited for; matrix products, arithmetic and copies ran while one was open for 0% of the time, Pallas kernels for 4%

profile of v3, /device:TPU:9, one launch (start us, length us, event | category | flops | bytes accessed | tf_op | source)
XLA Modules:
  0.0 121.5 jit_solution(17303656012352153136)
XLA Ops:
  0.0 0.7 pad_add_fusion.meta
  0.7 0.0 copy-start
  0.8 2.3 %copy-done = bf16[4,32,23,736]{3,1,2,0:T(8,128)(2,1)S(1)} copy-done((bf16[4,32,23,736]{3,1,2,0:T(8,128)(2,1)S(1)}, bf16[4,32,23,736]{3,1,2,0:T(8,128)(2,1)}, u32[]{:S(2)}) %copy-start) | copy-done | bytes 4333592
  3.0 2.3 %lon_filter.2 = (bf16[1058,128]{1,0:T(8,128)(2,1)S(1)}, bf16[1058,128]{1,0:T(8,128)(2,1)S(1)}, bf16[1058,128]{1,0:T(8,128)(2,1)S(1)}) custom-call(s32[34]{0:T(128)S(1)} %pad_add_fusion.meta, bf16[4,23,32,736]{3,2,1,0:T(8,128)(2,1)S(1)} %bitcast.6), custom_call_target="tpu_custom_call" | custom-call | tf_op jit(solution)/shard_map/lon_filter/pallas_call | solution.py:173
  5.3 0.1 collective-permute-start.1
  5.4 3.4 %collective-permute-start.2 = (bf16[1058,128]{1,0:T(8,128)(2,1)S(1)}, bf16[1058,128]{1,0:T(8,128)(2,1)S(1)}, u32[]{:S(2)}, u32[]{:S(2)}) collective-permute-start(bf16[1058,128]{1,0:T(8,128)(2,1)S(1)} %get-tuple-element.25), channel_id=1, source_target_pairs={{0,9},{1,8},{2,11},{3,10},{4,13},{5,12},{6,15},{7,14},{8,1},{9,0},... | collective-permute-start | bytes 812552 | tf_op jit(solution)/shard_map/ppermute | solution.py:188
  8.8 0.0 copy-start.2
  8.8 0.1 collective-permute-start
  8.9 0.0 copy-start.1
  8.9 4.7 %lon_filter.3 = (bf16[1058,128]{1,0:T(8,128)(2,1)S(1)}, bf16[1058,128]{1,0:T(8,128)(2,1)S(1)}, bf16[1058,128]{1,0:T(8,128)(2,1)S(1)}, bf16[1058,128]{1,0:T(8,128...) custom-call(s32[34]{0:T(128)S(1)} %pad_add_fusion.meta, ...), custom_call_target="tpu_custom_call" | custom-call | tf_op jit(solution)/shard_map/lon_filter/pallas_call | solution.py:173
  13.6 1.3 %collective-permute-start.3 = (bf16[1058,128]{1,0:T(8,128)(2,1)S(1)}, bf16[1058,128]{1,0:T(8,128)(2,1)S(1)}, u32[]{:S(2)}, u32[]{:S(2)}) collective-permute-start(bf16[1058,128]{1,0:T(8,128)(2,1)S(1)} %get-tuple-element.26), channel_id=1, source_target_pairs={{0,5},{1,4},{2,7},{3,6},{4,1},{5,0},{6,3},{7,2},{8,13},{9,12},{10,... | collective-permute-start | bytes 812552 | tf_op jit(solution)/shard_map/ppermute | solution.py:188
  14.9 3.3 %collective-permute-start.4 = (bf16[1058,128]{1,0:T(8,128)(2,1)S(1)}, bf16[1058,128]{1,0:T(8,128)(2,1)S(1)}, u32[]{:S(2)}, u32[]{:S(2)}) collective-permute-start(bf16[1058,128]{1,0:T(8,128)(2,1)S(1)} %get-tuple-element.27), channel_id=1, source_target_pairs={{0,10},{1,11},{2,8},{3,9},{4,14},{5,15},{6,12},{7,13},{8,2},{9,3},... | collective-permute-start | bytes 812552 | tf_op jit(solution)/shard_map/ppermute | solution.py:188
  18.2 0.0 collective-permute-done.1.refs_1_
  18.2 0.6 collective-permute-start.5
  18.7 5.8 %collective-permute-done.2.refs_2_ = bf16[1058,128]{1,0:T(8,128)(2,1)S(1)} collective-permute-done((bf16[1058,128]{1,0:T(8,128)(2,1)S(1)}, bf16[1058,128]{1,0:T(8,128)(2,1)S(1)}, u32[]{:S(2)}, u32[]{:S(2)}) %collective-permute-start.2) | collective-permute-done | bytes 270880 | tf_op jit(solution)/shard_map/ppermute | solution.py:188
  24.5 5.5 %collective-permute-start.6 = (bf16[1058,128]{1,0:T(8,128)(2,1)S(1)}, bf16[1058,128]{1,0:T(8,128)(2,1)S(1)}, u32[]{:S(2)}, u32[]{:S(2)}) collective-permute-start(bf16[1058,128]{1,0:T(8,128)(2,1)S(1)} %get-tuple-element.29), channel_id=1, source_target_pairs={{0,11},{1,10},{2,9},{3,8},{4,15},{5,14},{6,13},{7,12},{8,3},{9,2},... | collective-permute-start | bytes 812552 | tf_op jit(solution)/shard_map/ppermute | solution.py:188
  30.0 6.2 %collective-permute-done.refs_0_ = bf16[1058,128]{1,0:T(8,128)(2,1)S(1)} collective-permute-done((bf16[1058,128]{1,0:T(8,128)(2,1)S(1)}, bf16[1058,128]{1,0:T(8,128)(2,1)S(1)}, u32[]{:S(2)}, u32[]{:S(2)}) %collective-permute-start) | collective-permute-done | bytes 270880 | tf_op jit(solution)/shard_map/ppermute | solution.py:188
  36.2 0.0 collective-permute-start.7
  36.2 0.0 collective-permute-done.3.refs_3_
  36.2 0.4 collective-permute-start.8
  36.7 6.8 %collective-permute-done.4.refs_4_ = bf16[1058,128]{1,0:T(8,128)(2,1)S(1)} collective-permute-done((bf16[1058,128]{1,0:T(8,128)(2,1)S(1)}, bf16[1058,128]{1,0:T(8,128)(2,1)S(1)}, u32[]{:S(2)}, u32[]{:S(2)}) %collective-permute-start.4) | collective-permute-done | bytes 270880 | tf_op jit(solution)/shard_map/ppermute | solution.py:188
  43.5 0.0 collective-permute-start.9
  43.5 0.6 collective-permute-done.5.refs_5_
  44.0 1.2 %collective-permute-start.10 = (bf16[1058,128]{1,0:T(8,128)(2,1)S(1)}, bf16[1058,128]{1,0:T(8,128)(2,1)S(1)}, u32[]{:S(2)}, u32[]{:S(2)}) collective-permute-start(bf16[1058,128]{1,0:T(8,128)(2,1)S(1)} %get-tuple-element.33), channel_id=1, source_target_pairs={{0,13},{1,12},{2,15},{3,14},{4,9},{5,8},{6,11},{7,10},{8,5},{9,4},... | collective-permute-start | bytes 812552 | tf_op jit(solution)/shard_map/ppermute | solution.py:188
  45.3 9.8 %collective-permute-done.6.refs_6_ = bf16[1058,128]{1,0:T(8,128)(2,1)S(1)} collective-permute-done((bf16[1058,128]{1,0:T(8,128)(2,1)S(1)}, bf16[1058,128]{1,0:T(8,128)(2,1)S(1)}, u32[]{:S(2)}, u32[]{:S(2)}) %collective-permute-start.6) | collective-permute-done | bytes 270880 | tf_op jit(solution)/shard_map/ppermute | solution.py:188
  55.0 1.3 %collective-permute-start.11 = (bf16[1058,128]{1,0:T(8,128)(2,1)S(1)}, bf16[1058,128]{1,0:T(8,128)(2,1)S(1)}, u32[]{:S(2)}, u32[]{:S(2)}) collective-permute-start(bf16[1058,128]{1,0:T(8,128)(2,1)S(1)} %get-tuple-element.34), channel_id=1, source_target_pairs={{0,2},{1,3},{2,0},{3,1},{4,6},{5,7},{6,4},{7,5},{8,10},{9,11},{10,... | collective-permute-start | bytes 812552 | tf_op jit(solution)/shard_map/ppermute | solution.py:188
  56.4 0.4 collective-permute-done.7.refs_7_
  56.7 1.1 collective-permute-start.12
  57.8 22.6 %collective-permute-done.8.refs_8_ = bf16[1058,128]{1,0:T(8,128)(2,1)S(1)} collective-permute-done((bf16[1058,128]{1,0:T(8,128)(2,1)S(1)}, bf16[1058,128]{1,0:T(8,128)(2,1)S(1)}, u32[]{:S(2)}, u32[]{:S(2)}) %collective-permute-start.8) | collective-permute-done | bytes 270880 | tf_op jit(solution)/shard_map/ppermute | solution.py:188
  80.5 0.5 collective-permute-start.13
  81.0 0.0 collective-permute-done.9.refs_9_
  81.0 2.8 %collective-permute-start.14 = (bf16[1058,128]{1,0:T(8,128)(2,1)S(1)}, bf16[1058,128]{1,0:T(8,128)(2,1)S(1)}, u32[]{:S(2)}, u32[]{:S(2)}) collective-permute-start(bf16[1058,128]{1,0:T(8,128)(2,1)S(1)} %get-tuple-element.37), channel_id=1, source_target_pairs={{0,15},{1,14},{2,13},{3,12},{4,11},{5,10},{6,9},{7,8},{8,7},{9,6},... | collective-permute-start | bytes 812552 | tf_op jit(solution)/shard_map/ppermute | solution.py:188
  83.8 4.3 %collective-permute-done.10.refs_10_ = bf16[1058,128]{1,0:T(8,128)(2,1)S(1)} collective-permute-done((bf16[1058,128]{1,0:T(8,128)(2,1)S(1)}, bf16[1058,128]{1,0:T(8,128)(2,1)S(1)}, u32[]{:S(2)}, u32[]{:S(2)}) %collective-permute-start.10) | collective-permute-done | bytes 270880 | tf_op jit(solution)/shard_map/ppermute | solution.py:188
  88.1 0.0 collective-permute-done.11.refs_11_
  88.1 11.0 %collective-permute-done.12.refs_12_ = bf16[1058,128]{1,0:T(8,128)(2,1)S(1)} collective-permute-done((bf16[1058,128]{1,0:T(8,128)(2,1)S(1)}, bf16[1058,128]{1,0:T(8,128)(2,1)S(1)}, u32[]{:S(2)}, u32[]{:S(2)}) %collective-permute-start.12) | collective-permute-done | bytes 270880 | tf_op jit(solution)/shard_map/ppermute | solution.py:188
  99.1 0.0 collective-permute-done.13.refs_13_
  99.1 5.6 %collective-permute-done.14.refs_14_ = bf16[1058,128]{1,0:T(8,128)(2,1)S(1)} collective-permute-done((bf16[1058,128]{1,0:T(8,128)(2,1)S(1)}, bf16[1058,128]{1,0:T(8,128)(2,1)S(1)}, u32[]{:S(2)}, u32[]{:S(2)}) %collective-permute-start.14) | collective-permute-done | bytes 270880 | tf_op jit(solution)/shard_map/ppermute | solution.py:188
  104.7 0.0 copy-done.2
  104.7 0.0 copy-done.1
  104.7 11.3 %lat_filter.1 = (f32[46,16,368]{2,1,0:T(8,128)S(1)}, f32[46,16,368]{2,1,0:T(8,128)S(1)}) custom-call(s32[34]{0:T(128)S(1)} %pad_add_fusion.meta, bf16[32,32]{1,0:T(8,128)(2,1)S(1)} %copy-done.2, bf16[4,46,32,368]{3,2,1,0:T(8,128)(2,1)S(1)} %bitcast.8, bf16[1058,128]{1,0:T(8,128)(2,1)S(1)} %collective-permute-done.refs_0_, ...), custom_call_target="tpu_custom_call" | custom-call | tf_op jit(solution)/shard_map/lat_filter/pallas_call | solution.py:197
  116.0 2.0 %collective-permute-start.15 = (f32[46,16,368]{2,1,0:T(8,128)S(1)}, f32[46,16,368]{2,1,0:T(8,128)S(1)}, u32[]{:S(2)}, u32[]{:S(2)}) collective-permute-start(f32[46,16,368]{2,1,0:T(8,128)S(1)} %get-tuple-element.40), channel_id=1, source_target_pairs={{0,16},{16,0},{1,17},{17,1},{2,18},{18,2},{3,19},{19,3},{4,20},{20... | collective-permute-start | bytes 3250184 | tf_op jit(solution)/shard_map/ppermute | solution.py:212
  118.0 2.4 %collective-permute-done.15 = f32[46,16,368]{2,1,0:T(8,128)S(1)} collective-permute-done((f32[46,16,368]{2,1,0:T(8,128)S(1)}, f32[46,16,368]{2,1,0:T(8,128)S(1)}, u32[]{:S(2)}, u32[]{:S(2)}) %collective-permute-start.15) | collective-permute-done | bytes 1083424 | tf_op jit(solution)/shard_map/ppermute | solution.py:212
  120.4 1.1 add_bitcast_fusion
Async XLA Ops:
  0.7 2.3 %copy-start = (bf16[4,32,23,736]{3,1,2,0:T(8,128)(2,1)S(1)}, bf16[4,32,23,736]{3,1,2,0:T(8,128)(2,1)}, u32[]{:S(2)}) copy-start(bf16[4,32,23,736]{3,1,2,0:T(8,128)(2,1)} %param.5) | copy-start | bytes 13000708
  5.3 12.8 %collective-permute-start.1 = (bf16[1058,128]{1,0:T(8,128)(2,1)S(1)}, bf16[1058,128]{1,0:T(8,128)(2,1)S(1)}, u32[]{:S(2)}, u32[]{:S(2)}) collective-permute-start(bf16[1058,128]{1,0:T(8,128)(2,1)S(1)} %get-tuple-element.24), channel_id=1, source_target_pairs={{0,4},{1,5},{2,6},{3,7},{4,0},{5,1},{6,2},{7,3},{8,12},{9,13},{10,... | collective-permute-start | bytes 812552 | tf_op jit(solution)/shard_map/ppermute | solution.py:188
  5.4 19.1 %collective-permute-start.2 = (bf16[1058,128]{1,0:T(8,128)(2,1)S(1)}, bf16[1058,128]{1,0:T(8,128)(2,1)S(1)}, u32[]{:S(2)}, u32[]{:S(2)}) collective-permute-start(bf16[1058,128]{1,0:T(8,128)(2,1)S(1)} %get-tuple-element.25), channel_id=1, source_target_pairs={{0,9},{1,8},{2,11},{3,10},{4,13},{5,12},{6,15},{7,14},{8,1},{9,0},... | collective-permute-start | bytes 812552 | tf_op jit(solution)/shard_map/ppermute | solution.py:188
  8.8 95.9 %copy-start.2 = (bf16[32,32]{1,0:T(8,128)(2,1)S(1)}, bf16[32,32]{1,0:T(8,128)(2,1)}, u32[]{:S(2)}) copy-start(bf16[32,32]{1,0:T(8,128)(2,1)} %vertical.1) | copy-start | bytes 6148
  8.8 27.4 %collective-permute-start = (bf16[1058,128]{1,0:T(8,128)(2,1)S(1)}, bf16[1058,128]{1,0:T(8,128)(2,1)S(1)}, u32[]{:S(2)}, u32[]{:S(2)}) collective-permute-start(bf16[1058,128]{1,0:T(8,128)(2,1)S(1)} %get-tuple-element.23.refs_0_), channel_id=1, source_target_pairs={{0,8},{1,9},{2,10},{3,11},{4,12},{5,13},{6,14},{7,15},{8,0},{9,1},... | collective-permute-start | bytes 812552 | tf_op jit(solution)/shard_map/ppermute | solution.py:188
  8.9 95.8 %copy-start.1 = (bf16[4,32,46,368]{3,1,2,0:T(8,128)(2,1)S(1)}, bf16[4,32,46,368]{3,1,2,0:T(8,128)(2,1)}, u32[]{:S(2)}) copy-start(bf16[4,32,46,368]{3,1,2,0:T(8,128)(2,1)} %param.6) | copy-start | bytes 13000708
  13.6 22.7 %collective-permute-start.3 = (bf16[1058,128]{1,0:T(8,128)(2,1)S(1)}, bf16[1058,128]{1,0:T(8,128)(2,1)S(1)}, u32[]{:S(2)}, u32[]{:S(2)}) collective-permute-start(bf16[1058,128]{1,0:T(8,128)(2,1)S(1)} %get-tuple-element.26), channel_id=1, source_target_pairs={{0,5},{1,4},{2,7},{3,6},{4,1},{5,0},{6,3},{7,2},{8,13},{9,12},{10,... | collective-permute-start | bytes 812552 | tf_op jit(solution)/shard_map/ppermute | solution.py:188
  14.9 28.6 %collective-permute-start.4 = (bf16[1058,128]{1,0:T(8,128)(2,1)S(1)}, bf16[1058,128]{1,0:T(8,128)(2,1)S(1)}, u32[]{:S(2)}, u32[]{:S(2)}) collective-permute-start(bf16[1058,128]{1,0:T(8,128)(2,1)S(1)} %get-tuple-element.27), channel_id=1, source_target_pairs={{0,10},{1,11},{2,8},{3,9},{4,14},{5,15},{6,12},{7,13},{8,2},{9,3},... | collective-permute-start | bytes 812552 | tf_op jit(solution)/shard_map/ppermute | solution.py:188
  18.2 25.9 %collective-permute-start.5 = (bf16[1058,128]{1,0:T(8,128)(2,1)S(1)}, bf16[1058,128]{1,0:T(8,128)(2,1)S(1)}, u32[]{:S(2)}, u32[]{:S(2)}) collective-permute-start(bf16[1058,128]{1,0:T(8,128)(2,1)S(1)} %get-tuple-element.28), channel_id=1, source_target_pairs={{0,6},{1,7},{2,4},{3,5},{4,2},{5,3},{6,0},{7,1},{8,14},{9,15},{10,... | collective-permute-start | bytes 812552 | tf_op jit(solution)/shard_map/ppermute | solution.py:188
  24.5 30.5 %collective-permute-start.6 = (bf16[1058,128]{1,0:T(8,128)(2,1)S(1)}, bf16[1058,128]{1,0:T(8,128)(2,1)S(1)}, u32[]{:S(2)}, u32[]{:S(2)}) collective-permute-start(bf16[1058,128]{1,0:T(8,128)(2,1)S(1)} %get-tuple-element.29), channel_id=1, source_target_pairs={{0,11},{1,10},{2,9},{3,8},{4,15},{5,14},{6,13},{7,12},{8,3},{9,2},... | collective-permute-start | bytes 812552 | tf_op jit(solution)/shard_map/ppermute | solution.py:188
  36.2 20.5 %collective-permute-start.7 = (bf16[1058,128]{1,0:T(8,128)(2,1)S(1)}, bf16[1058,128]{1,0:T(8,128)(2,1)S(1)}, u32[]{:S(2)}, u32[]{:S(2)}) collective-permute-start(bf16[1058,128]{1,0:T(8,128)(2,1)S(1)} %get-tuple-element.30), channel_id=1, source_target_pairs={{0,7},{1,6},{2,5},{3,4},{4,3},{5,2},{6,1},{7,0},{8,15},{9,14},{10,... | collective-permute-start | bytes 812552 | tf_op jit(solution)/shard_map/ppermute | solution.py:188
  36.2 44.2 %collective-permute-start.8 = (bf16[1058,128]{1,0:T(8,128)(2,1)S(1)}, bf16[1058,128]{1,0:T(8,128)(2,1)S(1)}, u32[]{:S(2)}, u32[]{:S(2)}) collective-permute-start(bf16[1058,128]{1,0:T(8,128)(2,1)S(1)} %get-tuple-element.31), channel_id=1, source_target_pairs={{0,12},{1,13},{2,14},{3,15},{4,8},{5,9},{6,10},{7,11},{8,4},{9,5},... | collective-permute-start | bytes 812552 | tf_op jit(solution)/shard_map/ppermute | solution.py:188
  43.5 37.5 %collective-permute-start.9 = (bf16[1058,128]{1,0:T(8,128)(2,1)S(1)}, bf16[1058,128]{1,0:T(8,128)(2,1)S(1)}, u32[]{:S(2)}, u32[]{:S(2)}) collective-permute-start(bf16[1058,128]{1,0:T(8,128)(2,1)S(1)} %get-tuple-element.32), channel_id=1, source_target_pairs={{0,1},{1,0},{2,3},{3,2},{4,5},{5,4},{6,7},{7,6},{8,9},{9,8},{10,11... | collective-permute-start | bytes 812552 | tf_op jit(solution)/shard_map/ppermute | solution.py:188
  44.0 44.1 %collective-permute-start.10 = (bf16[1058,128]{1,0:T(8,128)(2,1)S(1)}, bf16[1058,128]{1,0:T(8,128)(2,1)S(1)}, u32[]{:S(2)}, u32[]{:S(2)}) collective-permute-start(bf16[1058,128]{1,0:T(8,128)(2,1)S(1)} %get-tuple-element.33), channel_id=1, source_target_pairs={{0,13},{1,12},{2,15},{3,14},{4,9},{5,8},{6,11},{7,10},{8,5},{9,4},... | collective-permute-start | bytes 812552 | tf_op jit(solution)/shard_map/ppermute | solution.py:188
  55.0 33.1 %collective-permute-start.11 = (bf16[1058,128]{1,0:T(8,128)(2,1)S(1)}, bf16[1058,128]{1,0:T(8,128)(2,1)S(1)}, u32[]{:S(2)}, u32[]{:S(2)}) collective-permute-start(bf16[1058,128]{1,0:T(8,128)(2,1)S(1)} %get-tuple-element.34), channel_id=1, source_target_pairs={{0,2},{1,3},{2,0},{3,1},{4,6},{5,7},{6,4},{7,5},{8,10},{9,11},{10,... | collective-permute-start | bytes 812552 | tf_op jit(solution)/shard_map/ppermute | solution.py:188
  56.7 42.4 %collective-permute-start.12 = (bf16[1058,128]{1,0:T(8,128)(2,1)S(1)}, bf16[1058,128]{1,0:T(8,128)(2,1)S(1)}, u32[]{:S(2)}, u32[]{:S(2)}) collective-permute-start(bf16[1058,128]{1,0:T(8,128)(2,1)S(1)} %get-tuple-element.35), channel_id=1, source_target_pairs={{0,14},{1,15},{2,12},{3,13},{4,10},{5,11},{6,8},{7,9},{8,6},{9,7},... | collective-permute-start | bytes 812552 | tf_op jit(solution)/shard_map/ppermute | solution.py:188
  80.5 18.6 %collective-permute-start.13 = (bf16[1058,128]{1,0:T(8,128)(2,1)S(1)}, bf16[1058,128]{1,0:T(8,128)(2,1)S(1)}, u32[]{:S(2)}, u32[]{:S(2)}) collective-permute-start(bf16[1058,128]{1,0:T(8,128)(2,1)S(1)} %get-tuple-element.36), channel_id=1, source_target_pairs={{0,3},{1,2},{2,1},{3,0},{4,7},{5,6},{6,5},{7,4},{8,11},{9,10},{10,... | collective-permute-start | bytes 812552 | tf_op jit(solution)/shard_map/ppermute | solution.py:188
  81.0 23.7 %collective-permute-start.14 = (bf16[1058,128]{1,0:T(8,128)(2,1)S(1)}, bf16[1058,128]{1,0:T(8,128)(2,1)S(1)}, u32[]{:S(2)}, u32[]{:S(2)}) collective-permute-start(bf16[1058,128]{1,0:T(8,128)(2,1)S(1)} %get-tuple-element.37), channel_id=1, source_target_pairs={{0,15},{1,14},{2,13},{3,12},{4,11},{5,10},{6,9},{7,8},{8,7},{9,6},... | collective-permute-start | bytes 812552 | tf_op jit(solution)/shard_map/ppermute | solution.py:188
  116.0 4.4 %collective-permute-start.15 = (f32[46,16,368]{2,1,0:T(8,128)S(1)}, f32[46,16,368]{2,1,0:T(8,128)S(1)}, u32[]{:S(2)}, u32[]{:S(2)}) collective-permute-start(f32[46,16,368]{2,1,0:T(8,128)S(1)} %get-tuple-element.40), channel_id=1, source_target_pairs={{0,16},{16,0},{1,17},{17,1},{2,18},{18,2},{3,19},{19,3},{4,20},{20... | collective-permute-start | bytes 3250184 | tf_op jit(solution)/shard_map/ppermute | solution.py:212

commit v4 on v3

--- a/solution.py
+++ b/solution.py
@@ -19,6 +19,7 @@
 LON_LIMIT = 24 * MIB
 LAT_LIMIT = 26 * MIB
 FIRST = 3
+AHEAD = 2
 NT = (((1,), (1,)), ((), ()))
 NN = (((1,), (0,)), ((), ()))
 
@@ -96,24 +97,35 @@
     table[...] = weights(down - across, down < FAR)
 
 
-def lat_columns(low, second, mixer, pert, table, field, kept, given):
+def lat_columns(second, mixer, pert, table, field, kept, given):
     columns, half = kept.shape[:2]
     members, _, levels, lat_pad = pert.shape
     lanes = members * levels
-    for c in range(0, columns, 2):
+
+    def filtered(c):
         part = jnp.concatenate(
             [field[pl.ds(c + r, lat_pad, columns), :].astype(jnp.bfloat16) for r in range(2)], axis=1
         )
-        smooth = lax.dot_general(table[...], part, NN, preferred_element_type=jnp.float32).astype(jnp.bfloat16)
+        return lax.dot_general(table[...], part, NN, preferred_element_type=jnp.float32).astype(jnp.bfloat16)
+
+    def finish(c, smooth):
         for r in range(2):
             mixed = lax.dot_general(
                 mixer[...], smooth[:, r * lanes:(r + 1) * lanes], NT, preferred_element_type=jnp.float32
             )
-            total = mixed[:levels] * pert[0, low + c + r].astype(jnp.float32)
+            total = mixed[:levels] * pert[0, c + r].astype(jnp.float32)
             for m in range(1, members):
-                total = total + mixed[m * levels:(m + 1) * levels] * pert[m, low + c + r].astype(jnp.float32)
+                total = total + mixed[m * levels:(m + 1) * levels] * pert[m, c + r].astype(jnp.float32)
             kept[c + r] = jnp.where(second, total[half:], total[:half])
-            given[c + r] = jnp.where(second, total[:half], total[half:])
+            given[c + r] = jnp.where(second, total[:half], total[half:]).astype(given.dtype)
+
+    ahead = []
+    for c in range(0, columns, 2):
+        ahead.append((c, filtered(c)))
+        if len(ahead) > AHEAD:
+            finish(*ahead.pop(0))
+    for item in ahead:
+        finish(*item)
 
 
 def block_diagonal(vertical, copies):
@@ -133,15 +145,17 @@
     return jnp.where(same, wide, 0.0).astype(jnp.bfloat16)
 
 
-def lat_kernel(groups, row_slots, masks, meta, vertical, pert, *refs):
-    received, (kept, given, mixer, table, field, starts) = refs[:groups], refs[groups:]
-    columns = kept.shape[0]
-    useful = row_slots * columns
-    mixer[...] = block_diagonal(vertical[...], pert.shape[0])
+def matrices_kernel(groups, row_slots, masks, meta, vertical, after, mixer, table, starts):
+    mixer[...] = block_diagonal(vertical[...], mixer.shape[0] // vertical.shape[0])
     lat_weights(groups, row_slots, masks, meta, starts, table)
+
+
+def lat_kernel(groups, meta, mixer, table, pert, *refs):
+    received, (kept, given, field) = refs[:groups], refs[groups:]
+    useful = received[0].shape[0]
     for g in range(groups):
         field[g * useful:(g + 1) * useful, :] = received[g][...].astype(jnp.float32)
-    lat_columns(0, meta[2 * groups + 1] == 1, mixer, pert, table, field, kept, given)
+    lat_columns(meta[2 * groups + 1] == 1, mixer, pert, table, field, kept, given)
 
 
 def sending_order(groups):
@@ -193,23 +207,34 @@
     values += lon_filter(masks[FIRST:], values[:1])
     received = [send(mask, value) if mask else value for mask, value in zip(masks, values)]
 
+    mixer, table = pl.pallas_call(
+        functools.partial(matrices_kernel, groups, row_slots, masks),
+        out_shape=[
+            jax.ShapeDtypeStruct((lanes, lanes), jnp.bfloat16),
+            jax.ShapeDtypeStruct((lat_pad, lat_pad), jnp.bfloat16),
+        ],
+        in_specs=[smem, vmem, hbm],
+        out_specs=[vmem] * 2,
+        scratch_shapes=[pltpu.SMEM((groups,), jnp.int32)],
+        compiler_params=pltpu.CompilerParams(vmem_limit_bytes=4 * MIB),
+        name="matrices",
+    )(meta, vertical, values[-1])
+
     half = levels // 2
     kept, given = pl.pallas_call(
-        functools.partial(lat_kernel, groups, row_slots, masks),
-        out_shape=[jax.ShapeDtypeStruct((col_slots, half, lat_pad), jnp.float32)] * 2,
-        in_specs=[smem] + [vmem] * (2 + groups),
+        functools.partial(lat_kernel, groups),
+        out_shape=[
+            jax.ShapeDtypeStruct((col_slots, half, lat_pad), jnp.float32),
+            jax.ShapeDtypeStruct((col_slots, half, lat_pad), jnp.bfloat16 if shares == 2 else jnp.float32),
+        ],
+        in_specs=[smem] + [vmem] * (3 + groups),
         out_specs=[vmem] * 2,
-        scratch_shapes=[
-            pltpu.VMEM((lanes, lanes), jnp.bfloat16),
-            pltpu.VMEM((lat_pad, lat_pad), jnp.bfloat16),
-            pltpu.VMEM((lat_pad * col_slots, lanes), jnp.float32),
-            pltpu.SMEM((groups,), jnp.int32),
-        ],
+        scratch_shapes=[pltpu.VMEM((lat_pad * col_slots, lanes), jnp.float32)],
         compiler_params=pltpu.CompilerParams(vmem_limit_bytes=LAT_LIMIT),
         name="lat_filter",
-    )(meta, vertical, pert, *received)
+    )(meta, mixer, table, pert, *received)
     if shares == 2:
-        total = kept + lax.ppermute(given, "mem", [(0, 1), (1, 0)])
+        total = kept + lax.ppermute(given, "mem", [(0, 1), (1, 0)]).astype(jnp.float32)
     else:
         total = lax.psum_scatter(
             jnp.concatenate([kept, given], axis=1), "mem", scatter_dimension=1, tiled=True

time: 122 us -> 115 us (0.943)
  Pallas kernels: 18.2 us -> 13.6 us
  waiting for transfers between devices: 75.5 us -> 73.4 us
    pallas_call x1 -> x2, Pallas kernels: 11.3 us -> 6.64 us  [the longest x1 5.1 us: per_device(): pl.pallas_call(functools.partial(lat_kernel, groups), out_shape=[jax.Shap...]
    ppermute x15, waiting for transfers between devices: 73.1 us -> 71.8 us  [send(): return lax.ppermute(value, 'grid', [(g, g ^ mask) for g in range(groups)])]
  transfers between devices with their start and end apart: 16 -> 16, of which waited for: 11 -> 11; matrix products, arithmetic and copies ran while one was open for 0% -> 0% of each run, Pallas kernels for 4% -> 5%
where the time goes in v4:
time: 115 us
  waiting for transfers between devices  73.4 us (64%)
  starting transfers between devices  23.3 us (20%)
  Pallas kernels  13.6 us (12%)
  local copies, waits for them, and re-layouts  2.29 us (2%)
  other arithmetic  1.92 us (2%)
    ppermute x15, waiting for transfers between devices, send(): return lax.ppermute(value, 'grid', [(g, g ^ mask) for g in range(groups)])  71.8 us
    ppermute x15, starting transfers between devices, send(): return lax.ppermute(value, 'grid', [(g, g ^ mask) for g in range(groups)])  21.3 us
    pallas_call x2, Pallas kernels, lon_filter(): pl.pallas_call(functools.partial(lon_kernel, groups, masks), out_shape=[j...  6.99 us
    pallas_call x1, Pallas kernels, per_device(): pl.pallas_call(functools.partial(lat_kernel, groups), out_shape=[jax.Shap...  5.1 us
  transfers between devices with their start and end apart: 16, of which 11 were waited for; matrix products, arithmetic and copies ran while one was open for 0% of the time, Pallas kernels for 5%

profile of v4, /device:TPU:9, one launch (start us, length us, event | category | flops | bytes accessed | tf_op | source)
XLA Modules:
  0.0 114.6 jit_solution(14007867888885546872)
XLA Ops:
  0.0 0.7 pad_add_fusion.meta
  0.7 0.0 copy-start
  0.8 2.3 %copy-done = bf16[4,32,23,736]{3,1,2,0:T(8,128)(2,1)S(1)} copy-done((bf16[4,32,23,736]{3,1,2,0:T(8,128)(2,1)S(1)}, bf16[4,32,23,736]{3,1,2,0:T(8,128)(2,1)}, u32[]{:S(2)}) %copy-start) | copy-done | bytes 4333592
  3.0 2.3 %lon_filter.2 = (bf16[1058,128]{1,0:T(8,128)(2,1)S(1)}, bf16[1058,128]{1,0:T(8,128)(2,1)S(1)}, bf16[1058,128]{1,0:T(8,128)(2,1)S(1)}) custom-call(s32[34]{0:T(128)S(1)} %pad_add_fusion.meta, bf16[4,23,32,736]{3,2,1,0:T(8,128)(2,1)S(1)} %bitcast.6), custom_call_target="tpu_custom_call" | custom-call | tf_op jit(solution)/shard_map/lon_filter/pallas_call | solution.py:187
  5.3 0.1 collective-permute-start.1
  5.4 3.4 %collective-permute-start.2 = (bf16[1058,128]{1,0:T(8,128)(2,1)S(1)}, bf16[1058,128]{1,0:T(8,128)(2,1)S(1)}, u32[]{:S(2)}, u32[]{:S(2)}) collective-permute-start(bf16[1058,128]{1,0:T(8,128)(2,1)S(1)} %get-tuple-element.30), channel_id=1, source_target_pairs={{0,9},{1,8},{2,11},{3,10},{4,13},{5,12},{6,15},{7,14},{8,1},{9,0},... | collective-permute-start | bytes 812552 | tf_op jit(solution)/shard_map/ppermute | solution.py:202
  8.8 0.0 copy-start.2
  8.8 0.1 collective-permute-start
  8.9 0.0 copy-start.1
  8.9 4.7 %lon_filter.3 = (bf16[1058,128]{1,0:T(8,128)(2,1)S(1)}, bf16[1058,128]{1,0:T(8,128)(2,1)S(1)}, bf16[1058,128]{1,0:T(8,128)(2,1)S(1)}, bf16[1058,128]{1,0:T(8,128...) custom-call(s32[34]{0:T(128)S(1)} %pad_add_fusion.meta, ...), custom_call_target="tpu_custom_call" | custom-call | tf_op jit(solution)/shard_map/lon_filter/pallas_call | solution.py:187
  13.6 1.3 %collective-permute-start.3 = (bf16[1058,128]{1,0:T(8,128)(2,1)S(1)}, bf16[1058,128]{1,0:T(8,128)(2,1)S(1)}, u32[]{:S(2)}, u32[]{:S(2)}) collective-permute-start(bf16[1058,128]{1,0:T(8,128)(2,1)S(1)} %get-tuple-element.31), channel_id=1, source_target_pairs={{0,5},{1,4},{2,7},{3,6},{4,1},{5,0},{6,3},{7,2},{8,13},{9,12},{10,... | collective-permute-start | bytes 812552 | tf_op jit(solution)/shard_map/ppermute | solution.py:202
  14.9 3.3 %collective-permute-start.4 = (bf16[1058,128]{1,0:T(8,128)(2,1)S(1)}, bf16[1058,128]{1,0:T(8,128)(2,1)S(1)}, u32[]{:S(2)}, u32[]{:S(2)}) collective-permute-start(bf16[1058,128]{1,0:T(8,128)(2,1)S(1)} %get-tuple-element.32), channel_id=1, source_target_pairs={{0,10},{1,11},{2,8},{3,9},{4,14},{5,15},{6,12},{7,13},{8,2},{9,3},... | collective-permute-start | bytes 812552 | tf_op jit(solution)/shard_map/ppermute | solution.py:202
  18.2 0.0 collective-permute-done.1.refs_1_
  18.2 0.6 collective-permute-start.5
  18.7 5.9 %collective-permute-done.2.refs_2_ = bf16[1058,128]{1,0:T(8,128)(2,1)S(1)} collective-permute-done((bf16[1058,128]{1,0:T(8,128)(2,1)S(1)}, bf16[1058,128]{1,0:T(8,128)(2,1)S(1)}, u32[]{:S(2)}, u32[]{:S(2)}) %collective-permute-start.2) | collective-permute-done | bytes 270880 | tf_op jit(solution)/shard_map/ppermute | solution.py:202
  24.6 5.5 %collective-permute-start.6 = (bf16[1058,128]{1,0:T(8,128)(2,1)S(1)}, bf16[1058,128]{1,0:T(8,128)(2,1)S(1)}, u32[]{:S(2)}, u32[]{:S(2)}) collective-permute-start(bf16[1058,128]{1,0:T(8,128)(2,1)S(1)} %get-tuple-element.34), channel_id=1, source_target_pairs={{0,11},{1,10},{2,9},{3,8},{4,15},{5,14},{6,13},{7,12},{8,3},{9,2},... | collective-permute-start | bytes 812552 | tf_op jit(solution)/shard_map/ppermute | solution.py:202
  30.0 6.3 %collective-permute-done.refs_0_ = bf16[1058,128]{1,0:T(8,128)(2,1)S(1)} collective-permute-done((bf16[1058,128]{1,0:T(8,128)(2,1)S(1)}, bf16[1058,128]{1,0:T(8,128)(2,1)S(1)}, u32[]{:S(2)}, u32[]{:S(2)}) %collective-permute-start) | collective-permute-done | bytes 270880 | tf_op jit(solution)/shard_map/ppermute | solution.py:202
  36.3 0.0 collective-permute-start.7
  36.3 0.0 collective-permute-done.3.refs_3_
  36.3 0.3 collective-permute-start.8
  36.7 6.9 %collective-permute-done.4.refs_4_ = bf16[1058,128]{1,0:T(8,128)(2,1)S(1)} collective-permute-done((bf16[1058,128]{1,0:T(8,128)(2,1)S(1)}, bf16[1058,128]{1,0:T(8,128)(2,1)S(1)}, u32[]{:S(2)}, u32[]{:S(2)}) %collective-permute-start.4) | collective-permute-done | bytes 270880 | tf_op jit(solution)/shard_map/ppermute | solution.py:202
  43.5 0.0 collective-permute-start.9
  43.5 0.5 collective-permute-done.5.refs_5_
  44.0 1.2 %collective-permute-start.10 = (bf16[1058,128]{1,0:T(8,128)(2,1)S(1)}, bf16[1058,128]{1,0:T(8,128)(2,1)S(1)}, u32[]{:S(2)}, u32[]{:S(2)}) collective-permute-start(bf16[1058,128]{1,0:T(8,128)(2,1)S(1)} %get-tuple-element.38), channel_id=1, source_target_pairs={{0,13},{1,12},{2,15},{3,14},{4,9},{5,8},{6,11},{7,10},{8,5},{9,4},... | collective-permute-start | bytes 812552 | tf_op jit(solution)/shard_map/ppermute | solution.py:202
  45.3 9.9 %collective-permute-done.6.refs_6_ = bf16[1058,128]{1,0:T(8,128)(2,1)S(1)} collective-permute-done((bf16[1058,128]{1,0:T(8,128)(2,1)S(1)}, bf16[1058,128]{1,0:T(8,128)(2,1)S(1)}, u32[]{:S(2)}, u32[]{:S(2)}) %collective-permute-start.6) | collective-permute-done | bytes 270880 | tf_op jit(solution)/shard_map/ppermute | solution.py:202
  55.1 1.2 %collective-permute-start.11 = (bf16[1058,128]{1,0:T(8,128)(2,1)S(1)}, bf16[1058,128]{1,0:T(8,128)(2,1)S(1)}, u32[]{:S(2)}, u32[]{:S(2)}) collective-permute-start(bf16[1058,128]{1,0:T(8,128)(2,1)S(1)} %get-tuple-element.39), channel_id=1, source_target_pairs={{0,2},{1,3},{2,0},{3,1},{4,6},{5,7},{6,4},{7,5},{8,10},{9,11},{10,... | collective-permute-start | bytes 812552 | tf_op jit(solution)/shard_map/ppermute | solution.py:202
  56.3 0.4 collective-permute-done.7.refs_7_
  56.7 1.1 collective-permute-start.12
  57.9 22.6 %collective-permute-done.8.refs_8_ = bf16[1058,128]{1,0:T(8,128)(2,1)S(1)} collective-permute-done((bf16[1058,128]{1,0:T(8,128)(2,1)S(1)}, bf16[1058,128]{1,0:T(8,128)(2,1)S(1)}, u32[]{:S(2)}, u32[]{:S(2)}) %collective-permute-start.8) | collective-permute-done | bytes 270880 | tf_op jit(solution)/shard_map/ppermute | solution.py:202
  80.5 0.5 collective-permute-start.13
  81.0 0.0 collective-permute-done.9.refs_9_
  81.0 2.8 %collective-permute-start.14 = (bf16[1058,128]{1,0:T(8,128)(2,1)S(1)}, bf16[1058,128]{1,0:T(8,128)(2,1)S(1)}, u32[]{:S(2)}, u32[]{:S(2)}) collective-permute-start(bf16[1058,128]{1,0:T(8,128)(2,1)S(1)} %get-tuple-element.42), channel_id=1, source_target_pairs={{0,15},{1,14},{2,13},{3,12},{4,11},{5,10},{6,9},{7,8},{8,7},{9,6},... | collective-permute-start | bytes 812552 | tf_op jit(solution)/shard_map/ppermute | solution.py:202
  83.8 0.0 copy-done.2
  83.8 1.5 %matrices.1 = (bf16[128,128]{1,0:T(8,128)(2,1)S(1)}, bf16[368,368]{1,0:T(8,128)(2,1)S(1)}) custom-call(s32[34]{0:T(128)S(1)} %pad_add_fusion.meta, bf16[32,32]{1,0:T(8,128)(2,1)S(1)} %copy-done.2, bf16[1058,128]{1,0:T(8,128)(2,1)S(1)} %get-tuple-element.26.after.refs_15_), custom_call_target="tpu_custom_call" | custom-call | tf_op jit(solution)/shard_map/matrices/pallas_call | solution.py:210
  85.4 2.8 %collective-permute-done.10.refs_10_ = bf16[1058,128]{1,0:T(8,128)(2,1)S(1)} collective-permute-done((bf16[1058,128]{1,0:T(8,128)(2,1)S(1)}, bf16[1058,128]{1,0:T(8,128)(2,1)S(1)}, u32[]{:S(2)}, u32[]{:S(2)}) %collective-permute-start.10) | collective-permute-done | bytes 270880 | tf_op jit(solution)/shard_map/ppermute | solution.py:202
  88.1 0.0 collective-permute-done.11.refs_11_
  88.1 10.9 %collective-permute-done.12.refs_12_ = bf16[1058,128]{1,0:T(8,128)(2,1)S(1)} collective-permute-done((bf16[1058,128]{1,0:T(8,128)(2,1)S(1)}, bf16[1058,128]{1,0:T(8,128)(2,1)S(1)}, u32[]{:S(2)}, u32[]{:S(2)}) %collective-permute-start.12) | collective-permute-done | bytes 270880 | tf_op jit(solution)/shard_map/ppermute | solution.py:202
  99.1 0.0 collective-permute-done.13.refs_13_
  99.1 5.6 %collective-permute-done.14.refs_14_ = bf16[1058,128]{1,0:T(8,128)(2,1)S(1)} collective-permute-done((bf16[1058,128]{1,0:T(8,128)(2,1)S(1)}, bf16[1058,128]{1,0:T(8,128)(2,1)S(1)}, u32[]{:S(2)}, u32[]{:S(2)}) %collective-permute-start.14) | collective-permute-done | bytes 270880 | tf_op jit(solution)/shard_map/ppermute | solution.py:202
  104.7 0.0 copy-done.1
  104.7 5.1 %lat_filter.1 = (f32[46,16,368]{2,1,0:T(8,128)S(1)}, bf16[46,16,368]{2,1,0:T(8,128)(2,1)S(1)}) custom-call(s32[34]{0:T(128)S(1)} %pad_add_fusion.meta, bf16[128,128]{1,0:T(8,128)(2,1)S(1)} %get-tuple-element.27.mixer, bf16[368,368]{1,0:T(8,128)(2,1)S(1)} %get-tuple-element.28.table, bf16[4,46,32,368]{3,2,1,0:T(8,128)(2,1)S(1)} %bitcast.8, ...), custom_call_target="tpu_custom_call" | custom-call | tf_op jit(solution)/shard_map/lat_filter/pallas_call | solution.py:224
  109.8 2.0 %collective-permute-start.15 = (bf16[46,16,368]{2,1,0:T(8,128)(2,1)S(1)}, bf16[46,16,368]{2,1,0:T(8,128)(2,1)S(1)}, u32[]{:S(2)}, u32[]{:S(2)}) collective-permute-start(bf16[46,16,368]{2,1,0:T(8,128)(2,1)S(1)} %get-tuple-element.44), channel_id=1, source_target_pairs={{0,16},{16,0},{1,17},{17,1},{2,18},{18,2},{3,19},{19,3},{4,20},{20... | collective-permute-start | bytes 1625096 | tf_op jit(solution)/shard_map/ppermute | solution.py:237
  111.8 1.6 %collective-permute-done.15 = bf16[46,16,368]{2,1,0:T(8,128)(2,1)S(1)} collective-permute-done((bf16[46,16,368]{2,1,0:T(8,128)(2,1)S(1)}, bf16[46,16,368]{2,1,0:T(8,128)(2,1)S(1)}, u32[]{:S(2)}, u32[]{:S(2)}) %collective-permute-start.15) | collective-permute-done | bytes 541728 | tf_op jit(solution)/shard_map/ppermute | solution.py:237
  113.4 1.2 %add_bitcast_fusion = f32[16,46,368]{2,0,1:T(8,128)} fusion(f32[46,16,368]{2,1,0:T(8,128)S(1)} %get-tuple-element.43, bf16[46,16,368]{2,1,0:T(8,128)(2,1)S(1)} %collective-permute-done.15), kind=kLoop, calls=%fused_computation | loop fusion | flops 541696 | bytes 2708480 | tf_op jit(solution)/shard_map/transpose | solution.py:242
Async XLA Ops:
  0.7 2.3 %copy-start = (bf16[4,32,23,736]{3,1,2,0:T(8,128)(2,1)S(1)}, bf16[4,32,23,736]{3,1,2,0:T(8,128)(2,1)}, u32[]{:S(2)}) copy-start(bf16[4,32,23,736]{3,1,2,0:T(8,128)(2,1)} %param.5) | copy-start | bytes 13000708
  5.3 12.8 %collective-permute-start.1 = (bf16[1058,128]{1,0:T(8,128)(2,1)S(1)}, bf16[1058,128]{1,0:T(8,128)(2,1)S(1)}, u32[]{:S(2)}, u32[]{:S(2)}) collective-permute-start(bf16[1058,128]{1,0:T(8,128)(2,1)S(1)} %get-tuple-element.29), channel_id=1, source_target_pairs={{0,4},{1,5},{2,6},{3,7},{4,0},{5,1},{6,2},{7,3},{8,12},{9,13},{10,... | collective-permute-start | bytes 812552 | tf_op jit(solution)/shard_map/ppermute | solution.py:202
  5.4 19.2 %collective-permute-start.2 = (bf16[1058,128]{1,0:T(8,128)(2,1)S(1)}, bf16[1058,128]{1,0:T(8,128)(2,1)S(1)}, u32[]{:S(2)}, u32[]{:S(2)}) collective-permute-start(bf16[1058,128]{1,0:T(8,128)(2,1)S(1)} %get-tuple-element.30), channel_id=1, source_target_pairs={{0,9},{1,8},{2,11},{3,10},{4,13},{5,12},{6,15},{7,14},{8,1},{9,0},... | collective-permute-start | bytes 812552 | tf_op jit(solution)/shard_map/ppermute | solution.py:202
  8.8 75.0 %copy-start.2 = (bf16[32,32]{1,0:T(8,128)(2,1)S(1)}, bf16[32,32]{1,0:T(8,128)(2,1)}, u32[]{:S(2)}) copy-start(bf16[32,32]{1,0:T(8,128)(2,1)} %vertical.1) | copy-start | bytes 6148
  8.8 27.5 %collective-permute-start = (bf16[1058,128]{1,0:T(8,128)(2,1)S(1)}, bf16[1058,128]{1,0:T(8,128)(2,1)S(1)}, u32[]{:S(2)}, u32[]{:S(2)}) collective-permute-start(bf16[1058,128]{1,0:T(8,128)(2,1)S(1)} %get-tuple-element.25.refs_0_), channel_id=1, source_target_pairs={{0,8},{1,9},{2,10},{3,11},{4,12},{5,13},{6,14},{7,15},{8,0},{9,1},... | collective-permute-start | bytes 812552 | tf_op jit(solution)/shard_map/ppermute | solution.py:202
  8.9 95.9 %copy-start.1 = (bf16[4,32,46,368]{3,1,2,0:T(8,128)(2,1)S(1)}, bf16[4,32,46,368]{3,1,2,0:T(8,128)(2,1)}, u32[]{:S(2)}) copy-start(bf16[4,32,46,368]{3,1,2,0:T(8,128)(2,1)} %param.6) | copy-start | bytes 13000708
  13.6 22.8 %collective-permute-start.3 = (bf16[1058,128]{1,0:T(8,128)(2,1)S(1)}, bf16[1058,128]{1,0:T(8,128)(2,1)S(1)}, u32[]{:S(2)}, u32[]{:S(2)}) collective-permute-start(bf16[1058,128]{1,0:T(8,128)(2,1)S(1)} %get-tuple-element.31), channel_id=1, source_target_pairs={{0,5},{1,4},{2,7},{3,6},{4,1},{5,0},{6,3},{7,2},{8,13},{9,12},{10,... | collective-permute-start | bytes 812552 | tf_op jit(solution)/shard_map/ppermute | solution.py:202
  14.9 28.6 %collective-permute-start.4 = (bf16[1058,128]{1,0:T(8,128)(2,1)S(1)}, bf16[1058,128]{1,0:T(8,128)(2,1)S(1)}, u32[]{:S(2)}, u32[]{:S(2)}) collective-permute-start(bf16[1058,128]{1,0:T(8,128)(2,1)S(1)} %get-tuple-element.32), channel_id=1, source_target_pairs={{0,10},{1,11},{2,8},{3,9},{4,14},{5,15},{6,12},{7,13},{8,2},{9,3},... | collective-permute-start | bytes 812552 | tf_op jit(solution)/shard_map/ppermute | solution.py:202
  18.2 25.9 %collective-permute-start.5 = (bf16[1058,128]{1,0:T(8,128)(2,1)S(1)}, bf16[1058,128]{1,0:T(8,128)(2,1)S(1)}, u32[]{:S(2)}, u32[]{:S(2)}) collective-permute-start(bf16[1058,128]{1,0:T(8,128)(2,1)S(1)} %get-tuple-element.33), channel_id=1, source_target_pairs={{0,6},{1,7},{2,4},{3,5},{4,2},{5,3},{6,0},{7,1},{8,14},{9,15},{10,... | collective-permute-start | bytes 812552 | tf_op jit(solution)/shard_map/ppermute | solution.py:202
  24.6 30.5 %collective-permute-start.6 = (bf16[1058,128]{1,0:T(8,128)(2,1)S(1)}, bf16[1058,128]{1,0:T(8,128)(2,1)S(1)}, u32[]{:S(2)}, u32[]{:S(2)}) collective-permute-start(bf16[1058,128]{1,0:T(8,128)(2,1)S(1)} %get-tuple-element.34), channel_id=1, source_target_pairs={{0,11},{1,10},{2,9},{3,8},{4,15},{5,14},{6,13},{7,12},{8,3},{9,2},... | collective-permute-start | bytes 812552 | tf_op jit(solution)/shard_map/ppermute | solution.py:202
  36.3 20.4 %collective-permute-start.7 = (bf16[1058,128]{1,0:T(8,128)(2,1)S(1)}, bf16[1058,128]{1,0:T(8,128)(2,1)S(1)}, u32[]{:S(2)}, u32[]{:S(2)}) collective-permute-start(bf16[1058,128]{1,0:T(8,128)(2,1)S(1)} %get-tuple-element.35), channel_id=1, source_target_pairs={{0,7},{1,6},{2,5},{3,4},{4,3},{5,2},{6,1},{7,0},{8,15},{9,14},{10,... | collective-permute-start | bytes 812552 | tf_op jit(solution)/shard_map/ppermute | solution.py:202
  36.3 44.2 %collective-permute-start.8 = (bf16[1058,128]{1,0:T(8,128)(2,1)S(1)}, bf16[1058,128]{1,0:T(8,128)(2,1)S(1)}, u32[]{:S(2)}, u32[]{:S(2)}) collective-permute-start(bf16[1058,128]{1,0:T(8,128)(2,1)S(1)} %get-tuple-element.36), channel_id=1, source_target_pairs={{0,12},{1,13},{2,14},{3,15},{4,8},{5,9},{6,10},{7,11},{8,4},{9,5},... | collective-permute-start | bytes 812552 | tf_op jit(solution)/shard_map/ppermute | solution.py:202
  43.5 37.5 %collective-permute-start.9 = (bf16[1058,128]{1,0:T(8,128)(2,1)S(1)}, bf16[1058,128]{1,0:T(8,128)(2,1)S(1)}, u32[]{:S(2)}, u32[]{:S(2)}) collective-permute-start(bf16[1058,128]{1,0:T(8,128)(2,1)S(1)} %get-tuple-element.37), channel_id=1, source_target_pairs={{0,1},{1,0},{2,3},{3,2},{4,5},{5,4},{6,7},{7,6},{8,9},{9,8},{10,11... | collective-permute-start | bytes 812552 | tf_op jit(solution)/shard_map/ppermute | solution.py:202
  44.0 44.1 %collective-permute-start.10 = (bf16[1058,128]{1,0:T(8,128)(2,1)S(1)}, bf16[1058,128]{1,0:T(8,128)(2,1)S(1)}, u32[]{:S(2)}, u32[]{:S(2)}) collective-permute-start(bf16[1058,128]{1,0:T(8,128)(2,1)S(1)} %get-tuple-element.38), channel_id=1, source_target_pairs={{0,13},{1,12},{2,15},{3,14},{4,9},{5,8},{6,11},{7,10},{8,5},{9,4},... | collective-permute-start | bytes 812552 | tf_op jit(solution)/shard_map/ppermute | solution.py:202
  55.1 33.0 %collective-permute-start.11 = (bf16[1058,128]{1,0:T(8,128)(2,1)S(1)}, bf16[1058,128]{1,0:T(8,128)(2,1)S(1)}, u32[]{:S(2)}, u32[]{:S(2)}) collective-permute-start(bf16[1058,128]{1,0:T(8,128)(2,1)S(1)} %get-tuple-element.39), channel_id=1, source_target_pairs={{0,2},{1,3},{2,0},{3,1},{4,6},{5,7},{6,4},{7,5},{8,10},{9,11},{10,... | collective-permute-start | bytes 812552 | tf_op jit(solution)/shard_map/ppermute | solution.py:202
  56.7 42.4 %collective-permute-start.12 = (bf16[1058,128]{1,0:T(8,128)(2,1)S(1)}, bf16[1058,128]{1,0:T(8,128)(2,1)S(1)}, u32[]{:S(2)}, u32[]{:S(2)}) collective-permute-start(bf16[1058,128]{1,0:T(8,128)(2,1)S(1)} %get-tuple-element.40), channel_id=1, source_target_pairs={{0,14},{1,15},{2,12},{3,13},{4,10},{5,11},{6,8},{7,9},{8,6},{9,7},... | collective-permute-start | bytes 812552 | tf_op jit(solution)/shard_map/ppermute | solution.py:202
  80.5 18.6 %collective-permute-start.13 = (bf16[1058,128]{1,0:T(8,128)(2,1)S(1)}, bf16[1058,128]{1,0:T(8,128)(2,1)S(1)}, u32[]{:S(2)}, u32[]{:S(2)}) collective-permute-start(bf16[1058,128]{1,0:T(8,128)(2,1)S(1)} %get-tuple-element.41), channel_id=1, source_target_pairs={{0,3},{1,2},{2,1},{3,0},{4,7},{5,6},{6,5},{7,4},{8,11},{9,10},{10,... | collective-permute-start | bytes 812552 | tf_op jit(solution)/shard_map/ppermute | solution.py:202
  81.0 23.7 %collective-permute-start.14 = (bf16[1058,128]{1,0:T(8,128)(2,1)S(1)}, bf16[1058,128]{1,0:T(8,128)(2,1)S(1)}, u32[]{:S(2)}, u32[]{:S(2)}) collective-permute-start(bf16[1058,128]{1,0:T(8,128)(2,1)S(1)} %get-tuple-element.42), channel_id=1, source_target_pairs={{0,15},{1,14},{2,13},{3,12},{4,11},{5,10},{6,9},{7,8},{8,7},{9,6},... | collective-permute-start | bytes 812552 | tf_op jit(solution)/shard_map/ppermute | solution.py:202
  109.8 3.6 %collective-permute-start.15 = (bf16[46,16,368]{2,1,0:T(8,128)(2,1)S(1)}, bf16[46,16,368]{2,1,0:T(8,128)(2,1)S(1)}, u32[]{:S(2)}, u32[]{:S(2)}) collective-permute-start(bf16[46,16,368]{2,1,0:T(8,128)(2,1)S(1)} %get-tuple-element.44), channel_id=1, source_target_pairs={{0,16},{16,0},{1,17},{17,1},{2,18},{18,2},{3,19},{19,3},{4,20},{20... | collective-permute-start | bytes 1625096 | tf_op jit(solution)/shard_map/ppermute | solution.py:237

commit v5 on v4

--- a/solution.py
+++ b/solution.py
@@ -16,9 +16,10 @@
 FAR = 1 << 20
 NORM = np.float32(math.sqrt(sum(math.exp(-2.0 * e / LENGTH) for e in range(BAND + 1))))
 MIB = 1024 * 1024
+FIRST_LIMIT = 60 * MIB
 LON_LIMIT = 24 * MIB
 LAT_LIMIT = 26 * MIB
-FIRST = 3
+FETCH = 12
 AHEAD = 2
 NT = (((1,), (1,)), ((), ()))
 NN = (((1,), (0,)), ((), ()))
@@ -46,41 +47,93 @@
     return jnp.where(inside, value, 0.0).astype(jnp.bfloat16)
 
 
-def lon_weights(groups, masks, meta, starts, table):
-    lon_pad = table.shape[1]
-    col_slots = lon_pad // groups
+def lon_weights(groups, masks, meta, me, starts, table, slots, col_slots):
     col_rows = table.shape[0] // len(masks)
     sums_before(meta, 0, starts, groups)
-    slots = lax.broadcasted_iota(jnp.int32, (1, lon_pad), 1)
     source = jnp.full_like(slots, FAR)
     for g in range(groups):
         source = jnp.minimum(source, place_of(meta, 0, starts, g, slots - g * col_slots, col_slots))
     own = lax.broadcasted_iota(jnp.int32, (col_rows, 1), 0)
     for n, mask in enumerate(masks):
-        slab = meta[2 * groups] ^ mask
+        slab = me ^ mask
         lag = own + starts[slab] - source
         lag = jnp.where(lag < 0, lag + LON, lag)
         table[n * col_rows:(n + 1) * col_rows, :] = weights(lag, own < meta[slab])
 
 
-def lon_kernel(groups, masks, meta, control, *refs):
-    outs, (table, packed, starts) = refs[-3 - len(masks):-3], refs[-3:]
-    members, row_slots, levels, lon_pad = control.shape
-    lanes = members * levels
-    col_slots = lon_pad // groups
+def lon_blocks(masks, row_range, col_slots, rows_of, table, packed, outs):
+    lanes = packed.shape[2]
     col_rows = table.shape[0] // len(masks)
-    lon_weights(groups, masks, meta, starts, table)
-    for i in range(0, row_slots, 2):
-        count = min(2, row_slots - i)
-        field = jnp.concatenate([control[:, i + r].reshape(lanes, lon_pad) for r in range(count)], axis=0)
+    for i in row_range[::2]:
+        count = min(2, row_range[-1] + 1 - i)
+        field = jnp.concatenate([rows_of(i + r).reshape(lanes, table.shape[1]) for r in range(count)], axis=0)
         smooth = lax.dot_general(table[...], field, NT, preferred_element_type=jnp.float32)
         for n in range(len(masks)):
             for r in range(count):
                 packed[n, (i + r) * col_slots:(i + r + 1) * col_slots, :] = smooth[
                     n * col_rows:n * col_rows + col_slots, r * lanes:(r + 1) * lanes
                 ]
-    for n in range(len(masks)):
-        outs[n][...] = packed[n].astype(jnp.bfloat16)
+    for n, out in enumerate(outs):
+        out[...] = packed[n].astype(jnp.bfloat16)
+
+
+def window_tiles(groups, lon_pad):
+    col_slots = lon_pad // groups
+    tiles = -(-lon_pad // 128)
+    reach = -(-(BAND + lon_pad - LON) // col_slots)
+    needed = (reach + 2) * col_slots + 127 + tiles * 128 - lon_pad
+    return reach, min(-(-needed // 128), tiles)
+
+
+def window_begin(groups, lon_pad, mask):
+    pair = (lax.axis_index("grid") ^ mask) // 2 * 2
+    reach, width = window_tiles(groups, lon_pad)
+    return lax.rem(pair - reach + groups, groups) * (lon_pad // groups) // 128
+
+
+def first_lon_kernel(groups, masks, row_slots, lon_pad, counts, *refs):
+    width = window_tiles(groups, lon_pad)[1]
+    window, outs, (table, packed, starts) = refs[:width], refs[width:-3], refs[-3:]
+    col_slots = lon_pad // groups
+    tiles = -(-lon_pad // 128)
+    begin = window_begin(groups, lon_pad, masks[0])
+    lane = lax.broadcasted_iota(jnp.int32, (1, 128), 1)
+    slots = [lane + lax.rem(begin + j, tiles) * 128 for j in range(width)]
+    step = pl.program_id(0)
+    size = window[0].shape[1]
+
+    @pl.when(step == 0)
+    def _():
+        lon_weights(
+            groups, masks, counts, lax.axis_index("grid"), starts, table, jnp.concatenate(slots, axis=1), col_slots
+        )
+
+    for n in range(-(-row_slots // size)):
+        @pl.when(step == n)
+        def _():
+            def rows_of(i):
+                return jnp.concatenate(
+                    [
+                        jnp.where(slots[j] < lon_pad, window[j][:, i - n * size].reshape(-1, 128), jnp.bfloat16(0))
+                        for j in range(width)
+                    ],
+                    axis=1,
+                )
+
+            last = n * size + size >= row_slots
+            lon_blocks(
+                masks, range(n * size, row_slots if last else n * size + size), col_slots, rows_of, table, packed,
+                outs if last else [],
+            )
+
+
+def lon_kernel(groups, masks, meta, control, *refs):
+    outs, (table, packed, starts) = refs[-3 - len(masks):-3], refs[-3:]
+    lon_pad = control.shape[3]
+    col_slots = lon_pad // groups
+    slots = lax.broadcasted_iota(jnp.int32, (1, lon_pad), 1)
+    lon_weights(groups, masks, meta, meta[2 * groups], starts, table, slots, col_slots)
+    lon_blocks(masks, range(control.shape[1]), col_slots, lambda i: control[:, i], table, packed, outs)
 
 
 def lat_weights(groups, row_slots, masks, meta, starts, table):
@@ -165,7 +218,8 @@
     order = []
     for n in range(2 * quarter):
         order += far[n:n + 1] + near[n:n + 1]
-    return order
+    order.remove(far[1])
+    return far[:1] + far[1:2] + order[1:]
 
 
 def per_device(control, perturbation, vertical, lat_counts, lon_counts):
@@ -183,28 +237,43 @@
 
     fields = jnp.transpose(control, (0, 2, 1, 3))
 
-    def lon_filter(masks, after):
+    def lon_filter(kernel, masks, columns, limit, grid, in_specs, *operands):
         return list(pl.pallas_call(
-            functools.partial(lon_kernel, groups, masks),
+            kernel,
             out_shape=[jax.ShapeDtypeStruct((row_slots * col_slots, lanes), jnp.bfloat16)] * len(masks),
-            in_specs=[smem, vmem] + [hbm] * len(after),
+            grid=grid,
+            in_specs=[smem, *in_specs],
             out_specs=[vmem] * len(masks),
             scratch_shapes=[
-                pltpu.VMEM((len(masks) * round_up(col_slots, 16), lon_pad), jnp.bfloat16),
+                pltpu.VMEM((len(masks) * round_up(col_slots, 16), columns), jnp.bfloat16),
                 pltpu.VMEM((len(masks), row_slots * col_slots, lanes), jnp.float32),
                 pltpu.SMEM((groups,), jnp.int32),
             ],
-            compiler_params=pltpu.CompilerParams(vmem_limit_bytes=LON_LIMIT),
+            compiler_params=pltpu.CompilerParams(vmem_limit_bytes=limit),
             name="lon_filter",
-        )(meta, fields, *after))
+        )(*operands))
 
     def send(mask, value):
         return lax.ppermute(value, "grid", [(g, g ^ mask) for g in range(groups)])
 
     order = sending_order(groups)
     masks = order + [0]
-    values = lon_filter(order[:FIRST], [])
-    values += lon_filter(masks[FIRST:], values[:1])
+    width = window_tiles(groups, lon_pad)[1]
+    tiles = -(-lon_pad // 128)
+    rows = min(FETCH, row_slots)
+    windows = [
+        pl.BlockSpec(
+            (members, rows, levels, 128),
+            lambda n, j=j: (0, n, 0, lax.rem(window_begin(groups, lon_pad, masks[0]) + j, tiles)),
+        )
+        for j in range(width)
+    ]
+    kernel = functools.partial(first_lon_kernel, groups, masks[:2], row_slots, lon_pad)
+    values = lon_filter(
+        kernel, masks[:2], width * 128, FIRST_LIMIT, (-(-row_slots // rows),), windows, lon_counts, *[fields] * width
+    )
+    kernel = functools.partial(lon_kernel, groups, masks[2:])
+    values += lon_filter(kernel, masks[2:], lon_pad, LON_LIMIT, (), [vmem, hbm], meta, fields, values[0])
     received = [send(mask, value) if mask else value for mask, value in zip(masks, values)]
 
     mixer, table = pl.pallas_call(

time: 115 us -> 112 us (0.974)
  waiting for transfers between devices: 73.4 us -> 51.9 us
  starting transfers between devices: 23.3 us -> 39.9 us
  Pallas kernels: 13.6 us -> 15 us
    ppermute x15, waiting for transfers between devices: 71.8 us -> 50.3 us  [send(): return lax.ppermute(value, 'grid', [(g, g ^ mask) for g in range(groups)])]
    ppermute x15, starting transfers between devices: 21.3 us -> 38.4 us  [send(): return lax.ppermute(value, 'grid', [(g, g ^ mask) for g in range(groups)])]
    pallas_call x2, Pallas kernels: 6.99 us -> 8.38 us  [lon_filter(): pl.pallas_call(kernel, out_shape=[jax.ShapeDtypeStruct((row_slots * col_s...]
    unnamed x6 -> x12, local copies, waits for them, and re-layouts: 2.29 us -> 3.25 us
  transfers between devices with their start and end apart: 16 -> 16, of which waited for: 11 -> 9; matrix products, arithmetic and copies ran while one was open for 0% -> 0% of each run, Pallas kernels for 5% -> 6%
where the time goes in v5:
time: 112 us; the launch traced here: 111 us
  waiting for transfers between devices  51.9 us (46%)
  starting transfers between devices  39.9 us (36%)
  Pallas kernels  15 us (13%)
  local copies, waits for them, and re-layouts  3.25 us (3%)
  other arithmetic  1.25 us (1%)
    ppermute x15, waiting for transfers between devices, send(): return lax.ppermute(value, 'grid', [(g, g ^ mask) for g in range(groups)])  50.3 us
    ppermute x15, starting transfers between devices, send(): return lax.ppermute(value, 'grid', [(g, g ^ mask) for g in range(groups)])  38.4 us
    pallas_call x2, Pallas kernels, lon_filter(): pl.pallas_call(kernel, out_shape=[jax.ShapeDtypeStruct((row_slots * col_s...  8.38 us
    pallas_call x1, Pallas kernels, per_device(): pl.pallas_call(functools.partial(lat_kernel, groups), out_shape=[jax.Shap...  5.09 us
    unnamed x12, local copies, waits for them, and re-layouts  3.25 us
  transfers between devices with their start and end apart: 16, of which 9 were waited for; matrix products, arithmetic and copies ran while one was open for 0% of the time, Pallas kernels for 6%

profile of v5, /device:TPU:9, one launch (start us, length us, event | category | flops | bytes accessed | tf_op | source)
XLA Modules:
  0.0 111.3 jit_solution(16619415029376334479)
XLA Ops:
  0.0 0.0 copy-start.4
  0.0 0.0 copy-start.5
  0.0 3.4 %lon_filter.2 = (bf16[1058,128]{1,0:T(8,128)(2,1)}, bf16[1058,128]{1,0:T(8,128)(2,1)}) custom-call(s32[16]{0:T(128)} %counts.1, bf16[4,23,32,736]{3,2,1,0:T(8,128)(2,1)} %bitcast.6, bf16[4,23,32,736]{3,2,1,0:T(8,128)(2,1)} %bitcast.7, bf16[4,23,32,736]{3,2,1,0:T(8,128)(2,1)} %bitcast.8), custom_call_target="tpu_custom_call" | custom-call | tf_op jit(solution)/shard_map/lon_filter/pallas_call | solution.py:241
  3.4 3.2 %collective-permute-start.1 = (bf16[1058,128]{1,0:T(8,128)(2,1)}, bf16[1058,128]{1,0:T(8,128)(2,1)S(1)}, u32[]{:S(2)}, u32[]{:S(2)}) collective-permute-start(bf16[1058,128]{1,0:T(8,128)(2,1)} %get-tuple-element.29), channel_id=1, source_target_pairs={{0,9},{1,8},{2,11},{3,10},{4,13},{5,12},{6,15},{7,14},{8,1},{9,0},... | collective-permute-start | bytes 812552 | tf_op jit(solution)/shard_map/ppermute | solution.py:257
  6.6 0.1 collective-permute-start
  6.7 0.0 copy-done.4
  6.7 0.0 copy-done.5
  6.7 0.1 pad_add_fusion.meta
  6.8 0.0 copy-start
  6.8 2.3 %copy-done = bf16[4,32,23,736]{3,1,2,0:T(8,128)(2,1)S(1)} copy-done((bf16[4,32,23,736]{3,1,2,0:T(8,128)(2,1)S(1)}, bf16[4,32,23,736]{3,1,2,0:T(8,128)(2,1)}, u32[]{:S(2)}) %copy-start) | copy-done | bytes 4333592
  9.1 0.0 copy-start.2
  9.1 1.0 copy-done.2
  10.0 5.0 %lon_filter.3 = (bf16[1058,128]{1,0:T(8,128)(2,1)S(1)}, bf16[1058,128]{1,0:T(8,128)(2,1)S(1)}, bf16[1058,128]{1,0:T(8,128)(2,1)S(1)}, bf16[1058,128]{1,0:T(8,128...) custom-call(s32[34]{0:T(128)S(1)} %pad_add_fusion.meta, ...), custom_call_target="tpu_custom_call" | custom-call | tf_op jit(solution)/shard_map/lon_filter/pallas_call | solution.py:241
  15.0 0.2 collective-permute-start.2
  15.2 1.3 %collective-permute-start.3 = (bf16[1058,128]{1,0:T(8,128)(2,1)S(1)}, bf16[1058,128]{1,0:T(8,128)(2,1)S(1)}, u32[]{:S(2)}, u32[]{:S(2)}) collective-permute-start(bf16[1058,128]{1,0:T(8,128)(2,1)S(1)} %get-tuple-element.31), channel_id=1, source_target_pairs={{0,5},{1,4},{2,7},{3,6},{4,1},{5,0},{6,3},{7,2},{8,13},{9,12},{10,... | collective-permute-start | bytes 812552 | tf_op jit(solution)/shard_map/ppermute | solution.py:257
  16.5 3.3 %collective-permute-start.4 = (bf16[1058,128]{1,0:T(8,128)(2,1)S(1)}, bf16[1058,128]{1,0:T(8,128)(2,1)S(1)}, u32[]{:S(2)}, u32[]{:S(2)}) collective-permute-start(bf16[1058,128]{1,0:T(8,128)(2,1)S(1)} %get-tuple-element.32), channel_id=1, source_target_pairs={{0,10},{1,11},{2,8},{3,9},{4,14},{5,15},{6,12},{7,13},{8,2},{9,3},... | collective-permute-start | bytes 812552 | tf_op jit(solution)/shard_map/ppermute | solution.py:257
  19.8 5.0 %collective-permute-done.1.refs_1_ = bf16[1058,128]{1,0:T(8,128)(2,1)S(1)} collective-permute-done((bf16[1058,128]{1,0:T(8,128)(2,1)}, bf16[1058,128]{1,0:T(8,128)(2,1)S(1)}, u32[]{:S(2)}, u32[]{:S(2)}) %collective-permute-start.1) | collective-permute-done | bytes 270880 | tf_op jit(solution)/shard_map/ppermute | solution.py:257
  24.8 0.9 collective-permute-start.5
  25.7 5.5 %collective-permute-done.refs_0_ = bf16[1058,128]{1,0:T(8,128)(2,1)S(1)} collective-permute-done((bf16[1058,128]{1,0:T(8,128)(2,1)}, bf16[1058,128]{1,0:T(8,128)(2,1)S(1)}, u32[]{:S(2)}, u32[]{:S(2)}) %collective-permute-start) | collective-permute-done | bytes 270880 | tf_op jit(solution)/shard_map/ppermute | solution.py:257
  31.2 4.4 %collective-permute-start.6 = (bf16[1058,128]{1,0:T(8,128)(2,1)S(1)}, bf16[1058,128]{1,0:T(8,128)(2,1)S(1)}, u32[]{:S(2)}, u32[]{:S(2)}) collective-permute-start(bf16[1058,128]{1,0:T(8,128)(2,1)S(1)} %get-tuple-element.34), channel_id=1, source_target_pairs={{0,11},{1,10},{2,9},{3,8},{4,15},{5,14},{6,13},{7,12},{8,3},{9,2},... | collective-permute-start | bytes 812552 | tf_op jit(solution)/shard_map/ppermute | solution.py:257
  35.6 0.0 collective-permute-done.2.refs_2_
  35.6 0.0 collective-permute-start.7
  35.6 7.8 %collective-permute-done.3.refs_3_ = bf16[1058,128]{1,0:T(8,128)(2,1)S(1)} collective-permute-done((bf16[1058,128]{1,0:T(8,128)(2,1)S(1)}, bf16[1058,128]{1,0:T(8,128)(2,1)S(1)}, u32[]{:S(2)}, u32[]{:S(2)}) %collective-permute-start.3) | collective-permute-done | bytes 270880 | tf_op jit(solution)/shard_map/ppermute | solution.py:257
  43.4 2.6 %collective-permute-start.8 = (bf16[1058,128]{1,0:T(8,128)(2,1)S(1)}, bf16[1058,128]{1,0:T(8,128)(2,1)S(1)}, u32[]{:S(2)}, u32[]{:S(2)}) collective-permute-start(bf16[1058,128]{1,0:T(8,128)(2,1)S(1)} %get-tuple-element.36), channel_id=1, source_target_pairs={{0,12},{1,13},{2,14},{3,15},{4,8},{5,9},{6,10},{7,11},{8,4},{9,5},... | collective-permute-start | bytes 812552 | tf_op jit(solution)/shard_map/ppermute | solution.py:257
  46.0 0.0 collective-permute-done.4.refs_4_
  46.0 0.3 collective-permute-start.9
  46.2 6.7 %collective-permute-done.5.refs_5_ = bf16[1058,128]{1,0:T(8,128)(2,1)S(1)} collective-permute-done((bf16[1058,128]{1,0:T(8,128)(2,1)S(1)}, bf16[1058,128]{1,0:T(8,128)(2,1)S(1)}, u32[]{:S(2)}, u32[]{:S(2)}) %collective-permute-start.5) | collective-permute-done | bytes 270880 | tf_op jit(solution)/shard_map/ppermute | solution.py:257
  52.9 10.4 %collective-permute-start.10 = (bf16[1058,128]{1,0:T(8,128)(2,1)S(1)}, bf16[1058,128]{1,0:T(8,128)(2,1)S(1)}, u32[]{:S(2)}, u32[]{:S(2)}) collective-permute-start(bf16[1058,128]{1,0:T(8,128)(2,1)S(1)} %get-tuple-element.38), channel_id=1, source_target_pairs={{0,13},{1,12},{2,15},{3,14},{4,9},{5,8},{6,11},{7,10},{8,5},{9,4},... | collective-permute-start | bytes 812552 | tf_op jit(solution)/shard_map/ppermute | solution.py:257
  63.4 0.0 collective-permute-done.6.refs_6_
  63.4 1.2 %collective-permute-start.11 = (bf16[1058,128]{1,0:T(8,128)(2,1)S(1)}, bf16[1058,128]{1,0:T(8,128)(2,1)S(1)}, u32[]{:S(2)}, u32[]{:S(2)}) collective-permute-start(bf16[1058,128]{1,0:T(8,128)(2,1)S(1)} %get-tuple-element.39), channel_id=1, source_target_pairs={{0,2},{1,3},{2,0},{3,1},{4,6},{5,7},{6,4},{7,5},{8,10},{9,11},{10,... | collective-permute-start | bytes 812552 | tf_op jit(solution)/shard_map/ppermute | solution.py:257
  64.6 0.8 collective-permute-done.7.refs_7_
  65.4 10.5 %collective-permute-start.12 = (bf16[1058,128]{1,0:T(8,128)(2,1)S(1)}, bf16[1058,128]{1,0:T(8,128)(2,1)S(1)}, u32[]{:S(2)}, u32[]{:S(2)}) collective-permute-start(bf16[1058,128]{1,0:T(8,128)(2,1)S(1)} %get-tuple-element.40), channel_id=1, source_target_pairs={{0,14},{1,15},{2,12},{3,13},{4,10},{5,11},{6,8},{7,9},{8,6},{9,7},... | collective-permute-start | bytes 812552 | tf_op jit(solution)/shard_map/ppermute | solution.py:257
  75.9 0.0 collective-permute-done.8.refs_8_
  75.9 0.0 collective-permute-start.13
  75.9 0.0 collective-permute-done.9.refs_9_
  75.9 0.1 collective-permute-start.14
  76.0 0.0 copy-done.3
  76.0 1.5 %matrices.1 = (bf16[128,128]{1,0:T(8,128)(2,1)S(1)}, bf16[368,368]{1,0:T(8,128)(2,1)S(1)}) custom-call(s32[34]{0:T(128)S(1)} %pad_add_fusion.meta, bf16[32,32]{1,0:T(8,128)(2,1)S(1)} %copy-done.3, bf16[1058,128]{1,0:T(8,128)(2,1)S(1)} %get-tuple-element.26.after.refs_15_), custom_call_target="tpu_custom_call" | custom-call | tf_op jit(solution)/shard_map/matrices/pallas_call | solution.py:279
  77.5 1.0 collective-permute-done.10.refs_10_
  78.6 0.0 collective-permute-done.11.refs_11_
  78.6 15.3 %collective-permute-done.12.refs_12_ = bf16[1058,128]{1,0:T(8,128)(2,1)S(1)} collective-permute-done((bf16[1058,128]{1,0:T(8,128)(2,1)S(1)}, bf16[1058,128]{1,0:T(8,128)(2,1)S(1)}, u32[]{:S(2)}, u32[]{:S(2)}) %collective-permute-start.12) | collective-permute-done | bytes 270880 | tf_op jit(solution)/shard_map/ppermute | solution.py:257
  93.9 0.0 collective-permute-done.13.refs_13_
  93.9 8.1 %collective-permute-done.14.refs_14_ = bf16[1058,128]{1,0:T(8,128)(2,1)S(1)} collective-permute-done((bf16[1058,128]{1,0:T(8,128)(2,1)S(1)}, bf16[1058,128]{1,0:T(8,128)(2,1)S(1)}, u32[]{:S(2)}, u32[]{:S(2)}) %collective-permute-start.14) | collective-permute-done | bytes 270880 | tf_op jit(solution)/shard_map/ppermute | solution.py:257
  102.0 0.0 copy-done.1
  102.0 5.1 %lat_filter.1 = (f32[46,16,368]{2,1,0:T(8,128)S(1)}, bf16[46,16,368]{2,1,0:T(8,128)(2,1)S(1)}) custom-call(s32[34]{0:T(128)S(1)} %pad_add_fusion.meta, bf16[128,128]{1,0:T(8,128)(2,1)S(1)} %get-tuple-element.27.mixer, bf16[368,368]{1,0:T(8,128)(2,1)S(1)} %get-tuple-element.28.table, bf16[4,46,32,368]{3,2,1,0:T(8,128)(2,1)S(1)} %bitcast.10, ...), custom_call_target="tpu_custom_call" | custom-call | tf_op jit(solution)/shard_map/lat_filter/pallas_call | solution.py:293
  107.1 1.5 %collective-permute-start.15 = (bf16[46,16,368]{2,1,0:T(8,128)(2,1)S(1)}, bf16[46,16,368]{2,1,0:T(8,128)(2,1)S(1)}, u32[]{:S(2)}, u32[]{:S(2)}) collective-permute-start(bf16[46,16,368]{2,1,0:T(8,128)(2,1)S(1)} %get-tuple-element.44), channel_id=1, source_target_pairs={{0,16},{16,0},{1,17},{17,1},{2,18},{18,2},{3,19},{19,3},{4,20},{20... | collective-permute-start | bytes 1625096 | tf_op jit(solution)/shard_map/ppermute | solution.py:306
  108.6 1.6 %collective-permute-done.15 = bf16[46,16,368]{2,1,0:T(8,128)(2,1)S(1)} collective-permute-done((bf16[46,16,368]{2,1,0:T(8,128)(2,1)S(1)}, bf16[46,16,368]{2,1,0:T(8,128)(2,1)S(1)}, u32[]{:S(2)}, u32[]{:S(2)}) %collective-permute-start.15) | collective-permute-done | bytes 541728 | tf_op jit(solution)/shard_map/ppermute | solution.py:306
  110.2 1.2 %add_bitcast_fusion = f32[16,46,368]{2,0,1:T(8,128)} fusion(f32[46,16,368]{2,1,0:T(8,128)S(1)} %get-tuple-element.43, bf16[46,16,368]{2,1,0:T(8,128)(2,1)S(1)} %collective-permute-done.15), kind=kLoop, calls=%fused_computation | loop fusion | flops 541696 | bytes 2708480 | tf_op jit(solution)/shard_map/transpose | solution.py:311
  (2 shorter events, 0.0 us)
Async XLA Ops:
  0.0 6.7 %copy-start.4 = (s32[16]{0:T(128)S(1)}, s32[16]{0:T(128)}, u32[]{:S(2)}) copy-start(s32[16]{0:T(128)} %counts.1) | copy-start | bytes 196
  0.0 6.7 %copy-start.5 = (s32[16]{0:T(128)S(1)}, s32[16]{0:T(128)}, u32[]{:S(2)}) copy-start(s32[16]{0:T(128)} %param.8) | copy-start | bytes 196
  3.4 21.4 %collective-permute-start.1 = (bf16[1058,128]{1,0:T(8,128)(2,1)}, bf16[1058,128]{1,0:T(8,128)(2,1)S(1)}, u32[]{:S(2)}, u32[]{:S(2)}) collective-permute-start(bf16[1058,128]{1,0:T(8,128)(2,1)} %get-tuple-element.29), channel_id=1, source_target_pairs={{0,9},{1,8},{2,11},{3,10},{4,13},{5,12},{6,15},{7,14},{8,1},{9,0},... | collective-permute-start | bytes 812552 | tf_op jit(solution)/shard_map/ppermute | solution.py:257
  6.6 24.6 %collective-permute-start = (bf16[1058,128]{1,0:T(8,128)(2,1)}, bf16[1058,128]{1,0:T(8,128)(2,1)S(1)}, u32[]{:S(2)}, u32[]{:S(2)}) collective-permute-start(bf16[1058,128]{1,0:T(8,128)(2,1)} %get-tuple-element.25.refs_0_), channel_id=1, source_target_pairs={{0,8},{1,9},{2,10},{3,11},{4,12},{5,13},{6,14},{7,15},{8,0},{9,1},... | collective-permute-start | bytes 812552 | tf_op jit(solution)/shard_map/ppermute | solution.py:257
  6.8 2.3 %copy-start = (bf16[4,32,23,736]{3,1,2,0:T(8,128)(2,1)S(1)}, bf16[4,32,23,736]{3,1,2,0:T(8,128)(2,1)}, u32[]{:S(2)}) copy-start(bf16[4,32,23,736]{3,1,2,0:T(8,128)(2,1)} %param.5) | copy-start | bytes 13000708
  9.1 1.0 copy-start.2
  10.0 65.9 %copy-start.3 = (bf16[32,32]{1,0:T(8,128)(2,1)S(1)}, bf16[32,32]{1,0:T(8,128)(2,1)}, u32[]{:S(2)}) copy-start(bf16[32,32]{1,0:T(8,128)(2,1)} %vertical.1) | copy-start | bytes 6148
  10.0 92.0 %copy-start.1 = (bf16[4,32,46,368]{3,1,2,0:T(8,128)(2,1)S(1)}, bf16[4,32,46,368]{3,1,2,0:T(8,128)(2,1)}, u32[]{:S(2)}) copy-start(bf16[4,32,46,368]{3,1,2,0:T(8,128)(2,1)} %param.6) | copy-start | bytes 13000708
  15.0 20.6 %collective-permute-start.2 = (bf16[1058,128]{1,0:T(8,128)(2,1)S(1)}, bf16[1058,128]{1,0:T(8,128)(2,1)S(1)}, u32[]{:S(2)}, u32[]{:S(2)}) collective-permute-start(bf16[1058,128]{1,0:T(8,128)(2,1)S(1)} %get-tuple-element.30), channel_id=1, source_target_pairs={{0,4},{1,5},{2,6},{3,7},{4,0},{5,1},{6,2},{7,3},{8,12},{9,13},{10,... | collective-permute-start | bytes 812552 | tf_op jit(solution)/shard_map/ppermute | solution.py:257
  15.2 28.2 %collective-permute-start.3 = (bf16[1058,128]{1,0:T(8,128)(2,1)S(1)}, bf16[1058,128]{1,0:T(8,128)(2,1)S(1)}, u32[]{:S(2)}, u32[]{:S(2)}) collective-permute-start(bf16[1058,128]{1,0:T(8,128)(2,1)S(1)} %get-tuple-element.31), channel_id=1, source_target_pairs={{0,5},{1,4},{2,7},{3,6},{4,1},{5,0},{6,3},{7,2},{8,13},{9,12},{10,... | collective-permute-start | bytes 812552 | tf_op jit(solution)/shard_map/ppermute | solution.py:257
  16.5 29.5 %collective-permute-start.4 = (bf16[1058,128]{1,0:T(8,128)(2,1)S(1)}, bf16[1058,128]{1,0:T(8,128)(2,1)S(1)}, u32[]{:S(2)}, u32[]{:S(2)}) collective-permute-start(bf16[1058,128]{1,0:T(8,128)(2,1)S(1)} %get-tuple-element.32), channel_id=1, source_target_pairs={{0,10},{1,11},{2,8},{3,9},{4,14},{5,15},{6,12},{7,13},{8,2},{9,3},... | collective-permute-start | bytes 812552 | tf_op jit(solution)/shard_map/ppermute | solution.py:257
  24.8 28.1 %collective-permute-start.5 = (bf16[1058,128]{1,0:T(8,128)(2,1)S(1)}, bf16[1058,128]{1,0:T(8,128)(2,1)S(1)}, u32[]{:S(2)}, u32[]{:S(2)}) collective-permute-start(bf16[1058,128]{1,0:T(8,128)(2,1)S(1)} %get-tuple-element.33), channel_id=1, source_target_pairs={{0,6},{1,7},{2,4},{3,5},{4,2},{5,3},{6,0},{7,1},{8,14},{9,15},{10,... | collective-permute-start | bytes 812552 | tf_op jit(solution)/shard_map/ppermute | solution.py:257
  31.2 32.2 %collective-permute-start.6 = (bf16[1058,128]{1,0:T(8,128)(2,1)S(1)}, bf16[1058,128]{1,0:T(8,128)(2,1)S(1)}, u32[]{:S(2)}, u32[]{:S(2)}) collective-permute-start(bf16[1058,128]{1,0:T(8,128)(2,1)S(1)} %get-tuple-element.34), channel_id=1, source_target_pairs={{0,11},{1,10},{2,9},{3,8},{4,15},{5,14},{6,13},{7,12},{8,3},{9,2},... | collective-permute-start | bytes 812552 | tf_op jit(solution)/shard_map/ppermute | solution.py:257
  35.6 29.8 %collective-permute-start.7 = (bf16[1058,128]{1,0:T(8,128)(2,1)S(1)}, bf16[1058,128]{1,0:T(8,128)(2,1)S(1)}, u32[]{:S(2)}, u32[]{:S(2)}) collective-permute-start(bf16[1058,128]{1,0:T(8,128)(2,1)S(1)} %get-tuple-element.35), channel_id=1, source_target_pairs={{0,7},{1,6},{2,5},{3,4},{4,3},{5,2},{6,1},{7,0},{8,15},{9,14},{10,... | collective-permute-start | bytes 812552 | tf_op jit(solution)/shard_map/ppermute | solution.py:257
  43.4 32.5 %collective-permute-start.8 = (bf16[1058,128]{1,0:T(8,128)(2,1)S(1)}, bf16[1058,128]{1,0:T(8,128)(2,1)S(1)}, u32[]{:S(2)}, u32[]{:S(2)}) collective-permute-start(bf16[1058,128]{1,0:T(8,128)(2,1)S(1)} %get-tuple-element.36), channel_id=1, source_target_pairs={{0,12},{1,13},{2,14},{3,15},{4,8},{5,9},{6,10},{7,11},{8,4},{9,5},... | collective-permute-start | bytes 812552 | tf_op jit(solution)/shard_map/ppermute | solution.py:257
  46.0 29.9 %collective-permute-start.9 = (bf16[1058,128]{1,0:T(8,128)(2,1)S(1)}, bf16[1058,128]{1,0:T(8,128)(2,1)S(1)}, u32[]{:S(2)}, u32[]{:S(2)}) collective-permute-start(bf16[1058,128]{1,0:T(8,128)(2,1)S(1)} %get-tuple-element.37), channel_id=1, source_target_pairs={{0,1},{1,0},{2,3},{3,2},{4,5},{5,4},{6,7},{7,6},{8,9},{9,8},{10,11... | collective-permute-start | bytes 812552 | tf_op jit(solution)/shard_map/ppermute | solution.py:257
  52.9 25.6 %collective-permute-start.10 = (bf16[1058,128]{1,0:T(8,128)(2,1)S(1)}, bf16[1058,128]{1,0:T(8,128)(2,1)S(1)}, u32[]{:S(2)}, u32[]{:S(2)}) collective-permute-start(bf16[1058,128]{1,0:T(8,128)(2,1)S(1)} %get-tuple-element.38), channel_id=1, source_target_pairs={{0,13},{1,12},{2,15},{3,14},{4,9},{5,8},{6,11},{7,10},{8,5},{9,4},... | collective-permute-start | bytes 812552 | tf_op jit(solution)/shard_map/ppermute | solution.py:257
  63.4 15.2 %collective-permute-start.11 = (bf16[1058,128]{1,0:T(8,128)(2,1)S(1)}, bf16[1058,128]{1,0:T(8,128)(2,1)S(1)}, u32[]{:S(2)}, u32[]{:S(2)}) collective-permute-start(bf16[1058,128]{1,0:T(8,128)(2,1)S(1)} %get-tuple-element.39), channel_id=1, source_target_pairs={{0,2},{1,3},{2,0},{3,1},{4,6},{5,7},{6,4},{7,5},{8,10},{9,11},{10,... | collective-permute-start | bytes 812552 | tf_op jit(solution)/shard_map/ppermute | solution.py:257
  65.4 28.5 %collective-permute-start.12 = (bf16[1058,128]{1,0:T(8,128)(2,1)S(1)}, bf16[1058,128]{1,0:T(8,128)(2,1)S(1)}, u32[]{:S(2)}, u32[]{:S(2)}) collective-permute-start(bf16[1058,128]{1,0:T(8,128)(2,1)S(1)} %get-tuple-element.40), channel_id=1, source_target_pairs={{0,14},{1,15},{2,12},{3,13},{4,10},{5,11},{6,8},{7,9},{8,6},{9,7},... | collective-permute-start | bytes 812552 | tf_op jit(solution)/shard_map/ppermute | solution.py:257
  75.9 18.0 %collective-permute-start.13 = (bf16[1058,128]{1,0:T(8,128)(2,1)S(1)}, bf16[1058,128]{1,0:T(8,128)(2,1)S(1)}, u32[]{:S(2)}, u32[]{:S(2)}) collective-permute-start(bf16[1058,128]{1,0:T(8,128)(2,1)S(1)} %get-tuple-element.41), channel_id=1, source_target_pairs={{0,3},{1,2},{2,1},{3,0},{4,7},{5,6},{6,5},{7,4},{8,11},{9,10},{10,... | collective-permute-start | bytes 812552 | tf_op jit(solution)/shard_map/ppermute | solution.py:257
  75.9 26.1 %collective-permute-start.14 = (bf16[1058,128]{1,0:T(8,128)(2,1)S(1)}, bf16[1058,128]{1,0:T(8,128)(2,1)S(1)}, u32[]{:S(2)}, u32[]{:S(2)}) collective-permute-start(bf16[1058,128]{1,0:T(8,128)(2,1)S(1)} %get-tuple-element.42), channel_id=1, source_target_pairs={{0,15},{1,14},{2,13},{3,12},{4,11},{5,10},{6,9},{7,8},{8,7},{9,6},... | collective-permute-start | bytes 812552 | tf_op jit(solution)/shard_map/ppermute | solution.py:257
  107.1 3.1 %collective-permute-start.15 = (bf16[46,16,368]{2,1,0:T(8,128)(2,1)S(1)}, bf16[46,16,368]{2,1,0:T(8,128)(2,1)S(1)}, u32[]{:S(2)}, u32[]{:S(2)}) collective-permute-start(bf16[46,16,368]{2,1,0:T(8,128)(2,1)S(1)} %get-tuple-element.44), channel_id=1, source_target_pairs={{0,16},{16,0},{1,17},{17,1},{2,18},{18,2},{3,19},{19,3},{4,20},{20... | collective-permute-start | bytes 1625096 | tf_op jit(solution)/shard_map/ppermute | solution.py:306

commit v6 on v5

--- a/solution.py
+++ b/solution.py
@@ -20,7 +20,7 @@
 LON_LIMIT = 24 * MIB
 LAT_LIMIT = 26 * MIB
 FETCH = 12
-AHEAD = 2
+AHEAD = 3
 NT = (((1,), (1,)), ((), ()))
 NN = (((1,), (0,)), ((), ()))
 
@@ -136,36 +136,43 @@
     lon_blocks(masks, range(control.shape[1]), col_slots, lambda i: control[:, i], table, packed, outs)
 
 
-def lat_weights(groups, row_slots, masks, meta, starts, table):
-    lat_pad = table.shape[0]
+def lat_reach(groups, row_slots):
+    return -(-(BAND + groups * row_slots - LAT) // row_slots)
+
+
+def lat_weights(groups, row_slots, meta, starts, table, first_down, first_across):
     sums_before(meta, groups, starts, groups)
-    down_slots = lax.broadcasted_iota(jnp.int32, (lat_pad, 1), 0)
-    across_slots = lax.broadcasted_iota(jnp.int32, (1, lat_pad), 1)
+    down_slots = lax.broadcasted_iota(jnp.int32, (table.shape[0], 1), 0) + first_down
+    across_slots = lax.broadcasted_iota(jnp.int32, (1, table.shape[1]), 1) + first_across
     down, across = jnp.full_like(down_slots, FAR), jnp.full_like(across_slots, FAR)
     for g in range(groups):
         down = jnp.minimum(down, place_of(meta, groups, starts, g, down_slots - g * row_slots, row_slots))
-        across = jnp.minimum(
-            across, place_of(meta, groups, starts, meta[2 * groups] ^ masks[g], across_slots - g * row_slots, row_slots)
-        )
+        across = jnp.minimum(across, place_of(meta, groups, starts, g, across_slots - g * row_slots, row_slots))
     table[...] = weights(down - across, down < FAR)
 
 
-def lat_columns(second, mixer, pert, table, field, kept, given):
+def lat_columns(second, mixer, pert, upper, lower, field, kept, given):
     columns, half = kept.shape[:2]
     members, _, levels, lat_pad = pert.shape
     lanes = members * levels
 
     def filtered(c):
-        part = jnp.concatenate(
-            [field[pl.ds(c + r, lat_pad, columns), :].astype(jnp.bfloat16) for r in range(2)], axis=1
-        )
-        return lax.dot_general(table[...], part, NN, preferred_element_type=jnp.float32).astype(jnp.bfloat16)
+        halves = []
+        for table, first in ((upper, 0), (lower, lat_pad - lower.shape[1])):
+            part = jnp.concatenate(
+                [
+                    field[pl.ds(first * columns + c + r, table.shape[1], columns), :].astype(jnp.bfloat16)
+                    for r in range(2)
+                ],
+                axis=1,
+            )
+            halves.append(lax.dot_general(table[...], part, NN, preferred_element_type=jnp.float32))
+        return jnp.concatenate(halves, axis=0).astype(jnp.bfloat16)
 
     def finish(c, smooth):
+        pair = lax.dot_general(mixer[...], smooth, NT, preferred_element_type=jnp.float32)
         for r in range(2):
-            mixed = lax.dot_general(
-                mixer[...], smooth[:, r * lanes:(r + 1) * lanes], NT, preferred_element_type=jnp.float32
-            )
+            mixed = pair[r * lanes:(r + 1) * lanes]
             total = mixed[:levels] * pert[0, c + r].astype(jnp.float32)
             for m in range(1, members):
                 total = total + mixed[m * levels:(m + 1) * levels] * pert[m, c + r].astype(jnp.float32)
@@ -198,17 +205,20 @@
     return jnp.where(same, wide, 0.0).astype(jnp.bfloat16)
 
 
-def matrices_kernel(groups, row_slots, masks, meta, vertical, after, mixer, table, starts):
+def matrices_kernel(groups, row_slots, meta, vertical, after, mixer, upper, lower, starts):
     mixer[...] = block_diagonal(vertical[...], mixer.shape[0] // vertical.shape[0])
-    lat_weights(groups, row_slots, masks, meta, starts, table)
-
-
-def lat_kernel(groups, meta, mixer, table, pert, *refs):
+    half, lat_pad = upper.shape[0], groups * row_slots
+    lat_weights(groups, row_slots, meta, starts, upper, 0, 0)
+    lat_weights(groups, row_slots, meta, starts, lower, half, lat_pad - lower.shape[1])
+
+
+def lat_kernel(groups, masks, meta, mixer, upper, lower, pert, *refs):
     received, (kept, given, field) = refs[:groups], refs[groups:]
     useful = received[0].shape[0]
     for g in range(groups):
-        field[g * useful:(g + 1) * useful, :] = received[g][...].astype(jnp.float32)
-    lat_columns(meta[2 * groups + 1] == 1, mixer, pert, table, field, kept, given)
+        place = (meta[2 * groups] ^ masks[g]) * useful
+        field[pl.ds(place, useful), :] = received[g][...].astype(jnp.float32)
+    lat_columns(meta[2 * groups + 1] == 1, mixer, pert, upper, lower, field, kept, given)
 
 
 def sending_order(groups):
@@ -276,14 +286,16 @@
     values += lon_filter(kernel, masks[2:], lon_pad, LON_LIMIT, (), [vmem, hbm], meta, fields, values[0])
     received = [send(mask, value) if mask else value for mask, value in zip(masks, values)]
 
-    mixer, table = pl.pallas_call(
-        functools.partial(matrices_kernel, groups, row_slots, masks),
+    reach = min(lat_reach(groups, row_slots), groups // 2)
+    mixer, upper, lower = pl.pallas_call(
+        functools.partial(matrices_kernel, groups, row_slots),
         out_shape=[
-            jax.ShapeDtypeStruct((lanes, lanes), jnp.bfloat16),
-            jax.ShapeDtypeStruct((lat_pad, lat_pad), jnp.bfloat16),
+            jax.ShapeDtypeStruct((2 * lanes, 2 * lanes), jnp.bfloat16),
+            jax.ShapeDtypeStruct((lat_pad // 2, lat_pad // 2), jnp.bfloat16),
+            jax.ShapeDtypeStruct((lat_pad // 2, lat_pad // 2 + reach * row_slots), jnp.bfloat16),
         ],
         in_specs=[smem, vmem, hbm],
-        out_specs=[vmem] * 2,
+        out_specs=[vmem] * 3,
         scratch_shapes=[pltpu.SMEM((groups,), jnp.int32)],
         compiler_params=pltpu.CompilerParams(vmem_limit_bytes=4 * MIB),
         name="matrices",
@@ -291,17 +303,17 @@
 
     half = levels // 2
     kept, given = pl.pallas_call(
-        functools.partial(lat_kernel, groups),
+        functools.partial(lat_kernel, groups, masks),
         out_shape=[
             jax.ShapeDtypeStruct((col_slots, half, lat_pad), jnp.float32),
             jax.ShapeDtypeStruct((col_slots, half, lat_pad), jnp.bfloat16 if shares == 2 else jnp.float32),
         ],
-        in_specs=[smem] + [vmem] * (3 + groups),
+        in_specs=[smem] + [vmem] * (4 + groups),
         out_specs=[vmem] * 2,
         scratch_shapes=[pltpu.VMEM((lat_pad * col_slots, lanes), jnp.float32)],
         compiler_params=pltpu.CompilerParams(vmem_limit_bytes=LAT_LIMIT),
         name="lat_filter",
-    )(meta, mixer, table, pert, *received)
+    )(meta, mixer, upper, lower, pert, *received)
     if shares == 2:
         total = kept + lax.ppermute(given, "mem", [(0, 1), (1, 0)]).astype(jnp.float32)
     else:

time: 112 us -> 111 us (level)
  no operation moved by 1% of the time
where the time goes in v6:
time: 111 us
  waiting for transfers between devices  52 us (47%)
  starting transfers between devices  39.9 us (36%)
  Pallas kernels  14.2 us (13%)
  local copies, waits for them, and re-layouts  3.25 us (3%)
  other arithmetic  1.22 us (1%)
    ppermute x15, waiting for transfers between devices, send(): return lax.ppermute(value, 'grid', [(g, g ^ mask) for g in range(groups)])  50.4 us
    ppermute x15, starting transfers between devices, send(): return lax.ppermute(value, 'grid', [(g, g ^ mask) for g in range(groups)])  38.4 us
    pallas_call x2, Pallas kernels, lon_filter(): pl.pallas_call(kernel, out_shape=[jax.ShapeDtypeStruct((row_slots * col_s...  8.38 us
    pallas_call x1, Pallas kernels, per_device(): pl.pallas_call(functools.partial(lat_kernel, groups, masks), out_shape=[j...  4.36 us
    unnamed x12, local copies, waits for them, and re-layouts  3.25 us
  transfers between devices with their start and end apart: 16, of which 9 were waited for; matrix products, arithmetic and copies ran while one was open for 0% of the time, Pallas kernels for 6%

profile of v6, /device:TPU:9, one launch (start us, length us, event | category | flops | bytes accessed | tf_op | source)
XLA Modules:
  0.0 110.6 jit_solution(13771331330686987314)
XLA Ops:
  0.0 0.0 copy-start.4
  0.0 0.0 copy-start.5
  0.0 3.4 %lon_filter.2 = (bf16[1058,128]{1,0:T(8,128)(2,1)}, bf16[1058,128]{1,0:T(8,128)(2,1)}) custom-call(s32[16]{0:T(128)} %counts.1, bf16[4,23,32,736]{3,2,1,0:T(8,128)(2,1)} %bitcast.6, bf16[4,23,32,736]{3,2,1,0:T(8,128)(2,1)} %bitcast.7, bf16[4,23,32,736]{3,2,1,0:T(8,128)(2,1)} %bitcast.8), custom_call_target="tpu_custom_call" | custom-call | tf_op jit(solution)/shard_map/lon_filter/pallas_call | solution.py:251
  3.4 3.2 %collective-permute-start.1 = (bf16[1058,128]{1,0:T(8,128)(2,1)}, bf16[1058,128]{1,0:T(8,128)(2,1)S(1)}, u32[]{:S(2)}, u32[]{:S(2)}) collective-permute-start(bf16[1058,128]{1,0:T(8,128)(2,1)} %get-tuple-element.31), channel_id=1, source_target_pairs={{0,9},{1,8},{2,11},{3,10},{4,13},{5,12},{6,15},{7,14},{8,1},{9,0},... | collective-permute-start | bytes 812552 | tf_op jit(solution)/shard_map/ppermute | solution.py:267
  6.6 0.1 collective-permute-start
  6.7 0.0 copy-done.4
  6.7 0.0 copy-done.5
  6.7 0.1 pad_add_fusion.meta
  6.8 0.0 copy-start
  6.8 2.3 %copy-done = bf16[4,32,23,736]{3,1,2,0:T(8,128)(2,1)S(1)} copy-done((bf16[4,32,23,736]{3,1,2,0:T(8,128)(2,1)S(1)}, bf16[4,32,23,736]{3,1,2,0:T(8,128)(2,1)}, u32[]{:S(2)}) %copy-start) | copy-done | bytes 4333592
  9.1 0.0 copy-start.2
  9.1 1.0 copy-done.2
  10.0 5.0 %lon_filter.3 = (bf16[1058,128]{1,0:T(8,128)(2,1)S(1)}, bf16[1058,128]{1,0:T(8,128)(2,1)S(1)}, bf16[1058,128]{1,0:T(8,128)(2,1)S(1)}, bf16[1058,128]{1,0:T(8,128...) custom-call(s32[34]{0:T(128)S(1)} %pad_add_fusion.meta, ...), custom_call_target="tpu_custom_call" | custom-call | tf_op jit(solution)/shard_map/lon_filter/pallas_call | solution.py:251
  15.0 0.2 collective-permute-start.2
  15.2 1.3 %collective-permute-start.3 = (bf16[1058,128]{1,0:T(8,128)(2,1)S(1)}, bf16[1058,128]{1,0:T(8,128)(2,1)S(1)}, u32[]{:S(2)}, u32[]{:S(2)}) collective-permute-start(bf16[1058,128]{1,0:T(8,128)(2,1)S(1)} %get-tuple-element.33), channel_id=1, source_target_pairs={{0,5},{1,4},{2,7},{3,6},{4,1},{5,0},{6,3},{7,2},{8,13},{9,12},{10,... | collective-permute-start | bytes 812552 | tf_op jit(solution)/shard_map/ppermute | solution.py:267
  16.5 3.3 %collective-permute-start.4 = (bf16[1058,128]{1,0:T(8,128)(2,1)S(1)}, bf16[1058,128]{1,0:T(8,128)(2,1)S(1)}, u32[]{:S(2)}, u32[]{:S(2)}) collective-permute-start(bf16[1058,128]{1,0:T(8,128)(2,1)S(1)} %get-tuple-element.34), channel_id=1, source_target_pairs={{0,10},{1,11},{2,8},{3,9},{4,14},{5,15},{6,12},{7,13},{8,2},{9,3},... | collective-permute-start | bytes 812552 | tf_op jit(solution)/shard_map/ppermute | solution.py:267
  19.8 5.0 %collective-permute-done.1.refs_1_ = bf16[1058,128]{1,0:T(8,128)(2,1)S(1)} collective-permute-done((bf16[1058,128]{1,0:T(8,128)(2,1)}, bf16[1058,128]{1,0:T(8,128)(2,1)S(1)}, u32[]{:S(2)}, u32[]{:S(2)}) %collective-permute-start.1) | collective-permute-done | bytes 270880 | tf_op jit(solution)/shard_map/ppermute | solution.py:267
  24.8 0.9 collective-permute-start.5
  25.7 5.5 %collective-permute-done.refs_0_ = bf16[1058,128]{1,0:T(8,128)(2,1)S(1)} collective-permute-done((bf16[1058,128]{1,0:T(8,128)(2,1)}, bf16[1058,128]{1,0:T(8,128)(2,1)S(1)}, u32[]{:S(2)}, u32[]{:S(2)}) %collective-permute-start) | collective-permute-done | bytes 270880 | tf_op jit(solution)/shard_map/ppermute | solution.py:267
  31.2 4.4 %collective-permute-start.6 = (bf16[1058,128]{1,0:T(8,128)(2,1)S(1)}, bf16[1058,128]{1,0:T(8,128)(2,1)S(1)}, u32[]{:S(2)}, u32[]{:S(2)}) collective-permute-start(bf16[1058,128]{1,0:T(8,128)(2,1)S(1)} %get-tuple-element.36), channel_id=1, source_target_pairs={{0,11},{1,10},{2,9},{3,8},{4,15},{5,14},{6,13},{7,12},{8,3},{9,2},... | collective-permute-start | bytes 812552 | tf_op jit(solution)/shard_map/ppermute | solution.py:267
  35.6 0.0 collective-permute-done.2.refs_2_
  35.6 0.0 collective-permute-start.7
  35.6 7.8 %collective-permute-done.3.refs_3_ = bf16[1058,128]{1,0:T(8,128)(2,1)S(1)} collective-permute-done((bf16[1058,128]{1,0:T(8,128)(2,1)S(1)}, bf16[1058,128]{1,0:T(8,128)(2,1)S(1)}, u32[]{:S(2)}, u32[]{:S(2)}) %collective-permute-start.3) | collective-permute-done | bytes 270880 | tf_op jit(solution)/shard_map/ppermute | solution.py:267
  43.4 2.6 %collective-permute-start.8 = (bf16[1058,128]{1,0:T(8,128)(2,1)S(1)}, bf16[1058,128]{1,0:T(8,128)(2,1)S(1)}, u32[]{:S(2)}, u32[]{:S(2)}) collective-permute-start(bf16[1058,128]{1,0:T(8,128)(2,1)S(1)} %get-tuple-element.38), channel_id=1, source_target_pairs={{0,12},{1,13},{2,14},{3,15},{4,8},{5,9},{6,10},{7,11},{8,4},{9,5},... | collective-permute-start | bytes 812552 | tf_op jit(solution)/shard_map/ppermute | solution.py:267
  46.0 0.0 collective-permute-done.4.refs_4_
  46.0 0.3 collective-permute-start.9
  46.2 6.7 %collective-permute-done.5.refs_5_ = bf16[1058,128]{1,0:T(8,128)(2,1)S(1)} collective-permute-done((bf16[1058,128]{1,0:T(8,128)(2,1)S(1)}, bf16[1058,128]{1,0:T(8,128)(2,1)S(1)}, u32[]{:S(2)}, u32[]{:S(2)}) %collective-permute-start.5) | collective-permute-done | bytes 270880 | tf_op jit(solution)/shard_map/ppermute | solution.py:267
  52.9 10.4 %collective-permute-start.10 = (bf16[1058,128]{1,0:T(8,128)(2,1)S(1)}, bf16[1058,128]{1,0:T(8,128)(2,1)S(1)}, u32[]{:S(2)}, u32[]{:S(2)}) collective-permute-start(bf16[1058,128]{1,0:T(8,128)(2,1)S(1)} %get-tuple-element.40), channel_id=1, source_target_pairs={{0,13},{1,12},{2,15},{3,14},{4,9},{5,8},{6,11},{7,10},{8,5},{9,4},... | collective-permute-start | bytes 812552 | tf_op jit(solution)/shard_map/ppermute | solution.py:267
  63.4 0.0 collective-permute-done.6.refs_6_
  63.4 1.2 %collective-permute-start.11 = (bf16[1058,128]{1,0:T(8,128)(2,1)S(1)}, bf16[1058,128]{1,0:T(8,128)(2,1)S(1)}, u32[]{:S(2)}, u32[]{:S(2)}) collective-permute-start(bf16[1058,128]{1,0:T(8,128)(2,1)S(1)} %get-tuple-element.41), channel_id=1, source_target_pairs={{0,2},{1,3},{2,0},{3,1},{4,6},{5,7},{6,4},{7,5},{8,10},{9,11},{10,... | collective-permute-start | bytes 812552 | tf_op jit(solution)/shard_map/ppermute | solution.py:267
  64.6 0.8 collective-permute-done.7.refs_7_
  65.4 10.5 %collective-permute-start.12 = (bf16[1058,128]{1,0:T(8,128)(2,1)S(1)}, bf16[1058,128]{1,0:T(8,128)(2,1)S(1)}, u32[]{:S(2)}, u32[]{:S(2)}) collective-permute-start(bf16[1058,128]{1,0:T(8,128)(2,1)S(1)} %get-tuple-element.42), channel_id=1, source_target_pairs={{0,14},{1,15},{2,12},{3,13},{4,10},{5,11},{6,8},{7,9},{8,6},{9,7},... | collective-permute-start | bytes 812552 | tf_op jit(solution)/shard_map/ppermute | solution.py:267
  75.9 0.0 collective-permute-done.8.refs_8_
  75.9 0.0 collective-permute-start.13
  75.9 0.0 collective-permute-done.9.refs_9_
  75.9 0.1 collective-permute-start.14
  76.0 0.0 copy-done.3
  76.0 1.4 %matrices.1 = (bf16[256,256]{1,0:T(8,128)(2,1)S(1)}, bf16[184,184]{1,0:T(8,128)(2,1)S(1)}, bf16[184,253]{1,0:T(8,128)(2,1)S(1)}) custom-call(s32[34]{0:T(128)S(1)} %pad_add_fusion.meta, bf16[32,32]{1,0:T(8,128)(2,1)S(1)} %copy-done.3, bf16[1058,128]{1,0:T(8,128)(2,1)S(1)} %get-tuple-element.27.after.refs_15_), custom_call_target="tpu_custom_call" | custom-call | tf_op jit(solution)/shard_map/matrices/pallas_call | solution.py:290
  77.4 1.2 %collective-permute-done.10.refs_10_ = bf16[1058,128]{1,0:T(8,128)(2,1)S(1)} collective-permute-done((bf16[1058,128]{1,0:T(8,128)(2,1)S(1)}, bf16[1058,128]{1,0:T(8,128)(2,1)S(1)}, u32[]{:S(2)}, u32[]{:S(2)}) %collective-permute-start.10) | collective-permute-done | bytes 270880 | tf_op jit(solution)/shard_map/ppermute | solution.py:267
  78.6 0.0 collective-permute-done.11.refs_11_
  78.6 15.3 %collective-permute-done.12.refs_12_ = bf16[1058,128]{1,0:T(8,128)(2,1)S(1)} collective-permute-done((bf16[1058,128]{1,0:T(8,128)(2,1)S(1)}, bf16[1058,128]{1,0:T(8,128)(2,1)S(1)}, u32[]{:S(2)}, u32[]{:S(2)}) %collective-permute-start.12) | collective-permute-done | bytes 270880 | tf_op jit(solution)/shard_map/ppermute | solution.py:267
  93.9 0.0 collective-permute-done.13.refs_13_
  93.9 8.1 %collective-permute-done.14.refs_14_ = bf16[1058,128]{1,0:T(8,128)(2,1)S(1)} collective-permute-done((bf16[1058,128]{1,0:T(8,128)(2,1)S(1)}, bf16[1058,128]{1,0:T(8,128)(2,1)S(1)}, u32[]{:S(2)}, u32[]{:S(2)}) %collective-permute-start.14) | collective-permute-done | bytes 270880 | tf_op jit(solution)/shard_map/ppermute | solution.py:267
  102.0 0.0 copy-done.1
  102.0 4.4 %lat_filter.1 = (f32[46,16,368]{2,1,0:T(8,128)S(1)}, bf16[46,16,368]{2,1,0:T(8,128)(2,1)S(1)}) custom-call(s32[34]{0:T(128)S(1)} %pad_add_fusion.meta, bf16[256,256]{1,0:T(8,128)(2,1)S(1)} %get-tuple-element.28.mixer, bf16[184,184]{1,0:T(8,128)(2,1)S(1)} %get-tuple-element.29.upper, bf16[184,253]{1,0:T(8,128)(2,1)S(1)} %get-tuple-element.30.lower, ...), custom_call_target="tpu_custom_call" | custom-call | tf_op jit(solution)/shard_map/lat_filter/pallas_call | solution.py:305
  106.4 1.5 %collective-permute-start.15 = (bf16[46,16,368]{2,1,0:T(8,128)(2,1)S(1)}, bf16[46,16,368]{2,1,0:T(8,128)(2,1)S(1)}, u32[]{:S(2)}, u32[]{:S(2)}) collective-permute-start(bf16[46,16,368]{2,1,0:T(8,128)(2,1)S(1)} %get-tuple-element.46), channel_id=1, source_target_pairs={{0,16},{16,0},{1,17},{17,1},{2,18},{18,2},{3,19},{19,3},{4,20},{20... | collective-permute-start | bytes 1625096 | tf_op jit(solution)/shard_map/ppermute | solution.py:318
  107.8 1.6 %collective-permute-done.15 = bf16[46,16,368]{2,1,0:T(8,128)(2,1)S(1)} collective-permute-done((bf16[46,16,368]{2,1,0:T(8,128)(2,1)S(1)}, bf16[46,16,368]{2,1,0:T(8,128)(2,1)S(1)}, u32[]{:S(2)}, u32[]{:S(2)}) %collective-permute-start.15) | collective-permute-done | bytes 541728 | tf_op jit(solution)/shard_map/ppermute | solution.py:318
  109.4 1.1 %add_bitcast_fusion = f32[16,46,368]{2,0,1:T(8,128)} fusion(f32[46,16,368]{2,1,0:T(8,128)S(1)} %get-tuple-element.45, bf16[46,16,368]{2,1,0:T(8,128)(2,1)S(1)} %collective-permute-done.15), kind=kLoop, calls=%fused_computation | loop fusion | flops 541696 | bytes 2708480 | tf_op jit(solution)/shard_map/transpose | solution.py:323
  (2 shorter events, 0.0 us)
Async XLA Ops:
  0.0 6.7 %copy-start.4 = (s32[16]{0:T(128)S(1)}, s32[16]{0:T(128)}, u32[]{:S(2)}) copy-start(s32[16]{0:T(128)} %counts.1) | copy-start | bytes 196
  0.0 6.7 %copy-start.5 = (s32[16]{0:T(128)S(1)}, s32[16]{0:T(128)}, u32[]{:S(2)}) copy-start(s32[16]{0:T(128)} %param.8) | copy-start | bytes 196
  3.4 21.4 %collective-permute-start.1 = (bf16[1058,128]{1,0:T(8,128)(2,1)}, bf16[1058,128]{1,0:T(8,128)(2,1)S(1)}, u32[]{:S(2)}, u32[]{:S(2)}) collective-permute-start(bf16[1058,128]{1,0:T(8,128)(2,1)} %get-tuple-element.31), channel_id=1, source_target_pairs={{0,9},{1,8},{2,11},{3,10},{4,13},{5,12},{6,15},{7,14},{8,1},{9,0},... | collective-permute-start | bytes 812552 | tf_op jit(solution)/shard_map/ppermute | solution.py:267
  6.6 24.6 %collective-permute-start = (bf16[1058,128]{1,0:T(8,128)(2,1)}, bf16[1058,128]{1,0:T(8,128)(2,1)S(1)}, u32[]{:S(2)}, u32[]{:S(2)}) collective-permute-start(bf16[1058,128]{1,0:T(8,128)(2,1)} %get-tuple-element.26.refs_0_), channel_id=1, source_target_pairs={{0,8},{1,9},{2,10},{3,11},{4,12},{5,13},{6,14},{7,15},{8,0},{9,1},... | collective-permute-start | bytes 812552 | tf_op jit(solution)/shard_map/ppermute | solution.py:267
  6.8 2.3 %copy-start = (bf16[4,32,23,736]{3,1,2,0:T(8,128)(2,1)S(1)}, bf16[4,32,23,736]{3,1,2,0:T(8,128)(2,1)}, u32[]{:S(2)}) copy-start(bf16[4,32,23,736]{3,1,2,0:T(8,128)(2,1)} %param.5) | copy-start | bytes 13000708
  9.1 1.0 copy-start.2
  10.0 65.9 %copy-start.3 = (bf16[32,32]{1,0:T(8,128)(2,1)S(1)}, bf16[32,32]{1,0:T(8,128)(2,1)}, u32[]{:S(2)}) copy-start(bf16[32,32]{1,0:T(8,128)(2,1)} %vertical.1) | copy-start | bytes 6148
  10.0 92.0 %copy-start.1 = (bf16[4,32,46,368]{3,1,2,0:T(8,128)(2,1)S(1)}, bf16[4,32,46,368]{3,1,2,0:T(8,128)(2,1)}, u32[]{:S(2)}) copy-start(bf16[4,32,46,368]{3,1,2,0:T(8,128)(2,1)} %param.6) | copy-start | bytes 13000708
  15.0 20.6 %collective-permute-start.2 = (bf16[1058,128]{1,0:T(8,128)(2,1)S(1)}, bf16[1058,128]{1,0:T(8,128)(2,1)S(1)}, u32[]{:S(2)}, u32[]{:S(2)}) collective-permute-start(bf16[1058,128]{1,0:T(8,128)(2,1)S(1)} %get-tuple-element.32), channel_id=1, source_target_pairs={{0,4},{1,5},{2,6},{3,7},{4,0},{5,1},{6,2},{7,3},{8,12},{9,13},{10,... | collective-permute-start | bytes 812552 | tf_op jit(solution)/shard_map/ppermute | solution.py:267
  15.2 28.2 %collective-permute-start.3 = (bf16[1058,128]{1,0:T(8,128)(2,1)S(1)}, bf16[1058,128]{1,0:T(8,128)(2,1)S(1)}, u32[]{:S(2)}, u32[]{:S(2)}) collective-permute-start(bf16[1058,128]{1,0:T(8,128)(2,1)S(1)} %get-tuple-element.33), channel_id=1, source_target_pairs={{0,5},{1,4},{2,7},{3,6},{4,1},{5,0},{6,3},{7,2},{8,13},{9,12},{10,... | collective-permute-start | bytes 812552 | tf_op jit(solution)/shard_map/ppermute | solution.py:267
  16.5 29.5 %collective-permute-start.4 = (bf16[1058,128]{1,0:T(8,128)(2,1)S(1)}, bf16[1058,128]{1,0:T(8,128)(2,1)S(1)}, u32[]{:S(2)}, u32[]{:S(2)}) collective-permute-start(bf16[1058,128]{1,0:T(8,128)(2,1)S(1)} %get-tuple-element.34), channel_id=1, source_target_pairs={{0,10},{1,11},{2,8},{3,9},{4,14},{5,15},{6,12},{7,13},{8,2},{9,3},... | collective-permute-start | bytes 812552 | tf_op jit(solution)/shard_map/ppermute | solution.py:267
  24.8 28.1 %collective-permute-start.5 = (bf16[1058,128]{1,0:T(8,128)(2,1)S(1)}, bf16[1058,128]{1,0:T(8,128)(2,1)S(1)}, u32[]{:S(2)}, u32[]{:S(2)}) collective-permute-start(bf16[1058,128]{1,0:T(8,128)(2,1)S(1)} %get-tuple-element.35), channel_id=1, source_target_pairs={{0,6},{1,7},{2,4},{3,5},{4,2},{5,3},{6,0},{7,1},{8,14},{9,15},{10,... | collective-permute-start | bytes 812552 | tf_op jit(solution)/shard_map/ppermute | solution.py:267
  31.2 32.2 %collective-permute-start.6 = (bf16[1058,128]{1,0:T(8,128)(2,1)S(1)}, bf16[1058,128]{1,0:T(8,128)(2,1)S(1)}, u32[]{:S(2)}, u32[]{:S(2)}) collective-permute-start(bf16[1058,128]{1,0:T(8,128)(2,1)S(1)} %get-tuple-element.36), channel_id=1, source_target_pairs={{0,11},{1,10},{2,9},{3,8},{4,15},{5,14},{6,13},{7,12},{8,3},{9,2},... | collective-permute-start | bytes 812552 | tf_op jit(solution)/shard_map/ppermute | solution.py:267
  35.6 29.8 %collective-permute-start.7 = (bf16[1058,128]{1,0:T(8,128)(2,1)S(1)}, bf16[1058,128]{1,0:T(8,128)(2,1)S(1)}, u32[]{:S(2)}, u32[]{:S(2)}) collective-permute-start(bf16[1058,128]{1,0:T(8,128)(2,1)S(1)} %get-tuple-element.37), channel_id=1, source_target_pairs={{0,7},{1,6},{2,5},{3,4},{4,3},{5,2},{6,1},{7,0},{8,15},{9,14},{10,... | collective-permute-start | bytes 812552 | tf_op jit(solution)/shard_map/ppermute | solution.py:267
  43.4 32.5 %collective-permute-start.8 = (bf16[1058,128]{1,0:T(8,128)(2,1)S(1)}, bf16[1058,128]{1,0:T(8,128)(2,1)S(1)}, u32[]{:S(2)}, u32[]{:S(2)}) collective-permute-start(bf16[1058,128]{1,0:T(8,128)(2,1)S(1)} %get-tuple-element.38), channel_id=1, source_target_pairs={{0,12},{1,13},{2,14},{3,15},{4,8},{5,9},{6,10},{7,11},{8,4},{9,5},... | collective-permute-start | bytes 812552 | tf_op jit(solution)/shard_map/ppermute | solution.py:267
  46.0 29.9 %collective-permute-start.9 = (bf16[1058,128]{1,0:T(8,128)(2,1)S(1)}, bf16[1058,128]{1,0:T(8,128)(2,1)S(1)}, u32[]{:S(2)}, u32[]{:S(2)}) collective-permute-start(bf16[1058,128]{1,0:T(8,128)(2,1)S(1)} %get-tuple-element.39), channel_id=1, source_target_pairs={{0,1},{1,0},{2,3},{3,2},{4,5},{5,4},{6,7},{7,6},{8,9},{9,8},{10,11... | collective-permute-start | bytes 812552 | tf_op jit(solution)/shard_map/ppermute | solution.py:267
  52.9 25.6 %collective-permute-start.10 = (bf16[1058,128]{1,0:T(8,128)(2,1)S(1)}, bf16[1058,128]{1,0:T(8,128)(2,1)S(1)}, u32[]{:S(2)}, u32[]{:S(2)}) collective-permute-start(bf16[1058,128]{1,0:T(8,128)(2,1)S(1)} %get-tuple-element.40), channel_id=1, source_target_pairs={{0,13},{1,12},{2,15},{3,14},{4,9},{5,8},{6,11},{7,10},{8,5},{9,4},... | collective-permute-start | bytes 812552 | tf_op jit(solution)/shard_map/ppermute | solution.py:267
  63.4 15.2 %collective-permute-start.11 = (bf16[1058,128]{1,0:T(8,128)(2,1)S(1)}, bf16[1058,128]{1,0:T(8,128)(2,1)S(1)}, u32[]{:S(2)}, u32[]{:S(2)}) collective-permute-start(bf16[1058,128]{1,0:T(8,128)(2,1)S(1)} %get-tuple-element.41), channel_id=1, source_target_pairs={{0,2},{1,3},{2,0},{3,1},{4,6},{5,7},{6,4},{7,5},{8,10},{9,11},{10,... | collective-permute-start | bytes 812552 | tf_op jit(solution)/shard_map/ppermute | solution.py:267
  65.4 28.5 %collective-permute-start.12 = (bf16[1058,128]{1,0:T(8,128)(2,1)S(1)}, bf16[1058,128]{1,0:T(8,128)(2,1)S(1)}, u32[]{:S(2)}, u32[]{:S(2)}) collective-permute-start(bf16[1058,128]{1,0:T(8,128)(2,1)S(1)} %get-tuple-element.42), channel_id=1, source_target_pairs={{0,14},{1,15},{2,12},{3,13},{4,10},{5,11},{6,8},{7,9},{8,6},{9,7},... | collective-permute-start | bytes 812552 | tf_op jit(solution)/shard_map/ppermute | solution.py:267
  75.9 18.0 %collective-permute-start.13 = (bf16[1058,128]{1,0:T(8,128)(2,1)S(1)}, bf16[1058,128]{1,0:T(8,128)(2,1)S(1)}, u32[]{:S(2)}, u32[]{:S(2)}) collective-permute-start(bf16[1058,128]{1,0:T(8,128)(2,1)S(1)} %get-tuple-element.43), channel_id=1, source_target_pairs={{0,3},{1,2},{2,1},{3,0},{4,7},{5,6},{6,5},{7,4},{8,11},{9,10},{10,... | collective-permute-start | bytes 812552 | tf_op jit(solution)/shard_map/ppermute | solution.py:267
  75.9 26.1 %collective-permute-start.14 = (bf16[1058,128]{1,0:T(8,128)(2,1)S(1)}, bf16[1058,128]{1,0:T(8,128)(2,1)S(1)}, u32[]{:S(2)}, u32[]{:S(2)}) collective-permute-start(bf16[1058,128]{1,0:T(8,128)(2,1)S(1)} %get-tuple-element.44), channel_id=1, source_target_pairs={{0,15},{1,14},{2,13},{3,12},{4,11},{5,10},{6,9},{7,8},{8,7},{9,6},... | collective-permute-start | bytes 812552 | tf_op jit(solution)/shard_map/ppermute | solution.py:267
  106.4 3.1 %collective-permute-start.15 = (bf16[46,16,368]{2,1,0:T(8,128)(2,1)S(1)}, bf16[46,16,368]{2,1,0:T(8,128)(2,1)S(1)}, u32[]{:S(2)}, u32[]{:S(2)}) collective-permute-start(bf16[46,16,368]{2,1,0:T(8,128)(2,1)S(1)} %get-tuple-element.46), channel_id=1, source_target_pairs={{0,16},{16,0},{1,17},{17,1},{2,18},{18,2},{3,19},{19,3},{4,20},{20... | collective-permute-start | bytes 1625096 | tf_op jit(solution)/shard_map/ppermute | solution.py:318

commit v7 on v6

--- a/solution.py
+++ b/solution.py
@@ -74,7 +74,7 @@
                     n * col_rows:n * col_rows + col_slots, r * lanes:(r + 1) * lanes
                 ]
     for n, out in enumerate(outs):
-        out[...] = packed[n].astype(jnp.bfloat16)
+        out[...] = packed[n, :out.shape[0]].astype(jnp.bfloat16)
 
 
 def window_tiles(groups, lon_pad):
@@ -256,7 +256,7 @@
             out_specs=[vmem] * len(masks),
             scratch_shapes=[
                 pltpu.VMEM((len(masks) * round_up(col_slots, 16), columns), jnp.bfloat16),
-                pltpu.VMEM((len(masks), row_slots * col_slots, lanes), jnp.float32),
+                pltpu.VMEM((len(masks), round_up(row_slots * col_slots, 8) + 8, lanes), jnp.float32),
                 pltpu.SMEM((groups,), jnp.int32),
             ],
             compiler_params=pltpu.CompilerParams(vmem_limit_bytes=limit),
@@ -310,7 +310,7 @@
         ],
         in_specs=[smem] + [vmem] * (4 + groups),
         out_specs=[vmem] * 2,
-        scratch_shapes=[pltpu.VMEM((lat_pad * col_slots, lanes), jnp.float32)],
+        scratch_shapes=[pltpu.VMEM(((lat_pad + 8) * col_slots, lanes), jnp.float32)],
         compiler_params=pltpu.CompilerParams(vmem_limit_bytes=LAT_LIMIT),
         name="lat_filter",
     )(meta, mixer, upper, lower, pert, *received)

time: 111 us -> 111 us (level)
  no operation moved by 1% of the time
where the time goes in v7:
time: 111 us
  waiting for transfers between devices  52 us (47%)
  starting transfers between devices  39.9 us (36%)
  Pallas kernels  14.1 us (13%)
  local copies, waits for them, and re-layouts  3.25 us (3%)
  other arithmetic  1.22 us (1%)
    ppermute x15, waiting for transfers between devices, send(): return lax.ppermute(value, 'grid', [(g, g ^ mask) for g in range(groups)])  50.4 us
    ppermute x15, starting transfers between devices, send(): return lax.ppermute(value, 'grid', [(g, g ^ mask) for g in range(groups)])  38.4 us
    pallas_call x2, Pallas kernels, lon_filter(): pl.pallas_call(kernel, out_shape=[jax.ShapeDtypeStruct((row_slots * col_s...  8.38 us
    pallas_call x1, Pallas kernels, per_device(): pl.pallas_call(functools.partial(lat_kernel, groups, masks), out_shape=[j...  4.33 us
    unnamed x12, local copies, waits for them, and re-layouts  3.25 us
  transfers between devices with their start and end apart: 16, of which 9 were waited for; matrix products, arithmetic and copies ran while one was open for 0% of the time, Pallas kernels for 6%

profile of v7, /device:TPU:9, one launch (start us, length us, event | category | flops | bytes accessed | tf_op | source)
XLA Modules:
  0.0 110.5 jit_solution(11460575672948560072)
XLA Ops:
  0.0 0.0 copy-start.4
  0.0 0.0 copy-start.5
  0.0 3.4 %lon_filter.2 = (bf16[1058,128]{1,0:T(8,128)(2,1)}, bf16[1058,128]{1,0:T(8,128)(2,1)}) custom-call(s32[16]{0:T(128)} %counts.1, bf16[4,23,32,736]{3,2,1,0:T(8,128)(2,1)} %bitcast.6, bf16[4,23,32,736]{3,2,1,0:T(8,128)(2,1)} %bitcast.7, bf16[4,23,32,736]{3,2,1,0:T(8,128)(2,1)} %bitcast.8), custom_call_target="tpu_custom_call" | custom-call | tf_op jit(solution)/shard_map/lon_filter/pallas_call | solution.py:251
  3.4 3.2 %collective-permute-start.1 = (bf16[1058,128]{1,0:T(8,128)(2,1)}, bf16[1058,128]{1,0:T(8,128)(2,1)S(1)}, u32[]{:S(2)}, u32[]{:S(2)}) collective-permute-start(bf16[1058,128]{1,0:T(8,128)(2,1)} %get-tuple-element.31), channel_id=1, source_target_pairs={{0,9},{1,8},{2,11},{3,10},{4,13},{5,12},{6,15},{7,14},{8,1},{9,0},... | collective-permute-start | bytes 812552 | tf_op jit(solution)/shard_map/ppermute | solution.py:267
  6.6 0.1 collective-permute-start
  6.7 0.0 copy-done.4
  6.7 0.0 copy-done.5
  6.7 0.1 pad_add_fusion.meta
  6.8 2.3 %copy-done = bf16[4,32,23,736]{3,1,2,0:T(8,128)(2,1)S(1)} copy-done((bf16[4,32,23,736]{3,1,2,0:T(8,128)(2,1)S(1)}, bf16[4,32,23,736]{3,1,2,0:T(8,128)(2,1)}, u32[]{:S(2)}) %copy-start) | copy-done | bytes 4333592
  9.1 0.0 copy-start.2
  9.1 1.0 copy-done.2
  10.0 0.0 copy-start.3
  10.0 5.0 %lon_filter.3 = (bf16[1058,128]{1,0:T(8,128)(2,1)S(1)}, bf16[1058,128]{1,0:T(8,128)(2,1)S(1)}, bf16[1058,128]{1,0:T(8,128)(2,1)S(1)}, bf16[1058,128]{1,0:T(8,128...) custom-call(s32[34]{0:T(128)S(1)} %pad_add_fusion.meta, ...), custom_call_target="tpu_custom_call" | custom-call | tf_op jit(solution)/shard_map/lon_filter/pallas_call | solution.py:251
  15.0 0.2 collective-permute-start.2
  15.2 1.3 %collective-permute-start.3 = (bf16[1058,128]{1,0:T(8,128)(2,1)S(1)}, bf16[1058,128]{1,0:T(8,128)(2,1)S(1)}, u32[]{:S(2)}, u32[]{:S(2)}) collective-permute-start(bf16[1058,128]{1,0:T(8,128)(2,1)S(1)} %get-tuple-element.33), channel_id=1, source_target_pairs={{0,5},{1,4},{2,7},{3,6},{4,1},{5,0},{6,3},{7,2},{8,13},{9,12},{10,... | collective-permute-start | bytes 812552 | tf_op jit(solution)/shard_map/ppermute | solution.py:267
  16.5 3.3 %collective-permute-start.4 = (bf16[1058,128]{1,0:T(8,128)(2,1)S(1)}, bf16[1058,128]{1,0:T(8,128)(2,1)S(1)}, u32[]{:S(2)}, u32[]{:S(2)}) collective-permute-start(bf16[1058,128]{1,0:T(8,128)(2,1)S(1)} %get-tuple-element.34), channel_id=1, source_target_pairs={{0,10},{1,11},{2,8},{3,9},{4,14},{5,15},{6,12},{7,13},{8,2},{9,3},... | collective-permute-start | bytes 812552 | tf_op jit(solution)/shard_map/ppermute | solution.py:267
  19.8 5.0 %collective-permute-done.1.refs_1_ = bf16[1058,128]{1,0:T(8,128)(2,1)S(1)} collective-permute-done((bf16[1058,128]{1,0:T(8,128)(2,1)}, bf16[1058,128]{1,0:T(8,128)(2,1)S(1)}, u32[]{:S(2)}, u32[]{:S(2)}) %collective-permute-start.1) | collective-permute-done | bytes 270880 | tf_op jit(solution)/shard_map/ppermute | solution.py:267
  24.8 0.9 collective-permute-start.5
  25.7 5.5 %collective-permute-done.refs_0_ = bf16[1058,128]{1,0:T(8,128)(2,1)S(1)} collective-permute-done((bf16[1058,128]{1,0:T(8,128)(2,1)}, bf16[1058,128]{1,0:T(8,128)(2,1)S(1)}, u32[]{:S(2)}, u32[]{:S(2)}) %collective-permute-start) | collective-permute-done | bytes 270880 | tf_op jit(solution)/shard_map/ppermute | solution.py:267
  31.2 4.4 %collective-permute-start.6 = (bf16[1058,128]{1,0:T(8,128)(2,1)S(1)}, bf16[1058,128]{1,0:T(8,128)(2,1)S(1)}, u32[]{:S(2)}, u32[]{:S(2)}) collective-permute-start(bf16[1058,128]{1,0:T(8,128)(2,1)S(1)} %get-tuple-element.36), channel_id=1, source_target_pairs={{0,11},{1,10},{2,9},{3,8},{4,15},{5,14},{6,13},{7,12},{8,3},{9,2},... | collective-permute-start | bytes 812552 | tf_op jit(solution)/shard_map/ppermute | solution.py:267
  35.6 0.0 collective-permute-done.2.refs_2_
  35.6 0.0 collective-permute-start.7
  35.6 7.8 %collective-permute-done.3.refs_3_ = bf16[1058,128]{1,0:T(8,128)(2,1)S(1)} collective-permute-done((bf16[1058,128]{1,0:T(8,128)(2,1)S(1)}, bf16[1058,128]{1,0:T(8,128)(2,1)S(1)}, u32[]{:S(2)}, u32[]{:S(2)}) %collective-permute-start.3) | collective-permute-done | bytes 270880 | tf_op jit(solution)/shard_map/ppermute | solution.py:267
  43.4 2.6 %collective-permute-start.8 = (bf16[1058,128]{1,0:T(8,128)(2,1)S(1)}, bf16[1058,128]{1,0:T(8,128)(2,1)S(1)}, u32[]{:S(2)}, u32[]{:S(2)}) collective-permute-start(bf16[1058,128]{1,0:T(8,128)(2,1)S(1)} %get-tuple-element.38), channel_id=1, source_target_pairs={{0,12},{1,13},{2,14},{3,15},{4,8},{5,9},{6,10},{7,11},{8,4},{9,5},... | collective-permute-start | bytes 812552 | tf_op jit(solution)/shard_map/ppermute | solution.py:267
  46.0 0.0 collective-permute-done.4.refs_4_
  46.0 0.3 collective-permute-start.9
  46.2 6.7 %collective-permute-done.5.refs_5_ = bf16[1058,128]{1,0:T(8,128)(2,1)S(1)} collective-permute-done((bf16[1058,128]{1,0:T(8,128)(2,1)S(1)}, bf16[1058,128]{1,0:T(8,128)(2,1)S(1)}, u32[]{:S(2)}, u32[]{:S(2)}) %collective-permute-start.5) | collective-permute-done | bytes 270880 | tf_op jit(solution)/shard_map/ppermute | solution.py:267
  52.9 10.4 %collective-permute-start.10 = (bf16[1058,128]{1,0:T(8,128)(2,1)S(1)}, bf16[1058,128]{1,0:T(8,128)(2,1)S(1)}, u32[]{:S(2)}, u32[]{:S(2)}) collective-permute-start(bf16[1058,128]{1,0:T(8,128)(2,1)S(1)} %get-tuple-element.40), channel_id=1, source_target_pairs={{0,13},{1,12},{2,15},{3,14},{4,9},{5,8},{6,11},{7,10},{8,5},{9,4},... | collective-permute-start | bytes 812552 | tf_op jit(solution)/shard_map/ppermute | solution.py:267
  63.4 0.0 collective-permute-done.6.refs_6_
  63.4 1.2 %collective-permute-start.11 = (bf16[1058,128]{1,0:T(8,128)(2,1)S(1)}, bf16[1058,128]{1,0:T(8,128)(2,1)S(1)}, u32[]{:S(2)}, u32[]{:S(2)}) collective-permute-start(bf16[1058,128]{1,0:T(8,128)(2,1)S(1)} %get-tuple-element.41), channel_id=1, source_target_pairs={{0,2},{1,3},{2,0},{3,1},{4,6},{5,7},{6,4},{7,5},{8,10},{9,11},{10,... | collective-permute-start | bytes 812552 | tf_op jit(solution)/shard_map/ppermute | solution.py:267
  64.6 0.8 collective-permute-done.7.refs_7_
  65.4 10.5 %collective-permute-start.12 = (bf16[1058,128]{1,0:T(8,128)(2,1)S(1)}, bf16[1058,128]{1,0:T(8,128)(2,1)S(1)}, u32[]{:S(2)}, u32[]{:S(2)}) collective-permute-start(bf16[1058,128]{1,0:T(8,128)(2,1)S(1)} %get-tuple-element.42), channel_id=1, source_target_pairs={{0,14},{1,15},{2,12},{3,13},{4,10},{5,11},{6,8},{7,9},{8,6},{9,7},... | collective-permute-start | bytes 812552 | tf_op jit(solution)/shard_map/ppermute | solution.py:267
  75.9 0.0 collective-permute-done.8.refs_8_
  75.9 0.0 collective-permute-start.13
  75.9 0.0 collective-permute-done.9.refs_9_
  75.9 0.1 collective-permute-start.14
  76.0 0.0 copy-done.3
  76.0 1.4 %matrices.1 = (bf16[256,256]{1,0:T(8,128)(2,1)S(1)}, bf16[184,184]{1,0:T(8,128)(2,1)S(1)}, bf16[184,253]{1,0:T(8,128)(2,1)S(1)}) custom-call(s32[34]{0:T(128)S(1)} %pad_add_fusion.meta, bf16[32,32]{1,0:T(8,128)(2,1)S(1)} %copy-done.3, bf16[1058,128]{1,0:T(8,128)(2,1)S(1)} %get-tuple-element.27.after.refs_15_), custom_call_target="tpu_custom_call" | custom-call | tf_op jit(solution)/shard_map/matrices/pallas_call | solution.py:290
  77.4 1.2 %collective-permute-done.10.refs_10_ = bf16[1058,128]{1,0:T(8,128)(2,1)S(1)} collective-permute-done((bf16[1058,128]{1,0:T(8,128)(2,1)S(1)}, bf16[1058,128]{1,0:T(8,128)(2,1)S(1)}, u32[]{:S(2)}, u32[]{:S(2)}) %collective-permute-start.10) | collective-permute-done | bytes 270880 | tf_op jit(solution)/shard_map/ppermute | solution.py:267
  78.6 0.0 collective-permute-done.11.refs_11_
  78.6 15.3 %collective-permute-done.12.refs_12_ = bf16[1058,128]{1,0:T(8,128)(2,1)S(1)} collective-permute-done((bf16[1058,128]{1,0:T(8,128)(2,1)S(1)}, bf16[1058,128]{1,0:T(8,128)(2,1)S(1)}, u32[]{:S(2)}, u32[]{:S(2)}) %collective-permute-start.12) | collective-permute-done | bytes 270880 | tf_op jit(solution)/shard_map/ppermute | solution.py:267
  93.9 0.0 collective-permute-done.13.refs_13_
  93.9 8.1 %collective-permute-done.14.refs_14_ = bf16[1058,128]{1,0:T(8,128)(2,1)S(1)} collective-permute-done((bf16[1058,128]{1,0:T(8,128)(2,1)S(1)}, bf16[1058,128]{1,0:T(8,128)(2,1)S(1)}, u32[]{:S(2)}, u32[]{:S(2)}) %collective-permute-start.14) | collective-permute-done | bytes 270880 | tf_op jit(solution)/shard_map/ppermute | solution.py:267
  102.0 0.0 copy-done.1
  102.0 4.3 %lat_filter.1 = (f32[46,16,368]{2,1,0:T(8,128)S(1)}, bf16[46,16,368]{2,1,0:T(8,128)(2,1)S(1)}) custom-call(s32[34]{0:T(128)S(1)} %pad_add_fusion.meta, bf16[256,256]{1,0:T(8,128)(2,1)S(1)} %get-tuple-element.28.mixer, bf16[184,184]{1,0:T(8,128)(2,1)S(1)} %get-tuple-element.29.upper, bf16[184,253]{1,0:T(8,128)(2,1)S(1)} %get-tuple-element.30.lower, ...), custom_call_target="tpu_custom_call" | custom-call | tf_op jit(solution)/shard_map/lat_filter/pallas_call | solution.py:305
  106.3 1.5 %collective-permute-start.15 = (bf16[46,16,368]{2,1,0:T(8,128)(2,1)S(1)}, bf16[46,16,368]{2,1,0:T(8,128)(2,1)S(1)}, u32[]{:S(2)}, u32[]{:S(2)}) collective-permute-start(bf16[46,16,368]{2,1,0:T(8,128)(2,1)S(1)} %get-tuple-element.46), channel_id=1, source_target_pairs={{0,16},{16,0},{1,17},{17,1},{2,18},{18,2},{3,19},{19,3},{4,20},{20... | collective-permute-start | bytes 1625096 | tf_op jit(solution)/shard_map/ppermute | solution.py:318
  107.8 1.6 %collective-permute-done.15 = bf16[46,16,368]{2,1,0:T(8,128)(2,1)S(1)} collective-permute-done((bf16[46,16,368]{2,1,0:T(8,128)(2,1)S(1)}, bf16[46,16,368]{2,1,0:T(8,128)(2,1)S(1)}, u32[]{:S(2)}, u32[]{:S(2)}) %collective-permute-start.15) | collective-permute-done | bytes 541728 | tf_op jit(solution)/shard_map/ppermute | solution.py:318
  109.4 1.1 %add_bitcast_fusion = f32[16,46,368]{2,0,1:T(8,128)} fusion(f32[46,16,368]{2,1,0:T(8,128)S(1)} %get-tuple-element.45, bf16[46,16,368]{2,1,0:T(8,128)(2,1)S(1)} %collective-permute-done.15), kind=kLoop, calls=%fused_computation | loop fusion | flops 541696 | bytes 2708480 | tf_op jit(solution)/shard_map/transpose | solution.py:323
  (2 shorter events, 0.0 us)
Async XLA Ops:
  0.0 6.7 %copy-start.4 = (s32[16]{0:T(128)S(1)}, s32[16]{0:T(128)}, u32[]{:S(2)}) copy-start(s32[16]{0:T(128)} %counts.1) | copy-start | bytes 196
  0.0 6.7 %copy-start.5 = (s32[16]{0:T(128)S(1)}, s32[16]{0:T(128)}, u32[]{:S(2)}) copy-start(s32[16]{0:T(128)} %param.8) | copy-start | bytes 196
  3.4 21.4 %collective-permute-start.1 = (bf16[1058,128]{1,0:T(8,128)(2,1)}, bf16[1058,128]{1,0:T(8,128)(2,1)S(1)}, u32[]{:S(2)}, u32[]{:S(2)}) collective-permute-start(bf16[1058,128]{1,0:T(8,128)(2,1)} %get-tuple-element.31), channel_id=1, source_target_pairs={{0,9},{1,8},{2,11},{3,10},{4,13},{5,12},{6,15},{7,14},{8,1},{9,0},... | collective-permute-start | bytes 812552 | tf_op jit(solution)/shard_map/ppermute | solution.py:267
  6.6 24.6 %collective-permute-start = (bf16[1058,128]{1,0:T(8,128)(2,1)}, bf16[1058,128]{1,0:T(8,128)(2,1)S(1)}, u32[]{:S(2)}, u32[]{:S(2)}) collective-permute-start(bf16[1058,128]{1,0:T(8,128)(2,1)} %get-tuple-element.26.refs_0_), channel_id=1, source_target_pairs={{0,8},{1,9},{2,10},{3,11},{4,12},{5,13},{6,14},{7,15},{8,0},{9,1},... | collective-permute-start | bytes 812552 | tf_op jit(solution)/shard_map/ppermute | solution.py:267
  6.8 2.3 %copy-start = (bf16[4,32,23,736]{3,1,2,0:T(8,128)(2,1)S(1)}, bf16[4,32,23,736]{3,1,2,0:T(8,128)(2,1)}, u32[]{:S(2)}) copy-start(bf16[4,32,23,736]{3,1,2,0:T(8,128)(2,1)} %param.5) | copy-start | bytes 13000708
  9.1 1.0 copy-start.2
  10.0 65.9 %copy-start.3 = (bf16[32,32]{1,0:T(8,128)(2,1)S(1)}, bf16[32,32]{1,0:T(8,128)(2,1)}, u32[]{:S(2)}) copy-start(bf16[32,32]{1,0:T(8,128)(2,1)} %vertical.1) | copy-start | bytes 6148
  10.0 92.0 %copy-start.1 = (bf16[4,32,46,368]{3,1,2,0:T(8,128)(2,1)S(1)}, bf16[4,32,46,368]{3,1,2,0:T(8,128)(2,1)}, u32[]{:S(2)}) copy-start(bf16[4,32,46,368]{3,1,2,0:T(8,128)(2,1)} %param.6) | copy-start | bytes 13000708
  15.0 20.6 %collective-permute-start.2 = (bf16[1058,128]{1,0:T(8,128)(2,1)S(1)}, bf16[1058,128]{1,0:T(8,128)(2,1)S(1)}, u32[]{:S(2)}, u32[]{:S(2)}) collective-permute-start(bf16[1058,128]{1,0:T(8,128)(2,1)S(1)} %get-tuple-element.32), channel_id=1, source_target_pairs={{0,4},{1,5},{2,6},{3,7},{4,0},{5,1},{6,2},{7,3},{8,12},{9,13},{10,... | collective-permute-start | bytes 812552 | tf_op jit(solution)/shard_map/ppermute | solution.py:267
  15.2 28.2 %collective-permute-start.3 = (bf16[1058,128]{1,0:T(8,128)(2,1)S(1)}, bf16[1058,128]{1,0:T(8,128)(2,1)S(1)}, u32[]{:S(2)}, u32[]{:S(2)}) collective-permute-start(bf16[1058,128]{1,0:T(8,128)(2,1)S(1)} %get-tuple-element.33), channel_id=1, source_target_pairs={{0,5},{1,4},{2,7},{3,6},{4,1},{5,0},{6,3},{7,2},{8,13},{9,12},{10,... | collective-permute-start | bytes 812552 | tf_op jit(solution)/shard_map/ppermute | solution.py:267
  16.5 29.5 %collective-permute-start.4 = (bf16[1058,128]{1,0:T(8,128)(2,1)S(1)}, bf16[1058,128]{1,0:T(8,128)(2,1)S(1)}, u32[]{:S(2)}, u32[]{:S(2)}) collective-permute-start(bf16[1058,128]{1,0:T(8,128)(2,1)S(1)} %get-tuple-element.34), channel_id=1, source_target_pairs={{0,10},{1,11},{2,8},{3,9},{4,14},{5,15},{6,12},{7,13},{8,2},{9,3},... | collective-permute-start | bytes 812552 | tf_op jit(solution)/shard_map/ppermute | solution.py:267
  24.8 28.1 %collective-permute-start.5 = (bf16[1058,128]{1,0:T(8,128)(2,1)S(1)}, bf16[1058,128]{1,0:T(8,128)(2,1)S(1)}, u32[]{:S(2)}, u32[]{:S(2)}) collective-permute-start(bf16[1058,128]{1,0:T(8,128)(2,1)S(1)} %get-tuple-element.35), channel_id=1, source_target_pairs={{0,6},{1,7},{2,4},{3,5},{4,2},{5,3},{6,0},{7,1},{8,14},{9,15},{10,... | collective-permute-start | bytes 812552 | tf_op jit(solution)/shard_map/ppermute | solution.py:267
  31.2 32.2 %collective-permute-start.6 = (bf16[1058,128]{1,0:T(8,128)(2,1)S(1)}, bf16[1058,128]{1,0:T(8,128)(2,1)S(1)}, u32[]{:S(2)}, u32[]{:S(2)}) collective-permute-start(bf16[1058,128]{1,0:T(8,128)(2,1)S(1)} %get-tuple-element.36), channel_id=1, source_target_pairs={{0,11},{1,10},{2,9},{3,8},{4,15},{5,14},{6,13},{7,12},{8,3},{9,2},... | collective-permute-start | bytes 812552 | tf_op jit(solution)/shard_map/ppermute | solution.py:267
  35.6 29.8 %collective-permute-start.7 = (bf16[1058,128]{1,0:T(8,128)(2,1)S(1)}, bf16[1058,128]{1,0:T(8,128)(2,1)S(1)}, u32[]{:S(2)}, u32[]{:S(2)}) collective-permute-start(bf16[1058,128]{1,0:T(8,128)(2,1)S(1)} %get-tuple-element.37), channel_id=1, source_target_pairs={{0,7},{1,6},{2,5},{3,4},{4,3},{5,2},{6,1},{7,0},{8,15},{9,14},{10,... | collective-permute-start | bytes 812552 | tf_op jit(solution)/shard_map/ppermute | solution.py:267
  43.4 32.5 %collective-permute-start.8 = (bf16[1058,128]{1,0:T(8,128)(2,1)S(1)}, bf16[1058,128]{1,0:T(8,128)(2,1)S(1)}, u32[]{:S(2)}, u32[]{:S(2)}) collective-permute-start(bf16[1058,128]{1,0:T(8,128)(2,1)S(1)} %get-tuple-element.38), channel_id=1, source_target_pairs={{0,12},{1,13},{2,14},{3,15},{4,8},{5,9},{6,10},{7,11},{8,4},{9,5},... | collective-permute-start | bytes 812552 | tf_op jit(solution)/shard_map/ppermute | solution.py:267
  46.0 29.9 %collective-permute-start.9 = (bf16[1058,128]{1,0:T(8,128)(2,1)S(1)}, bf16[1058,128]{1,0:T(8,128)(2,1)S(1)}, u32[]{:S(2)}, u32[]{:S(2)}) collective-permute-start(bf16[1058,128]{1,0:T(8,128)(2,1)S(1)} %get-tuple-element.39), channel_id=1, source_target_pairs={{0,1},{1,0},{2,3},{3,2},{4,5},{5,4},{6,7},{7,6},{8,9},{9,8},{10,11... | collective-permute-start | bytes 812552 | tf_op jit(solution)/shard_map/ppermute | solution.py:267
  52.9 25.6 %collective-permute-start.10 = (bf16[1058,128]{1,0:T(8,128)(2,1)S(1)}, bf16[1058,128]{1,0:T(8,128)(2,1)S(1)}, u32[]{:S(2)}, u32[]{:S(2)}) collective-permute-start(bf16[1058,128]{1,0:T(8,128)(2,1)S(1)} %get-tuple-element.40), channel_id=1, source_target_pairs={{0,13},{1,12},{2,15},{3,14},{4,9},{5,8},{6,11},{7,10},{8,5},{9,4},... | collective-permute-start | bytes 812552 | tf_op jit(solution)/shard_map/ppermute | solution.py:267
  63.4 15.2 %collective-permute-start.11 = (bf16[1058,128]{1,0:T(8,128)(2,1)S(1)}, bf16[1058,128]{1,0:T(8,128)(2,1)S(1)}, u32[]{:S(2)}, u32[]{:S(2)}) collective-permute-start(bf16[1058,128]{1,0:T(8,128)(2,1)S(1)} %get-tuple-element.41), channel_id=1, source_target_pairs={{0,2},{1,3},{2,0},{3,1},{4,6},{5,7},{6,4},{7,5},{8,10},{9,11},{10,... | collective-permute-start | bytes 812552 | tf_op jit(solution)/shard_map/ppermute | solution.py:267
  65.4 28.5 %collective-permute-start.12 = (bf16[1058,128]{1,0:T(8,128)(2,1)S(1)}, bf16[1058,128]{1,0:T(8,128)(2,1)S(1)}, u32[]{:S(2)}, u32[]{:S(2)}) collective-permute-start(bf16[1058,128]{1,0:T(8,128)(2,1)S(1)} %get-tuple-element.42), channel_id=1, source_target_pairs={{0,14},{1,15},{2,12},{3,13},{4,10},{5,11},{6,8},{7,9},{8,6},{9,7},... | collective-permute-start | bytes 812552 | tf_op jit(solution)/shard_map/ppermute | solution.py:267
  75.9 18.0 %collective-permute-start.13 = (bf16[1058,128]{1,0:T(8,128)(2,1)S(1)}, bf16[1058,128]{1,0:T(8,128)(2,1)S(1)}, u32[]{:S(2)}, u32[]{:S(2)}) collective-permute-start(bf16[1058,128]{1,0:T(8,128)(2,1)S(1)} %get-tuple-element.43), channel_id=1, source_target_pairs={{0,3},{1,2},{2,1},{3,0},{4,7},{5,6},{6,5},{7,4},{8,11},{9,10},{10,... | collective-permute-start | bytes 812552 | tf_op jit(solution)/shard_map/ppermute | solution.py:267
  75.9 26.1 %collective-permute-start.14 = (bf16[1058,128]{1,0:T(8,128)(2,1)S(1)}, bf16[1058,128]{1,0:T(8,128)(2,1)S(1)}, u32[]{:S(2)}, u32[]{:S(2)}) collective-permute-start(bf16[1058,128]{1,0:T(8,128)(2,1)S(1)} %get-tuple-element.44), channel_id=1, source_target_pairs={{0,15},{1,14},{2,13},{3,12},{4,11},{5,10},{6,9},{7,8},{8,7},{9,6},... | collective-permute-start | bytes 812552 | tf_op jit(solution)/shard_map/ppermute | solution.py:267
  106.3 3.1 %collective-permute-start.15 = (bf16[46,16,368]{2,1,0:T(8,128)(2,1)S(1)}, bf16[46,16,368]{2,1,0:T(8,128)(2,1)S(1)}, u32[]{:S(2)}, u32[]{:S(2)}) collective-permute-start(bf16[46,16,368]{2,1,0:T(8,128)(2,1)S(1)} %get-tuple-element.46), channel_id=1, source_target_pairs={{0,16},{16,0},{1,17},{17,1},{2,18},{18,2},{3,19},{19,3},{4,20},{20... | collective-permute-start | bytes 1625096 | tf_op jit(solution)/shard_map/ppermute | solution.py:318

commit v8 on v7

--- a/solution.py
+++ b/solution.py
@@ -19,7 +19,7 @@
 FIRST_LIMIT = 60 * MIB
 LON_LIMIT = 24 * MIB
 LAT_LIMIT = 26 * MIB
-FETCH = 12
+FETCH = 24
 AHEAD = 3
 NT = (((1,), (1,)), ((), ()))
 NN = (((1,), (0,)), ((), ()))

time: 111 us -> 111 us (level)
  no operation moved by 1% of the time
where the time goes in v8:
time: 111 us
  waiting for transfers between devices  51.9 us (47%)
  starting transfers between devices  39.9 us (36%)
  Pallas kernels  14.1 us (13%)
  local copies, waits for them, and re-layouts  3.25 us (3%)
  other arithmetic  1.22 us (1%)
    ppermute x15, waiting for transfers between devices, send(): return lax.ppermute(value, 'grid', [(g, g ^ mask) for g in range(groups)])  50.3 us
    ppermute x15, starting transfers between devices, send(): return lax.ppermute(value, 'grid', [(g, g ^ mask) for g in range(groups)])  38.5 us
    pallas_call x2, Pallas kernels, lon_filter(): pl.pallas_call(kernel, out_shape=[jax.ShapeDtypeStruct((row_slots * col_s...  8.36 us
    pallas_call x1, Pallas kernels, per_device(): pl.pallas_call(functools.partial(lat_kernel, groups, masks), out_shape=[j...  4.34 us
    unnamed x12, local copies, waits for them, and re-layouts  3.25 us
  transfers between devices with their start and end apart: 16, of which 9 were waited for; matrix products, arithmetic and copies ran while one was open for 0% of the time, Pallas kernels for 6%

profile of v8, /device:TPU:9, one launch (start us, length us, event | category | flops | bytes accessed | tf_op | source)
XLA Modules:
  0.0 110.5 jit_solution(12358197683127958797)
XLA Ops:
  0.0 0.0 copy-start.4
  0.0 3.4 %lon_filter.2 = (bf16[1058,128]{1,0:T(8,128)(2,1)}, bf16[1058,128]{1,0:T(8,128)(2,1)}) custom-call(s32[16]{0:T(128)} %counts.1, bf16[4,23,32,736]{3,2,1,0:T(8,128)(2,1)} %bitcast.6, bf16[4,23,32,736]{3,2,1,0:T(8,128)(2,1)} %bitcast.7, bf16[4,23,32,736]{3,2,1,0:T(8,128)(2,1)} %bitcast.8), custom_call_target="tpu_custom_call" | custom-call | tf_op jit(solution)/shard_map/lon_filter/pallas_call | solution.py:251
  3.4 3.2 %collective-permute-start.1 = (bf16[1058,128]{1,0:T(8,128)(2,1)}, bf16[1058,128]{1,0:T(8,128)(2,1)S(1)}, u32[]{:S(2)}, u32[]{:S(2)}) collective-permute-start(bf16[1058,128]{1,0:T(8,128)(2,1)} %get-tuple-element.31), channel_id=1, source_target_pairs={{0,9},{1,8},{2,11},{3,10},{4,13},{5,12},{6,15},{7,14},{8,1},{9,0},... | collective-permute-start | bytes 812552 | tf_op jit(solution)/shard_map/ppermute | solution.py:267
  6.6 0.1 collective-permute-start
  6.7 0.0 copy-done.4
  6.7 0.0 copy-done.5
  6.7 0.1 pad_add_fusion.meta
  6.8 0.0 copy-start
  6.8 2.3 %copy-done = bf16[4,32,23,736]{3,1,2,0:T(8,128)(2,1)S(1)} copy-done((bf16[4,32,23,736]{3,1,2,0:T(8,128)(2,1)S(1)}, bf16[4,32,23,736]{3,1,2,0:T(8,128)(2,1)}, u32[]{:S(2)}) %copy-start) | copy-done | bytes 4333592
  9.0 0.0 copy-start.2
  9.0 1.0 copy-done.2
  10.0 0.0 copy-start.3
  10.0 5.0 %lon_filter.3 = (bf16[1058,128]{1,0:T(8,128)(2,1)S(1)}, bf16[1058,128]{1,0:T(8,128)(2,1)S(1)}, bf16[1058,128]{1,0:T(8,128)(2,1)S(1)}, bf16[1058,128]{1,0:T(8,128...) custom-call(s32[34]{0:T(128)S(1)} %pad_add_fusion.meta, ...), custom_call_target="tpu_custom_call" | custom-call | tf_op jit(solution)/shard_map/lon_filter/pallas_call | solution.py:251
  15.0 0.2 collective-permute-start.2
  15.2 1.3 %collective-permute-start.3 = (bf16[1058,128]{1,0:T(8,128)(2,1)S(1)}, bf16[1058,128]{1,0:T(8,128)(2,1)S(1)}, u32[]{:S(2)}, u32[]{:S(2)}) collective-permute-start(bf16[1058,128]{1,0:T(8,128)(2,1)S(1)} %get-tuple-element.33), channel_id=1, source_target_pairs={{0,5},{1,4},{2,7},{3,6},{4,1},{5,0},{6,3},{7,2},{8,13},{9,12},{10,... | collective-permute-start | bytes 812552 | tf_op jit(solution)/shard_map/ppermute | solution.py:267
  16.5 3.3 %collective-permute-start.4 = (bf16[1058,128]{1,0:T(8,128)(2,1)S(1)}, bf16[1058,128]{1,0:T(8,128)(2,1)S(1)}, u32[]{:S(2)}, u32[]{:S(2)}) collective-permute-start(bf16[1058,128]{1,0:T(8,128)(2,1)S(1)} %get-tuple-element.34), channel_id=1, source_target_pairs={{0,10},{1,11},{2,8},{3,9},{4,14},{5,15},{6,12},{7,13},{8,2},{9,3},... | collective-permute-start | bytes 812552 | tf_op jit(solution)/shard_map/ppermute | solution.py:267
  19.8 5.0 %collective-permute-done.1.refs_1_ = bf16[1058,128]{1,0:T(8,128)(2,1)S(1)} collective-permute-done((bf16[1058,128]{1,0:T(8,128)(2,1)}, bf16[1058,128]{1,0:T(8,128)(2,1)S(1)}, u32[]{:S(2)}, u32[]{:S(2)}) %collective-permute-start.1) | collective-permute-done | bytes 270880 | tf_op jit(solution)/shard_map/ppermute | solution.py:267
  24.8 0.9 collective-permute-start.5
  25.7 5.5 %collective-permute-done.refs_0_ = bf16[1058,128]{1,0:T(8,128)(2,1)S(1)} collective-permute-done((bf16[1058,128]{1,0:T(8,128)(2,1)}, bf16[1058,128]{1,0:T(8,128)(2,1)S(1)}, u32[]{:S(2)}, u32[]{:S(2)}) %collective-permute-start) | collective-permute-done | bytes 270880 | tf_op jit(solution)/shard_map/ppermute | solution.py:267
  31.2 4.4 %collective-permute-start.6 = (bf16[1058,128]{1,0:T(8,128)(2,1)S(1)}, bf16[1058,128]{1,0:T(8,128)(2,1)S(1)}, u32[]{:S(2)}, u32[]{:S(2)}) collective-permute-start(bf16[1058,128]{1,0:T(8,128)(2,1)S(1)} %get-tuple-element.36), channel_id=1, source_target_pairs={{0,11},{1,10},{2,9},{3,8},{4,15},{5,14},{6,13},{7,12},{8,3},{9,2},... | collective-permute-start | bytes 812552 | tf_op jit(solution)/shard_map/ppermute | solution.py:267
  35.6 0.0 collective-permute-done.2.refs_2_
  35.6 0.0 collective-permute-start.7
  35.6 7.8 %collective-permute-done.3.refs_3_ = bf16[1058,128]{1,0:T(8,128)(2,1)S(1)} collective-permute-done((bf16[1058,128]{1,0:T(8,128)(2,1)S(1)}, bf16[1058,128]{1,0:T(8,128)(2,1)S(1)}, u32[]{:S(2)}, u32[]{:S(2)}) %collective-permute-start.3) | collective-permute-done | bytes 270880 | tf_op jit(solution)/shard_map/ppermute | solution.py:267
  43.4 2.6 %collective-permute-start.8 = (bf16[1058,128]{1,0:T(8,128)(2,1)S(1)}, bf16[1058,128]{1,0:T(8,128)(2,1)S(1)}, u32[]{:S(2)}, u32[]{:S(2)}) collective-permute-start(bf16[1058,128]{1,0:T(8,128)(2,1)S(1)} %get-tuple-element.38), channel_id=1, source_target_pairs={{0,12},{1,13},{2,14},{3,15},{4,8},{5,9},{6,10},{7,11},{8,4},{9,5},... | collective-permute-start | bytes 812552 | tf_op jit(solution)/shard_map/ppermute | solution.py:267
  46.0 0.0 collective-permute-done.4.refs_4_
  46.0 0.3 collective-permute-start.9
  46.2 6.6 %collective-permute-done.5.refs_5_ = bf16[1058,128]{1,0:T(8,128)(2,1)S(1)} collective-permute-done((bf16[1058,128]{1,0:T(8,128)(2,1)S(1)}, bf16[1058,128]{1,0:T(8,128)(2,1)S(1)}, u32[]{:S(2)}, u32[]{:S(2)}) %collective-permute-start.5) | collective-permute-done | bytes 270880 | tf_op jit(solution)/shard_map/ppermute | solution.py:267
  52.9 10.5 %collective-permute-start.10 = (bf16[1058,128]{1,0:T(8,128)(2,1)S(1)}, bf16[1058,128]{1,0:T(8,128)(2,1)S(1)}, u32[]{:S(2)}, u32[]{:S(2)}) collective-permute-start(bf16[1058,128]{1,0:T(8,128)(2,1)S(1)} %get-tuple-element.40), channel_id=1, source_target_pairs={{0,13},{1,12},{2,15},{3,14},{4,9},{5,8},{6,11},{7,10},{8,5},{9,4},... | collective-permute-start | bytes 812552 | tf_op jit(solution)/shard_map/ppermute | solution.py:267
  63.3 0.0 collective-permute-done.6.refs_6_
  63.4 1.2 %collective-permute-start.11 = (bf16[1058,128]{1,0:T(8,128)(2,1)S(1)}, bf16[1058,128]{1,0:T(8,128)(2,1)S(1)}, u32[]{:S(2)}, u32[]{:S(2)}) collective-permute-start(bf16[1058,128]{1,0:T(8,128)(2,1)S(1)} %get-tuple-element.41), channel_id=1, source_target_pairs={{0,2},{1,3},{2,0},{3,1},{4,6},{5,7},{6,4},{7,5},{8,10},{9,11},{10,... | collective-permute-start | bytes 812552 | tf_op jit(solution)/shard_map/ppermute | solution.py:267
  64.6 0.8 collective-permute-done.7.refs_7_
  65.4 10.5 %collective-permute-start.12 = (bf16[1058,128]{1,0:T(8,128)(2,1)S(1)}, bf16[1058,128]{1,0:T(8,128)(2,1)S(1)}, u32[]{:S(2)}, u32[]{:S(2)}) collective-permute-start(bf16[1058,128]{1,0:T(8,128)(2,1)S(1)} %get-tuple-element.42), channel_id=1, source_target_pairs={{0,14},{1,15},{2,12},{3,13},{4,10},{5,11},{6,8},{7,9},{8,6},{9,7},... | collective-permute-start | bytes 812552 | tf_op jit(solution)/shard_map/ppermute | solution.py:267
  75.9 0.0 collective-permute-done.8.refs_8_
  75.9 0.0 collective-permute-start.13
  75.9 0.0 collective-permute-done.9.refs_9_
  75.9 0.1 collective-permute-start.14
  75.9 0.0 copy-done.3
  76.0 1.4 %matrices.1 = (bf16[256,256]{1,0:T(8,128)(2,1)S(1)}, bf16[184,184]{1,0:T(8,128)(2,1)S(1)}, bf16[184,253]{1,0:T(8,128)(2,1)S(1)}) custom-call(s32[34]{0:T(128)S(1)} %pad_add_fusion.meta, bf16[32,32]{1,0:T(8,128)(2,1)S(1)} %copy-done.3, bf16[1058,128]{1,0:T(8,128)(2,1)S(1)} %get-tuple-element.27.after.refs_15_), custom_call_target="tpu_custom_call" | custom-call | tf_op jit(solution)/shard_map/matrices/pallas_call | solution.py:290
  77.4 1.1 %collective-permute-done.10.refs_10_ = bf16[1058,128]{1,0:T(8,128)(2,1)S(1)} collective-permute-done((bf16[1058,128]{1,0:T(8,128)(2,1)S(1)}, bf16[1058,128]{1,0:T(8,128)(2,1)S(1)}, u32[]{:S(2)}, u32[]{:S(2)}) %collective-permute-start.10) | collective-permute-done | bytes 270880 | tf_op jit(solution)/shard_map/ppermute | solution.py:267
  78.5 0.0 collective-permute-done.11.refs_11_
  78.5 15.3 %collective-permute-done.12.refs_12_ = bf16[1058,128]{1,0:T(8,128)(2,1)S(1)} collective-permute-done((bf16[1058,128]{1,0:T(8,128)(2,1)S(1)}, bf16[1058,128]{1,0:T(8,128)(2,1)S(1)}, u32[]{:S(2)}, u32[]{:S(2)}) %collective-permute-start.12) | collective-permute-done | bytes 270880 | tf_op jit(solution)/shard_map/ppermute | solution.py:267
  93.8 0.0 collective-permute-done.13.refs_13_
  93.8 8.1 %collective-permute-done.14.refs_14_ = bf16[1058,128]{1,0:T(8,128)(2,1)S(1)} collective-permute-done((bf16[1058,128]{1,0:T(8,128)(2,1)S(1)}, bf16[1058,128]{1,0:T(8,128)(2,1)S(1)}, u32[]{:S(2)}, u32[]{:S(2)}) %collective-permute-start.14) | collective-permute-done | bytes 270880 | tf_op jit(solution)/shard_map/ppermute | solution.py:267
  102.0 0.0 copy-done.1
  102.0 4.3 %lat_filter.1 = (f32[46,16,368]{2,1,0:T(8,128)S(1)}, bf16[46,16,368]{2,1,0:T(8,128)(2,1)S(1)}) custom-call(s32[34]{0:T(128)S(1)} %pad_add_fusion.meta, bf16[256,256]{1,0:T(8,128)(2,1)S(1)} %get-tuple-element.28.mixer, bf16[184,184]{1,0:T(8,128)(2,1)S(1)} %get-tuple-element.29.upper, bf16[184,253]{1,0:T(8,128)(2,1)S(1)} %get-tuple-element.30.lower, ...), custom_call_target="tpu_custom_call" | custom-call | tf_op jit(solution)/shard_map/lat_filter/pallas_call | solution.py:305
  106.3 1.5 %collective-permute-start.15 = (bf16[46,16,368]{2,1,0:T(8,128)(2,1)S(1)}, bf16[46,16,368]{2,1,0:T(8,128)(2,1)S(1)}, u32[]{:S(2)}, u32[]{:S(2)}) collective-permute-start(bf16[46,16,368]{2,1,0:T(8,128)(2,1)S(1)} %get-tuple-element.46), channel_id=1, source_target_pairs={{0,16},{16,0},{1,17},{17,1},{2,18},{18,2},{3,19},{19,3},{4,20},{20... | collective-permute-start | bytes 1625096 | tf_op jit(solution)/shard_map/ppermute | solution.py:318
  107.8 1.6 %collective-permute-done.15 = bf16[46,16,368]{2,1,0:T(8,128)(2,1)S(1)} collective-permute-done((bf16[46,16,368]{2,1,0:T(8,128)(2,1)S(1)}, bf16[46,16,368]{2,1,0:T(8,128)(2,1)S(1)}, u32[]{:S(2)}, u32[]{:S(2)}) %collective-permute-start.15) | collective-permute-done | bytes 541728 | tf_op jit(solution)/shard_map/ppermute | solution.py:318
  109.4 1.1 %add_bitcast_fusion = f32[16,46,368]{2,0,1:T(8,128)} fusion(f32[46,16,368]{2,1,0:T(8,128)S(1)} %get-tuple-element.45, bf16[46,16,368]{2,1,0:T(8,128)(2,1)S(1)} %collective-permute-done.15), kind=kLoop, calls=%fused_computation | loop fusion | flops 541696 | bytes 2708480 | tf_op jit(solution)/shard_map/transpose | solution.py:323
  (2 shorter events, 0.0 us)
Async XLA Ops:
  0.0 6.7 %copy-start.4 = (s32[16]{0:T(128)S(1)}, s32[16]{0:T(128)}, u32[]{:S(2)}) copy-start(s32[16]{0:T(128)} %counts.1) | copy-start | bytes 196
  0.0 6.7 %copy-start.5 = (s32[16]{0:T(128)S(1)}, s32[16]{0:T(128)}, u32[]{:S(2)}) copy-start(s32[16]{0:T(128)} %param.8) | copy-start | bytes 196
  3.4 21.4 %collective-permute-start.1 = (bf16[1058,128]{1,0:T(8,128)(2,1)}, bf16[1058,128]{1,0:T(8,128)(2,1)S(1)}, u32[]{:S(2)}, u32[]{:S(2)}) collective-permute-start(bf16[1058,128]{1,0:T(8,128)(2,1)} %get-tuple-element.31), channel_id=1, source_target_pairs={{0,9},{1,8},{2,11},{3,10},{4,13},{5,12},{6,15},{7,14},{8,1},{9,0},... | collective-permute-start | bytes 812552 | tf_op jit(solution)/shard_map/ppermute | solution.py:267
  6.6 24.6 %collective-permute-start = (bf16[1058,128]{1,0:T(8,128)(2,1)}, bf16[1058,128]{1,0:T(8,128)(2,1)S(1)}, u32[]{:S(2)}, u32[]{:S(2)}) collective-permute-start(bf16[1058,128]{1,0:T(8,128)(2,1)} %get-tuple-element.26.refs_0_), channel_id=1, source_target_pairs={{0,8},{1,9},{2,10},{3,11},{4,12},{5,13},{6,14},{7,15},{8,0},{9,1},... | collective-permute-start | bytes 812552 | tf_op jit(solution)/shard_map/ppermute | solution.py:267
  6.8 2.3 %copy-start = (bf16[4,32,23,736]{3,1,2,0:T(8,128)(2,1)S(1)}, bf16[4,32,23,736]{3,1,2,0:T(8,128)(2,1)}, u32[]{:S(2)}) copy-start(bf16[4,32,23,736]{3,1,2,0:T(8,128)(2,1)} %param.5) | copy-start | bytes 13000708
  9.0 1.0 copy-start.2
  10.0 65.9 %copy-start.3 = (bf16[32,32]{1,0:T(8,128)(2,1)S(1)}, bf16[32,32]{1,0:T(8,128)(2,1)}, u32[]{:S(2)}) copy-start(bf16[32,32]{1,0:T(8,128)(2,1)} %vertical.1) | copy-start | bytes 6148
  10.0 92.0 %copy-start.1 = (bf16[4,32,46,368]{3,1,2,0:T(8,128)(2,1)S(1)}, bf16[4,32,46,368]{3,1,2,0:T(8,128)(2,1)}, u32[]{:S(2)}) copy-start(bf16[4,32,46,368]{3,1,2,0:T(8,128)(2,1)} %param.6) | copy-start | bytes 13000708
  15.0 20.6 %collective-permute-start.2 = (bf16[1058,128]{1,0:T(8,128)(2,1)S(1)}, bf16[1058,128]{1,0:T(8,128)(2,1)S(1)}, u32[]{:S(2)}, u32[]{:S(2)}) collective-permute-start(bf16[1058,128]{1,0:T(8,128)(2,1)S(1)} %get-tuple-element.32), channel_id=1, source_target_pairs={{0,4},{1,5},{2,6},{3,7},{4,0},{5,1},{6,2},{7,3},{8,12},{9,13},{10,... | collective-permute-start | bytes 812552 | tf_op jit(solution)/shard_map/ppermute | solution.py:267
  15.2 28.1 %collective-permute-start.3 = (bf16[1058,128]{1,0:T(8,128)(2,1)S(1)}, bf16[1058,128]{1,0:T(8,128)(2,1)S(1)}, u32[]{:S(2)}, u32[]{:S(2)}) collective-permute-start(bf16[1058,128]{1,0:T(8,128)(2,1)S(1)} %get-tuple-element.33), channel_id=1, source_target_pairs={{0,5},{1,4},{2,7},{3,6},{4,1},{5,0},{6,3},{7,2},{8,13},{9,12},{10,... | collective-permute-start | bytes 812552 | tf_op jit(solution)/shard_map/ppermute | solution.py:267
  16.5 29.5 %collective-permute-start.4 = (bf16[1058,128]{1,0:T(8,128)(2,1)S(1)}, bf16[1058,128]{1,0:T(8,128)(2,1)S(1)}, u32[]{:S(2)}, u32[]{:S(2)}) collective-permute-start(bf16[1058,128]{1,0:T(8,128)(2,1)S(1)} %get-tuple-element.34), channel_id=1, source_target_pairs={{0,10},{1,11},{2,8},{3,9},{4,14},{5,15},{6,12},{7,13},{8,2},{9,3},... | collective-permute-start | bytes 812552 | tf_op jit(solution)/shard_map/ppermute | solution.py:267
  24.8 28.1 %collective-permute-start.5 = (bf16[1058,128]{1,0:T(8,128)(2,1)S(1)}, bf16[1058,128]{1,0:T(8,128)(2,1)S(1)}, u32[]{:S(2)}, u32[]{:S(2)}) collective-permute-start(bf16[1058,128]{1,0:T(8,128)(2,1)S(1)} %get-tuple-element.35), channel_id=1, source_target_pairs={{0,6},{1,7},{2,4},{3,5},{4,2},{5,3},{6,0},{7,1},{8,14},{9,15},{10,... | collective-permute-start | bytes 812552 | tf_op jit(solution)/shard_map/ppermute | solution.py:267
  31.2 32.2 %collective-permute-start.6 = (bf16[1058,128]{1,0:T(8,128)(2,1)S(1)}, bf16[1058,128]{1,0:T(8,128)(2,1)S(1)}, u32[]{:S(2)}, u32[]{:S(2)}) collective-permute-start(bf16[1058,128]{1,0:T(8,128)(2,1)S(1)} %get-tuple-element.36), channel_id=1, source_target_pairs={{0,11},{1,10},{2,9},{3,8},{4,15},{5,14},{6,13},{7,12},{8,3},{9,2},... | collective-permute-start | bytes 812552 | tf_op jit(solution)/shard_map/ppermute | solution.py:267
  35.6 29.8 %collective-permute-start.7 = (bf16[1058,128]{1,0:T(8,128)(2,1)S(1)}, bf16[1058,128]{1,0:T(8,128)(2,1)S(1)}, u32[]{:S(2)}, u32[]{:S(2)}) collective-permute-start(bf16[1058,128]{1,0:T(8,128)(2,1)S(1)} %get-tuple-element.37), channel_id=1, source_target_pairs={{0,7},{1,6},{2,5},{3,4},{4,3},{5,2},{6,1},{7,0},{8,15},{9,14},{10,... | collective-permute-start | bytes 812552 | tf_op jit(solution)/shard_map/ppermute | solution.py:267
  43.4 32.5 %collective-permute-start.8 = (bf16[1058,128]{1,0:T(8,128)(2,1)S(1)}, bf16[1058,128]{1,0:T(8,128)(2,1)S(1)}, u32[]{:S(2)}, u32[]{:S(2)}) collective-permute-start(bf16[1058,128]{1,0:T(8,128)(2,1)S(1)} %get-tuple-element.38), channel_id=1, source_target_pairs={{0,12},{1,13},{2,14},{3,15},{4,8},{5,9},{6,10},{7,11},{8,4},{9,5},... | collective-permute-start | bytes 812552 | tf_op jit(solution)/shard_map/ppermute | solution.py:267
  46.0 29.9 %collective-permute-start.9 = (bf16[1058,128]{1,0:T(8,128)(2,1)S(1)}, bf16[1058,128]{1,0:T(8,128)(2,1)S(1)}, u32[]{:S(2)}, u32[]{:S(2)}) collective-permute-start(bf16[1058,128]{1,0:T(8,128)(2,1)S(1)} %get-tuple-element.39), channel_id=1, source_target_pairs={{0,1},{1,0},{2,3},{3,2},{4,5},{5,4},{6,7},{7,6},{8,9},{9,8},{10,11... | collective-permute-start | bytes 812552 | tf_op jit(solution)/shard_map/ppermute | solution.py:267
  52.9 25.7 %collective-permute-start.10 = (bf16[1058,128]{1,0:T(8,128)(2,1)S(1)}, bf16[1058,128]{1,0:T(8,128)(2,1)S(1)}, u32[]{:S(2)}, u32[]{:S(2)}) collective-permute-start(bf16[1058,128]{1,0:T(8,128)(2,1)S(1)} %get-tuple-element.40), channel_id=1, source_target_pairs={{0,13},{1,12},{2,15},{3,14},{4,9},{5,8},{6,11},{7,10},{8,5},{9,4},... | collective-permute-start | bytes 812552 | tf_op jit(solution)/shard_map/ppermute | solution.py:267
  63.4 15.2 %collective-permute-start.11 = (bf16[1058,128]{1,0:T(8,128)(2,1)S(1)}, bf16[1058,128]{1,0:T(8,128)(2,1)S(1)}, u32[]{:S(2)}, u32[]{:S(2)}) collective-permute-start(bf16[1058,128]{1,0:T(8,128)(2,1)S(1)} %get-tuple-element.41), channel_id=1, source_target_pairs={{0,2},{1,3},{2,0},{3,1},{4,6},{5,7},{6,4},{7,5},{8,10},{9,11},{10,... | collective-permute-start | bytes 812552 | tf_op jit(solution)/shard_map/ppermute | solution.py:267
  65.4 28.5 %collective-permute-start.12 = (bf16[1058,128]{1,0:T(8,128)(2,1)S(1)}, bf16[1058,128]{1,0:T(8,128)(2,1)S(1)}, u32[]{:S(2)}, u32[]{:S(2)}) collective-permute-start(bf16[1058,128]{1,0:T(8,128)(2,1)S(1)} %get-tuple-element.42), channel_id=1, source_target_pairs={{0,14},{1,15},{2,12},{3,13},{4,10},{5,11},{6,8},{7,9},{8,6},{9,7},... | collective-permute-start | bytes 812552 | tf_op jit(solution)/shard_map/ppermute | solution.py:267
  75.9 18.0 %collective-permute-start.13 = (bf16[1058,128]{1,0:T(8,128)(2,1)S(1)}, bf16[1058,128]{1,0:T(8,128)(2,1)S(1)}, u32[]{:S(2)}, u32[]{:S(2)}) collective-permute-start(bf16[1058,128]{1,0:T(8,128)(2,1)S(1)} %get-tuple-element.43), channel_id=1, source_target_pairs={{0,3},{1,2},{2,1},{3,0},{4,7},{5,6},{6,5},{7,4},{8,11},{9,10},{10,... | collective-permute-start | bytes 812552 | tf_op jit(solution)/shard_map/ppermute | solution.py:267
  75.9 26.1 %collective-permute-start.14 = (bf16[1058,128]{1,0:T(8,128)(2,1)S(1)}, bf16[1058,128]{1,0:T(8,128)(2,1)S(1)}, u32[]{:S(2)}, u32[]{:S(2)}) collective-permute-start(bf16[1058,128]{1,0:T(8,128)(2,1)S(1)} %get-tuple-element.44), channel_id=1, source_target_pairs={{0,15},{1,14},{2,13},{3,12},{4,11},{5,10},{6,9},{7,8},{8,7},{9,6},... | collective-permute-start | bytes 812552 | tf_op jit(solution)/shard_map/ppermute | solution.py:267
  106.3 3.1 %collective-permute-start.15 = (bf16[46,16,368]{2,1,0:T(8,128)(2,1)S(1)}, bf16[46,16,368]{2,1,0:T(8,128)(2,1)S(1)}, u32[]{:S(2)}, u32[]{:S(2)}) collective-permute-start(bf16[46,16,368]{2,1,0:T(8,128)(2,1)S(1)} %get-tuple-element.46), channel_id=1, source_target_pairs={{0,16},{16,0},{1,17},{17,1},{2,18},{18,2},{3,19},{19,3},{4,20},{20... | collective-permute-start | bytes 1625096 | tf_op jit(solution)/shard_map/ppermute | solution.py:318
